TPU v7x, 32 devices: a whole 2x2x4 slice. The times are simulated.
32 devices in a mesh: seq: 8 (over y, x, core), tp: 4 (over z).
Axes of the slice: x: 2, y: 2, z: 4, core: 2. Of those that a mesh axis runs over, the one named last changes fastest.
Arguments:
- queries: bfloat16 [2048, 4096], P('seq', 'tp'), may hold values from -4.5 to 4.5
- sequence_keys: bfloat16 [2048, 1024], P('seq', 'tp'), may hold values from -4.5 to 4.5
- sequence_values: bfloat16 [2048, 1024], P('seq', 'tp'), may hold values from -6 to 6
- output_gradient: bfloat16 [2048, 4096], P('seq', 'tp'), may hold values from -6 to 6
- enc_keys: bfloat16 [512, 16, 1024], P('seq', 'tp'), may hold values from -4.5 to 4.5
- encoded_values: bfloat16 [512, 16, 1024], P('seq', 'tp'), may hold values from -6 to 6
- nbr_owner: int32 [32, 4], P('seq'), may hold values from 0 to 7, as said below
- nbr_slot: int32 [32, 4], P('seq'), may hold values from 0 to 63
Outputs:
- attended: bfloat16 [2048, 4096], P('seq', 'tp')
- query_gradient: bfloat16 [2048, 4096], P('seq', 'tp')
- key_gradient: bfloat16 [2048, 1024], P('seq', 'tp')
- value_gradient: bfloat16 [2048, 1024], P('seq', 'tp')
- encoded_key_gradient: bfloat16 [512, 16, 1024], P('seq', 'tp')
- encoded_value_gradient: bfloat16 [512, 16, 1024], P('seq', 'tp')
Inputs may be any that keep to these rules, and one draw needn't show every extreme that they name: `nbr_owner`: among the 16 entries of the stretches of one index of seq, at most 4 name the same owner; in every draw one owner is named exactly 4 times by the entries of every index of seq. The same owner may appear twice in one stretch.
All inputs are finite; a program needn't handle non-finite values.
Results may differ from a plain program's by a relative error of at most 0.0083.
Values may be sent and summed in bfloat16 or wider, within the bound.
No kernel may reach another device: no remote copies, remote signals or barrier semaphores. Data moves between devices by JAX's collectives and lax.ppermute only.
A program may use at most 64 MiB of HBM per device.

v0:
```python
import functools
import math

import jax
import jax.numpy as jnp
from jax import lax
from jax.experimental import pallas as pl
from jax.experimental.pallas import tpu as pltpu
from jax.sharding import PartitionSpec as P

QUERY_HEADS = 32
KEY_VALUE_HEADS = 8
HEAD_SIZE = 128
SPAN_TOKENS = 64
NEIGHBOUR_COUNT = 4
NEIGHBOUR_LENGTH = 16
WINDOW_KEYS = 128
GROUP = QUERY_HEADS // KEY_VALUE_HEADS
SCALE = 1.0 / math.sqrt(HEAD_SIZE)
LOG2E = math.log2(math.e)

F32 = jnp.float32
BF16 = jnp.bfloat16
VMEM = pl.BlockSpec(memory_space=pltpu.VMEM)
SMEM = pl.BlockSpec(memory_space=pltpu.SMEM)
HBM = pl.BlockSpec(memory_space=pltpu.HBM)
LANES = 128
PARAMS = pltpu.CompilerParams(vmem_limit_bytes=16 * 1024 * 1024)


def dot_nn(a, b):
    return lax.dot_general(a, b, (((1,), (0,)), ((), ())), preferred_element_type=F32)


def dot_nt(a, b):
    return lax.dot_general(a, b, (((1,), (1,)), ((), ())), preferred_element_type=F32)


def dot_tn(a, b):
    return lax.dot_general(a, b, (((0,), (0,)), ((), ())), preferred_element_type=F32)


def stacked_heads(ref, first_row, rows, group):
    return jnp.concatenate(
        [
            ref[
                first_row : first_row + rows,
                (group * GROUP + h) * HEAD_SIZE : (group * GROUP + h + 1) * HEAD_SIZE,
            ]
            for h in range(GROUP)
        ],
        axis=0,
    )


def probs_and_grads(scores, grad_probs, allowed):
    scores = scores * (SCALE * LOG2E)
    if allowed is not None:
        scores = jnp.where(allowed, scores, -jnp.inf)
    raised = jnp.exp2(scores - jnp.max(scores, axis=0, keepdims=True))
    probs = raised * (1.0 / jnp.sum(raised, axis=0, keepdims=True))
    delta = jnp.sum(probs * grad_probs, axis=0, keepdims=True)
    grad_scores = (probs * (grad_probs - delta) * SCALE).astype(BF16)
    return probs.astype(BF16), grad_scores


def plan_kernel(
    tokens, cap, owner_hbm, slot_hbm, want_ref, owner_out, rank_out, owner_ref, slot_ref, sems
):
    copies = [
        pltpu.make_async_copy(owner_hbm, owner_ref, sems.at[0]),
        pltpu.make_async_copy(slot_hbm, slot_ref, sems.at[1]),
    ]
    for copy in copies:
        copy.start()
    spans, per_span = owner_ref.shape
    row = lax.broadcasted_iota(jnp.int32, want_ref.shape, 0)
    lane = lax.broadcasted_iota(jnp.int32, want_ref.shape, 1)
    place = row * cap + (lane // tokens) % cap
    token = lane % tokens
    want = jnp.full(want_ref.shape, -1, jnp.int32)
    for copy in copies:
        copy.wait()
    owners = []
    for i in range(spans):
        for j in range(per_span):
            owner = owner_ref[i, j]
            rank = jnp.int32(0)
            for earlier in owners:
                rank = rank + jnp.where(earlier == owner, 1, 0)
            owners.append(owner)
            want = jnp.where(place == owner * cap + rank, slot_ref[i, j] * tokens + token, want)
            owner_out[i * per_span + j] = owner
            rank_out[i * per_span + j] = rank
    want_ref[...] = want


def stage_kernel(
    rows_each, me_ref, owner_ref, rank_ref, k_ref, v_ref, sk_ref, sv_ref, store_ref, halo_ref, placed_ref
):
    slots, tokens, features = k_ref.shape
    rows, columns = store_ref.shape
    kv_width = sk_ref.shape[1]
    for z in range(features // kv_width):
        cols = slice(z * kv_width, (z + 1) * kv_width)
        at = 2 * z * kv_width
        store_ref[:, at : at + kv_width] = k_ref[:, :, cols].reshape(rows, kv_width)
        store_ref[:, at + kv_width : at + 2 * kv_width] = v_ref[:, :, cols].reshape(rows, kv_width)
    halo_ref[:, :kv_width] = sk_ref[sk_ref.shape[0] - halo_ref.shape[0] :]
    halo_ref[:, kv_width:] = sv_ref[sv_ref.shape[0] - halo_ref.shape[0] :]
    lanes, used = placed_ref.shape
    me = me_ref[0]
    lane = lax.broadcasted_iota(jnp.int32, (1, used), 1)
    place = lane % tokens
    for r in range(used // tokens):
        first = (owner_ref[r] ^ me) * rows_each + rank_ref[r] * tokens
        place = place + jnp.where(lane // tokens == r, first, 0)
    row = lax.broadcasted_iota(jnp.int32, (lanes, used), 0)
    placed_ref[...] = jnp.where(row == place, 1.0, 0.0).astype(BF16)


def pack_kernel(pieces, me_ref, store_ref, *refs):
    wanted_refs, send_refs, owned_ref = refs[:pieces], refs[pieces:-1], refs[-1]
    rows_each = send_refs[0].shape[0]
    rows, lanes = owned_ref.shape
    me = me_ref[0]
    width = wanted_refs[0].shape[2]
    lane = lax.broadcasted_iota(jnp.int32, (1, width), 1)
    parts = [jnp.full((1, width), -1, jnp.int32) for _ in range(lanes // width)]
    apart = 0
    for wanted_ref in wanted_refs:
        for i in range(wanted_ref.shape[0]):
            part, at = divmod(apart * rows_each, width)
            from_there = wanted_ref[i, pl.ds(me, 1), :]
            here = (lane >= at) & (lane < at + rows_each)
            parts[part] = jnp.where(here, from_there, parts[part])
            apart += 1
    target = jnp.concatenate(parts, axis=1)
    row = lax.broadcasted_iota(jnp.int32, (rows, lanes), 0)
    owned = jnp.where(row == target, 1.0, 0.0).astype(BF16)
    owned_ref[...] = owned
    picked = dot_tn(owned, store_ref[...]).astype(BF16)
    for at, send_ref in enumerate(send_refs):
        send_ref[...] = picked[at * rows_each : (at + 1) * rows_each]


def spread_kernel(tp, z_ref, placed_ref, *refs):
    got_refs, send_refs, near_ref = refs[: -tp - 1], refs[-tp - 1 : -1], refs[-1]
    both = send_refs[0].shape[1]
    got = jnp.concatenate([ref[...] for ref in got_refs], axis=0)
    near_ref[...] = dot_tn(placed_ref[...], got).astype(BF16)
    for apart, send_ref in enumerate(send_refs):
        start = pl.multiple_of((z_ref[0] ^ apart) * both, both)
        send_ref[...] = near_ref[:, pl.ds(start, both)]


def scatter_kernel(tp, z_ref, placed_ref, *refs):
    grad_refs, send_refs, all_ref = refs[:tp], refs[tp:-1], refs[-1]
    both = grad_refs[0].shape[1]
    rows_each = send_refs[0].shape[0]
    for apart, grad_ref in enumerate(grad_refs):
        start = pl.multiple_of((z_ref[0] ^ apart) * both, both)
        all_ref[:, pl.ds(start, both)] = grad_ref[...]
    rows = dot_nn(placed_ref[...], all_ref[...]).astype(BF16)
    for at, send_ref in enumerate(send_refs):
        send_ref[...] = rows[at * rows_each : (at + 1) * rows_each]


def self_kernel(
    rank_ref, q_ref, k_ref, v_ref, do_ref, halo_ref, out_ref, dq_ref, dkv_ref, back_ref
):
    tokens, kv_width = k_ref.shape
    block = WINDOW_KEYS
    blocks = tokens // block
    key_at = lax.broadcasted_iota(jnp.int32, (2 * block, GROUP * block), 0)
    query_at = lax.broadcasted_iota(jnp.int32, (2 * block, GROUP * block), 1) % block
    band = (key_at > query_at) & (key_at <= query_at + block)
    first_band = band & ((key_at >= block) | (rank_ref[0] > 0))
    for group in range(kv_width // HEAD_SIZE):
        cols = slice(group * HEAD_SIZE, (group + 1) * HEAD_SIZE)
        vcols = slice(kv_width + group * HEAD_SIZE, kv_width + (group + 1) * HEAD_SIZE)
        carried_k = carried_v = None
        for b in range(blocks):
            here = slice(b * block, (b + 1) * block)
            if b == 0:
                keys = jnp.concatenate([halo_ref[:, cols], k_ref[here, cols]], 0)
                values = jnp.concatenate([halo_ref[:, vcols], v_ref[here, cols]], 0)
            else:
                keys = k_ref[(b - 1) * block : (b + 1) * block, cols]
                values = v_ref[(b - 1) * block : (b + 1) * block, cols]
            query_rows = stacked_heads(q_ref, b * block, block, group)
            grad_rows = stacked_heads(do_ref, b * block, block, group)
            weights, grad_scores = probs_and_grads(
                dot_nt(keys, query_rows),
                dot_nt(values, grad_rows),
                first_band if b == 0 else band,
            )
            out = dot_tn(weights, values)
            dq = dot_tn(grad_scores, keys)
            for h in range(GROUP):
                head = slice((group * GROUP + h) * HEAD_SIZE, (group * GROUP + h + 1) * HEAD_SIZE)
                out_ref[here, head] = out[h * block : (h + 1) * block]
                dq_ref[here, head] = dq[h * block : (h + 1) * block]
            dk = dot_nn(grad_scores, query_rows)
            dv = dot_nn(weights, grad_rows)
            if b == 0:
                back_ref[:, cols] = dk[:block].astype(BF16)
                back_ref[:, vcols] = dv[:block].astype(BF16)
            else:
                before = slice((b - 1) * block, b * block)
                dkv_ref[before, cols] = carried_k + dk[:block]
                dkv_ref[before, vcols] = carried_v + dv[:block]
            carried_k, carried_v = dk[block:], dv[block:]
        last = slice((blocks - 1) * block, blocks * block)
        dkv_ref[last, cols] = carried_k
        dkv_ref[last, vcols] = carried_v


def span_rows(near_refs, span, rows, cols):
    return jnp.concatenate([ref[span * rows : (span + 1) * rows, cols] for ref in near_refs], axis=0)


def cross_kernel(tp, q_ref, do_ref, *refs):
    near_refs, grad_refs, w_ref, ds_ref = refs[:tp], refs[tp : 2 * tp], refs[2 * tp], refs[2 * tp + 1]
    kv_width = near_refs[0].shape[1] // 2
    groups = kv_width // HEAD_SIZE
    blocks, rows_span, columns = w_ref.shape
    rows = rows_span // tp
    queries, grads, scores, grad_probs = [], [], [], []
    for at in range(blocks):
        span, group = at // groups, at % groups
        cols = slice(group * HEAD_SIZE, (group + 1) * HEAD_SIZE)
        vcols = slice(kv_width + group * HEAD_SIZE, kv_width + (group + 1) * HEAD_SIZE)
        queries.append(stacked_heads(q_ref, span * SPAN_TOKENS, SPAN_TOKENS, group))
        grads.append(stacked_heads(do_ref, span * SPAN_TOKENS, SPAN_TOKENS, group))
        scores.append(dot_nt(span_rows(near_refs, span, rows, cols), queries[at]))
        grad_probs.append(dot_nt(span_rows(near_refs, span, rows, vcols), grads[at]))
    weights, grad_scores = probs_and_grads(
        jnp.concatenate(scores, axis=1), jnp.concatenate(grad_probs, axis=1), None
    )
    for at in range(blocks):
        span, group = at // groups, at % groups
        here = slice(span * rows, (span + 1) * rows)
        cols = slice(group * HEAD_SIZE, (group + 1) * HEAD_SIZE)
        vcols = slice(kv_width + group * HEAD_SIZE, kv_width + (group + 1) * HEAD_SIZE)
        part = slice(at * columns, (at + 1) * columns)
        w_ref[at] = weights[:, part]
        ds_ref[at] = grad_scores[:, part]
        dk = dot_nn(grad_scores[:, part], queries[at]).astype(BF16)
        dv = dot_nn(weights[:, part], grads[at]).astype(BF16)
        for apart, grad_ref in enumerate(grad_refs):
            grad_ref[here, cols] = dk[apart * rows : (apart + 1) * rows]
            grad_ref[here, vcols] = dv[apart * rows : (apart + 1) * rows]


def join_kernel(tp, w_ref, ds_ref, out_ref, dq_ref, dkv_ref, back_ref, *refs):
    near_refs, (att_ref, qg_ref, kg_ref, vg_ref) = refs[:tp], refs[tp:]
    tokens, kv_width = kg_ref.shape
    groups = kv_width // HEAD_SIZE
    blocks, rows_span, _ = w_ref.shape
    for span in range(blocks // groups):
        rows = slice(span * SPAN_TOKENS, (span + 1) * SPAN_TOKENS)
        for group in range(groups):
            cols = slice(group * HEAD_SIZE, (group + 1) * HEAD_SIZE)
            vcols = slice(kv_width + group * HEAD_SIZE, kv_width + (group + 1) * HEAD_SIZE)
            at = span * groups + group
            out = dot_tn(w_ref[at], span_rows(near_refs, span, rows_span // tp, vcols))
            dq = dot_tn(ds_ref[at], span_rows(near_refs, span, rows_span // tp, cols))
            for h in range(GROUP):
                head = slice((group * GROUP + h) * HEAD_SIZE, (group * GROUP + h + 1) * HEAD_SIZE)
                part = slice(h * SPAN_TOKENS, (h + 1) * SPAN_TOKENS)
                att_ref[rows, head] = (out_ref[rows, head] + out[part]).astype(BF16)
                qg_ref[rows, head] = (dq_ref[rows, head] + dq[part]).astype(BF16)
    halo = back_ref.shape[0]
    kg_ref[: tokens - halo] = dkv_ref[: tokens - halo, :kv_width].astype(BF16)
    vg_ref[: tokens - halo] = dkv_ref[: tokens - halo, kv_width:].astype(BF16)
    kg_ref[tokens - halo :] = (
        dkv_ref[tokens - halo :, :kv_width] + back_ref[:, :kv_width].astype(F32)
    ).astype(BF16)
    vg_ref[tokens - halo :] = (
        dkv_ref[tokens - halo :, kv_width:] + back_ref[:, kv_width:].astype(F32)
    ).astype(BF16)


def sum_kernel(tp, owned_ref, *refs):
    got_refs, (kg_ref, vg_ref) = refs[:-2], refs[-2:]
    store_rows, tokens, features = kg_ref.shape
    width = features // tp
    owned = owned_ref[...]
    got = jnp.concatenate([ref[...] for ref in got_refs], axis=0)
    for z in range(tp):
        total = dot_nn(owned, got[:, 2 * z * width : 2 * (z + 1) * width]).astype(BF16)
        cols = slice(z * width, (z + 1) * width)
        kg_ref[:, :, cols] = total[:, :width].reshape(store_rows, tokens, width)
        vg_ref[:, :, cols] = total[:, width:].reshape(store_rows, tokens, width)


def call(kernel, name, ins, outs, flops, bytes_accessed, scratch=(), scalars=0, places=None):
    return pl.pallas_call(
        kernel,
        out_shape=tuple(outs),
        in_specs=places or [SMEM] * scalars + [VMEM] * (len(ins) - scalars),
        out_specs=tuple(SMEM if len(out.shape) == 1 else VMEM for out in outs),
        scratch_shapes=list(scratch),
        compiler_params=PARAMS,
        cost_estimate=pl.CostEstimate(
            flops=flops, bytes_accessed=bytes_accessed, transcendentals=0
        ),
        name=name,
    )(*ins)


def swapped(block, axis, apart):
    return lax.ppermute(block, axis, [(i, i ^ apart) for i in range(lax.axis_size(axis))])


def body(
    queries,
    sequence_keys,
    sequence_values,
    output_gradient,
    enc_keys,
    encoded_values,
    nbr_owner,
    nbr_slot,
):
    tokens_here, query_width = queries.shape
    kv_width = sequence_keys.shape[1]
    both = 2 * kv_width
    groups = kv_width // HEAD_SIZE
    devices = lax.axis_size("seq")
    tp = lax.axis_size("tp")
    spans, per_span = nbr_owner.shape
    requests = spans * per_span
    cap = max(2, 2 * requests // devices)
    tokens = enc_keys.shape[1]
    rows_each = cap * tokens
    window = WINDOW_KEYS
    struct = jax.ShapeDtypeStruct
    store_rows = enc_keys.shape[0] * tokens
    lanes = devices * rows_each
    used = requests * tokens
    int32 = jnp.int32
    rank = lax.axis_index("seq").astype(int32).reshape(1)
    z_rank = lax.axis_index("tp").astype(int32).reshape(1)

    want, owner_of, rank_of = call(
        functools.partial(plan_kernel, tokens, cap),
        "plan_requests",
        (nbr_owner, nbr_slot),
        (
            struct((devices, min(lanes, LANES)), int32),
            struct((requests,), int32),
            struct((requests,), int32),
        ),
        0,
        10_000,
        scratch=[
            pltpu.SMEM(nbr_owner.shape, int32),
            pltpu.SMEM(nbr_slot.shape, int32),
            pltpu.SemaphoreType.DMA((2,)),
        ],
        places=[HBM, HBM],
    )
    pieces = [want[None]]
    step = 1
    while step < devices:
        known = jnp.concatenate(pieces, axis=0) if step > 1 else pieces[0]
        pieces.append(swapped(known, "seq", step))
        step *= 2

    store, halo, placed = call(
        functools.partial(stage_kernel, rows_each),
        "stage_store",
        (rank, owner_of, rank_of, enc_keys, encoded_values, sequence_keys, sequence_values),
        (
            struct((store_rows, 2 * enc_keys.shape[2]), BF16),
            struct((window, both), BF16),
            struct((lanes, used), BF16),
        ),
        0,
        3_000_000,
        scalars=3,
    )
    *sent, owned = call(
        functools.partial(pack_kernel, len(pieces)),
        "pack_requests",
        (rank, store, *pieces),
        [struct((rows_each, tp * both), BF16)] * devices + [struct((store_rows, lanes), BF16)],
        200_000_000,
        2_000_000,
        scalars=1,
    )
    sent, halo = lax.optimization_barrier((sent, halo))
    got = [sent[0]] + [swapped(sent[j], "seq", j) for j in range(1, devices)]
    halo = lax.ppermute(halo, "seq", [(i, i + 1) for i in range(devices - 1)])

    self_out, self_dq, self_dkv, back = call(
        self_kernel,
        "self_attention",
        (rank, queries, sequence_keys, sequence_values, output_gradient, halo),
        (
            struct((tokens_here, query_width), F32),
            struct((tokens_here, query_width), F32),
            struct((tokens_here, both), F32),
            struct((window, both), BF16),
        ),
        1_600_000_000,
        6_000_000,
        scalars=1,
    )

    spread = call(
        functools.partial(spread_kernel, tp),
        "spread_rows",
        (z_rank, placed, *got),
        [struct((used, both), BF16)] * tp,
        50_000_000,
        1_000_000,
        scratch=[pltpu.VMEM((used, tp * both), BF16)],
        scalars=1,
    )
    near = [spread[0]] + [swapped(spread[j], "tp", j) for j in range(1, tp)]

    blocks = spans * groups
    rows_span = per_span * NEIGHBOUR_LENGTH
    *grads, weights, grad_scores = call(
        functools.partial(cross_kernel, tp),
        "cross_attention",
        (queries, output_gradient, *near),
        [struct((used, both), BF16)] * tp
        + [struct((blocks, rows_span, GROUP * SPAN_TOKENS), BF16)] * 2,
        600_000_000,
        3_000_000,
    )
    grads = [grads[0]] + [swapped(grads[j], "tp", j) for j in range(1, tp)]
    back = lax.ppermute(back, "seq", [(i + 1, i) for i in range(devices - 1)])

    returned = call(
        functools.partial(scatter_kernel, tp),
        "scatter_gradients",
        (z_rank, placed, *grads),
        [struct((rows_each, tp * both), BF16)] * devices,
        50_000_000,
        1_000_000,
        scratch=[pltpu.VMEM((used, tp * both), BF16)],
        scalars=1,
    )
    returned = [returned[0]] + [swapped(returned[j], "seq", j) for j in range(1, devices)]

    attended, query_gradient, key_gradient, value_gradient = call(
        functools.partial(join_kernel, tp),
        "join_outputs",
        (weights, grad_scores, self_out, self_dq, self_dkv, back, *near),
        (
            struct((tokens_here, query_width), BF16),
            struct((tokens_here, query_width), BF16),
            struct((tokens_here, kv_width), BF16),
            struct((tokens_here, kv_width), BF16),
        ),
        300_000_000,
        5_000_000,
    )
    store_kgrad, store_vgrad = call(
        functools.partial(sum_kernel, tp),
        "sum_store_gradients",
        (owned, *returned),
        (struct(enc_keys.shape, BF16), struct(encoded_values.shape, BF16)),
        200_000_000,
        2_000_000,
    )
    return (
        attended,
        query_gradient,
        key_gradient,
        value_gradient,
        store_kgrad,
        store_vgrad,
    )


def solution(mesh):
    arguments = (P("seq", "tp"),) * 4 + (P("seq", "tp", None),) * 2 + (P("seq", None),) * 2
    results = (P("seq", "tp"),) * 4 + (P("seq", "tp", None),) * 2
    return jax.shard_map(
        body, mesh=mesh, in_specs=arguments, out_specs=results, check_vma=False
    )
```

profile of v0, /device:TPU:0, one launch (start us, length us, event | category | flops | bytes accessed | tf_op | source)
XLA Modules:
  0.0 60.5 jit_solution(11132772188094830634)
XLA Ops:
  2.0 1.4 %plan_requests.1 = (s32[8,128]{1,0:T(8,128)S(1)}, s32[16]{0:T(128)S(1)}, s32[16]{0:T(128)S(1)}) custom-call(s32[4,4]{1,0:T(4,128)S(1)} %copy-done.6, s32[4,4]{1,0:T(4,128)S(1)} %copy-done.7), custom_call_target="tpu_custom_call" | custom-call | bytes 10000 | tf_op jit(solution)/shard_map/plan_requests/pallas_call | solution.py:299
  3.9 0.8 %collective-permute-done.refs_1_ = s32[1,8,128]{2,1,0:T(8,128)S(1)} collective-permute-done((s32[1,8,128]{2,1,0:T(8,128)S(1)}, s32[1,8,128]{2,1,0:T(8,128)S(1)}, u32[]{:S(2)}, u32[]{:S(2)}) %collective-permute-start) | collective-permute-done | bytes 4128 | tf_op jit(solution)/shard_map/ppermute | solution.py:314
  4.7 2.8 %collective-permute-start.1 = (s32[2,8,128]{2,1,0:T(8,128)S(1)}, s32[2,8,128]{2,1,0:T(8,128)S(1)}, u32[]{:S(2)}, u32[]{:S(2)}) collective-permute-start(s32[2,8,128]{2,1,0:T(8,128)S(1)} %pad_add_fusion.1), channel_id=1, source_target_pairs={{0,8},{4,12},{8,0},{12,4},{16,24},{20,28},{24,16},{28,20},{1,9},{5... | collective-permute-start | bytes 24584 | tf_op jit(solution)/shard_map/ppermute | solution.py:314
  7.5 1.6 %collective-permute-done.1.refs_2_ = s32[2,8,128]{2,1,0:T(8,128)S(1)} collective-permute-done((s32[2,8,128]{2,1,0:T(8,128)S(1)}, s32[2,8,128]{2,1,0:T(8,128)S(1)}, u32[]{:S(2)}, u32[]{:S(2)}) %collective-permute-start.1) | collective-permute-done | bytes 8224 | tf_op jit(solution)/shard_map/ppermute | solution.py:314
  9.2 2.1 %collective-permute-start.2 = (s32[4,8,128]{2,1,0:T(8,128)S(1)}, s32[4,8,128]{2,1,0:T(8,128)S(1)}, u32[]{:S(2)}, u32[]{:S(2)}) collective-permute-start(s32[4,8,128]{2,1,0:T(8,128)S(1)} %pad_add_fusion), channel_id=1, source_target_pairs={{0,16},{4,20},{8,24},{12,28},{16,0},{20,4},{24,8},{28,12},{1,17},{... | collective-permute-start | bytes 49160 | tf_op jit(solution)/shard_map/ppermute | solution.py:314
  11.2 1.0 %copy-done = bf16[64,4,1024]{2,1,0:T(4,128)(2,1)S(1)} copy-done((bf16[64,4,1024]{2,1,0:T(4,128)(2,1)S(1)}, bf16[64,4,1024]{2,1,0:T(4,128)(2,1)}, u32[]{:S(2)}) %copy-start) | copy-done | bytes 524312
  12.3 1.0 %copy-done.1 = bf16[64,4,1024]{2,1,0:T(4,128)(2,1)S(1)} copy-done((bf16[64,4,1024]{2,1,0:T(4,128)(2,1)S(1)}, bf16[64,4,1024]{2,1,0:T(4,128)(2,1)}, u32[]{:S(2)}) %copy-start.1) | copy-done | bytes 524312
  13.3 0.9 %copy-done.2 = bf16[256,256]{1,0:T(8,128)(2,1)S(1)} copy-done((bf16[256,256]{1,0:T(8,128)(2,1)S(1)}, bf16[256,256]{1,0:T(8,128)(2,1)}, u32[]{:S(2)}) %copy-start.2) | copy-done | bytes 131096
  14.2 0.9 %copy-done.4 = bf16[256,256]{1,0:T(8,128)(2,1)S(1)} copy-done((bf16[256,256]{1,0:T(8,128)(2,1)S(1)}, bf16[256,256]{1,0:T(8,128)(2,1)}, u32[]{:S(2)}) %copy-start.4) | copy-done | bytes 131096
  16.3 1.6 %collective-permute-start.4 = (bf16[16,2048]{1,0:T(8,128)(2,1)S(1)}, bf16[16,2048]{1,0:T(8,128)(2,1)S(1)}, u32[]{:S(2)}, u32[]{:S(2)}) collective-permute-start(bf16[16,2048]{1,0:T(8,128)(2,1)S(1)} %get-tuple-element.74), channel_id=1, source_target_pairs={{0,8},{4,12},{8,0},{12,4},{16,24},{20,28},{24,16},{28,20},{1,9},{5... | collective-permute-start | bytes 196616 | tf_op jit(solution)/shard_map/ppermute | solution.py:314
  18.5 1.4 %collective-permute-start.7 = (bf16[16,2048]{1,0:T(8,128)(2,1)S(1)}, bf16[16,2048]{1,0:T(8,128)(2,1)S(1)}, u32[]{:S(2)}, u32[]{:S(2)}) collective-permute-start(bf16[16,2048]{1,0:T(8,128)(2,1)S(1)} %get-tuple-element.77), channel_id=1, source_target_pairs={{0,20},{4,16},{8,28},{12,24},{16,4},{20,0},{24,12},{28,8},{1,21},{... | collective-permute-start | bytes 196616 | tf_op jit(solution)/shard_map/ppermute | solution.py:314
  19.9 1.4 %collective-permute-start.8 = (bf16[16,2048]{1,0:T(8,128)(2,1)S(1)}, bf16[16,2048]{1,0:T(8,128)(2,1)S(1)}, u32[]{:S(2)}, u32[]{:S(2)}) collective-permute-start(bf16[16,2048]{1,0:T(8,128)(2,1)S(1)} %get-tuple-element.78), channel_id=1, source_target_pairs={{0,24},{4,28},{8,16},{12,20},{16,8},{20,12},{24,0},{28,4},{1,25},{... | collective-permute-start | bytes 196616 | tf_op jit(solution)/shard_map/ppermute | solution.py:314
  21.3 1.3 %collective-permute-start.9 = (bf16[16,2048]{1,0:T(8,128)(2,1)S(1)}, bf16[16,2048]{1,0:T(8,128)(2,1)S(1)}, u32[]{:S(2)}, u32[]{:S(2)}) collective-permute-start(bf16[16,2048]{1,0:T(8,128)(2,1)S(1)} %get-tuple-element.79), channel_id=1, source_target_pairs={{0,28},{4,24},{8,20},{12,16},{16,12},{20,8},{24,4},{28,0},{1,29},{... | collective-permute-start | bytes 196616 | tf_op jit(solution)/shard_map/ppermute | solution.py:314
  22.6 2.2 %collective-permute-start.13 = (bf16[128,512]{1,0:T(8,128)(2,1)S(1)}, bf16[128,512]{1,0:T(8,128)(2,1)S(1)}, u32[]{:S(2)}, u32[]{:S(2)}) collective-permute-start(bf16[128,512]{1,0:T(8,128)(2,1)S(1)} %get-tuple-element.86), channel_id=1, source_target_pairs={{0,4},{4,8},{8,12},{12,16},{16,20},{20,24},{24,28},{1,5},{5,9},{9,... | collective-permute-start | bytes 393224 | tf_op jit(solution)/shard_map/ppermute | solution.py:396
  25.4 1.0 %collective-permute-done.9.refs_7_ = bf16[16,2048]{1,0:T(8,128)(2,1)S(1)} collective-permute-done((bf16[16,2048]{1,0:T(8,128)(2,1)S(1)}, bf16[16,2048]{1,0:T(8,128)(2,1)S(1)}, u32[]{:S(2)}, u32[]{:S(2)}) %collective-permute-start.9) | collective-permute-done | bytes 65568 | tf_op jit(solution)/shard_map/ppermute | solution.py:314
  26.8 1.6 %collective-permute-start.10 = (bf16[64,512]{1,0:T(8,128)(2,1)S(1)}, bf16[64,512]{1,0:T(8,128)(2,1)S(1)}, u32[]{:S(2)}, u32[]{:S(2)}) collective-permute-start(bf16[64,512]{1,0:T(8,128)(2,1)S(1)} %get-tuple-element.81), channel_id=1, source_target_pairs={{0,1},{1,0},{2,3},{3,2},{4,5},{5,4},{6,7},{7,6},{8,9},{9,8},{10,11... | collective-permute-start | bytes 196616 | tf_op jit(solution)/shard_map/ppermute | solution.py:314
  28.4 2.6 %collective-permute-start.11 = (bf16[64,512]{1,0:T(8,128)(2,1)S(1)}, bf16[64,512]{1,0:T(8,128)(2,1)S(1)}, u32[]{:S(2)}, u32[]{:S(2)}) collective-permute-start(bf16[64,512]{1,0:T(8,128)(2,1)S(1)} %get-tuple-element.82), channel_id=1, source_target_pairs={{0,2},{1,3},{2,0},{3,1},{4,6},{5,7},{6,4},{7,5},{8,10},{9,11},{10,... | collective-permute-start | bytes 196616 | tf_op jit(solution)/shard_map/ppermute | solution.py:314
  31.2 4.7 %collective-permute-done.11.refs_2_ = bf16[64,512]{1,0:T(8,128)(2,1)S(1)} collective-permute-done((bf16[64,512]{1,0:T(8,128)(2,1)S(1)}, bf16[64,512]{1,0:T(8,128)(2,1)S(1)}, u32[]{:S(2)}, u32[]{:S(2)}) %collective-permute-start.11) | collective-permute-done | bytes 65568 | tf_op jit(solution)/shard_map/ppermute | solution.py:314
  35.9 1.2 %collective-permute-done.12.refs_3_ = bf16[64,512]{1,0:T(8,128)(2,1)S(1)} collective-permute-done((bf16[64,512]{1,0:T(8,128)(2,1)S(1)}, bf16[64,512]{1,0:T(8,128)(2,1)S(1)}, u32[]{:S(2)}, u32[]{:S(2)}) %collective-permute-start.12) | collective-permute-done | bytes 65568 | tf_op jit(solution)/shard_map/ppermute | solution.py:314
  37.9 0.9 %collective-permute-start.15 = (bf16[64,512]{1,0:T(8,128)(2,1)S(1)}, bf16[64,512]{1,0:T(8,128)(2,1)S(1)}, u32[]{:S(2)}, u32[]{:S(2)}) collective-permute-start(bf16[64,512]{1,0:T(8,128)(2,1)S(1)} %get-tuple-element.97), channel_id=1, source_target_pairs={{0,1},{1,0},{2,3},{3,2},{4,5},{5,4},{6,7},{7,6},{8,9},{9,8},{10,11... | collective-permute-start | bytes 196616 | tf_op jit(solution)/shard_map/ppermute | solution.py:314
  38.8 1.7 %collective-permute-start.16 = (bf16[64,512]{1,0:T(8,128)(2,1)S(1)}, bf16[64,512]{1,0:T(8,128)(2,1)S(1)}, u32[]{:S(2)}, u32[]{:S(2)}) collective-permute-start(bf16[64,512]{1,0:T(8,128)(2,1)S(1)} %get-tuple-element.98), channel_id=1, source_target_pairs={{0,2},{1,3},{2,0},{3,1},{4,6},{5,7},{6,4},{7,5},{8,10},{9,11},{10,... | collective-permute-start | bytes 196616 | tf_op jit(solution)/shard_map/ppermute | solution.py:314
  40.5 1.8 %collective-permute-start.17 = (bf16[64,512]{1,0:T(8,128)(2,1)S(1)}, bf16[64,512]{1,0:T(8,128)(2,1)S(1)}, u32[]{:S(2)}, u32[]{:S(2)}) collective-permute-start(bf16[64,512]{1,0:T(8,128)(2,1)S(1)} %get-tuple-element.99), channel_id=1, source_target_pairs={{0,3},{1,2},{2,1},{3,0},{4,7},{5,6},{6,5},{7,4},{8,11},{9,10},{10,... | collective-permute-start | bytes 196616 | tf_op jit(solution)/shard_map/ppermute | solution.py:314
  42.4 2.9 %self_attention.1 = (f32[256,1024]{1,0:T(8,128)S(1)}, f32[256,1024]{1,0:T(8,128)S(1)}, f32[256,512]{1,0:T(8,128)S(1)}, bf16[128,512]{1,0:T(8,128)(2,1)S(1)}) custom-call(s32[1]{0:T(128)} %bitcast.1.me_ref.rank_ref, bf16[256,1024]{1,0:T(8,128)(2,1)S(1)} %copy-done.8, bf16[256,256]{1,0:T(8,128)(2,1)S(1)} %copy-done.3, bf16[256,256]{1,0:T(8,128)(2,1)S(1)} %copy-done.5, ...), custom_call_target="tpu_custom_call" | custom-call | flops 1600000000 | bytes 6000000 | tf_op jit(solution)/shard_map/self_attention/pallas_call | solution.py:299
  45.3 1.3 %collective-permute-start.14 = (bf16[128,512]{1,0:T(8,128)(2,1)S(1)}, bf16[128,512]{1,0:T(8,128)(2,1)S(1)}, u32[]{:S(2)}, u32[]{:S(2)}) collective-permute-start(bf16[128,512]{1,0:T(8,128)(2,1)S(1)} %get-tuple-element.90), channel_id=1, source_target_pairs={{4,0},{8,4},{12,8},{16,12},{20,16},{24,20},{28,24},{5,1},{9,5},{13... | collective-permute-start | bytes 393224 | tf_op jit(solution)/shard_map/ppermute | solution.py:437
  46.9 1.2 %collective-permute-start.18 = (bf16[16,2048]{1,0:T(8,128)(2,1)S(1)}, bf16[16,2048]{1,0:T(8,128)(2,1)S(1)}, u32[]{:S(2)}, u32[]{:S(2)}) collective-permute-start(bf16[16,2048]{1,0:T(8,128)(2,1)S(1)} %get-tuple-element.101), channel_id=1, source_target_pairs={{0,4},{4,0},{8,12},{12,8},{16,20},{20,16},{24,28},{28,24},{1,5},{5... | collective-permute-start | bytes 196616 | tf_op jit(solution)/shard_map/ppermute | solution.py:314
  48.1 1.6 %collective-permute-start.19 = (bf16[16,2048]{1,0:T(8,128)(2,1)S(1)}, bf16[16,2048]{1,0:T(8,128)(2,1)S(1)}, u32[]{:S(2)}, u32[]{:S(2)}) collective-permute-start(bf16[16,2048]{1,0:T(8,128)(2,1)S(1)} %get-tuple-element.102), channel_id=1, source_target_pairs={{0,8},{4,12},{8,0},{12,4},{16,24},{20,28},{24,16},{28,20},{1,9},{5... | collective-permute-start | bytes 196616 | tf_op jit(solution)/shard_map/ppermute | solution.py:314
  49.7 1.1 %collective-permute-start.21 = (bf16[16,2048]{1,0:T(8,128)(2,1)S(1)}, bf16[16,2048]{1,0:T(8,128)(2,1)S(1)}, u32[]{:S(2)}, u32[]{:S(2)}) collective-permute-start(bf16[16,2048]{1,0:T(8,128)(2,1)S(1)} %get-tuple-element.104), channel_id=1, source_target_pairs={{0,16},{4,20},{8,24},{12,28},{16,0},{20,4},{24,8},{28,12},{1,17},{... | collective-permute-start | bytes 196616 | tf_op jit(solution)/shard_map/ppermute | solution.py:314
  51.6 2.9 %collective-permute-start.23 = (bf16[16,2048]{1,0:T(8,128)(2,1)S(1)}, bf16[16,2048]{1,0:T(8,128)(2,1)S(1)}, u32[]{:S(2)}, u32[]{:S(2)}) collective-permute-start(bf16[16,2048]{1,0:T(8,128)(2,1)S(1)} %get-tuple-element.106), channel_id=1, source_target_pairs={{0,24},{4,28},{8,16},{12,20},{16,8},{20,12},{24,0},{28,4},{1,25},{... | collective-permute-start | bytes 196616 | tf_op jit(solution)/shard_map/ppermute | solution.py:314
  54.5 1.6 %join_outputs.1 = (bf16[256,1024]{1,0:T(8,128)(2,1)}, bf16[256,1024]{1,0:T(8,128)(2,1)}, bf16[256,256]{1,0:T(8,128)(2,1)}, bf16[256,256]{1,0:T(8,128)(2,1)}) custom-call(bf16[8,64,256]{2,1,0:T(8,128)(2,1)S(1)} %get-tuple-element.84.w_ref, bf16[8,64,256]{2,1,0:T(8,128)(2,1)S(1)} %get-tuple-element.85.ds_ref, f32[256,1024]{1,0:T(8,128)S(1)} %get-tuple-element.87.out_ref, ...), custom_call_target="tpu_custom_call" | custom-call | flops 300000000 | bytes 5000000 | tf_op jit(solution)/shard_map/join_outputs/pallas_call | solution.py:299
  56.1 1.1 %collective-permute-done.23.refs_6_ = bf16[16,2048]{1,0:T(8,128)(2,1)S(1)} collective-permute-done((bf16[16,2048]{1,0:T(8,128)(2,1)S(1)}, bf16[16,2048]{1,0:T(8,128)(2,1)S(1)}, u32[]{:S(2)}, u32[]{:S(2)}) %collective-permute-start.23) | collective-permute-done | bytes 65568 | tf_op jit(solution)/shard_map/ppermute | solution.py:314
  57.3 1.8 %collective-permute-done.24.refs_7_ = bf16[16,2048]{1,0:T(8,128)(2,1)S(1)} collective-permute-done((bf16[16,2048]{1,0:T(8,128)(2,1)S(1)}, bf16[16,2048]{1,0:T(8,128)(2,1)S(1)}, u32[]{:S(2)}, u32[]{:S(2)}) %collective-permute-start.24) | collective-permute-done | bytes 65568 | tf_op jit(solution)/shard_map/ppermute | solution.py:314
  59.1 1.4 %sum_store_gradients.1 = (bf16[64,4,1024]{2,1,0:T(4,128)(2,1)}, bf16[64,4,1024]{2,1,0:T(4,128)(2,1)}) custom-call(bf16[256,128]{1,0:T(8,128)(2,1)S(1)} %get-tuple-element.95.owned_ref, bf16[16,2048]{1,0:T(8,128)(2,1)S(1)} %get-tuple-element.100.refs_0_, bf16[16,2048]{1,0:T(8,128)(2,1)S(1)} %collective-permute-done.18.refs_1_, ...), custom_call_target="tpu_custom_call" | custom-call | flops 200000000 | bytes 2000000 | tf_op jit(solution)/shard_map/sum_store_gradients/pallas_call | solution.py:299
  (49 shorter events, 6.6 us)
Async XLA Ops:
  3.4 1.3 %collective-permute-start = (s32[1,8,128]{2,1,0:T(8,128)S(1)}, s32[1,8,128]{2,1,0:T(8,128)S(1)}, u32[]{:S(2)}, u32[]{:S(2)}) collective-permute-start(s32[1,8,128]{2,1,0:T(8,128)S(1)} %bitcast.3), channel_id=1, source_target_pairs={{0,4},{4,0},{8,12},{12,8},{16,20},{20,16},{24,28},{28,24},{1,5},{5... | collective-permute-start | bytes 12296 | tf_op jit(solution)/shard_map/ppermute | solution.py:314
  4.7 4.5 %collective-permute-start.1 = (s32[2,8,128]{2,1,0:T(8,128)S(1)}, s32[2,8,128]{2,1,0:T(8,128)S(1)}, u32[]{:S(2)}, u32[]{:S(2)}) collective-permute-start(s32[2,8,128]{2,1,0:T(8,128)S(1)} %pad_add_fusion.1), channel_id=1, source_target_pairs={{0,8},{4,12},{8,0},{12,4},{16,24},{20,28},{24,16},{28,20},{1,9},{5... | collective-permute-start | bytes 24584 | tf_op jit(solution)/shard_map/ppermute | solution.py:314
  9.2 6.7 %collective-permute-start.2 = (s32[4,8,128]{2,1,0:T(8,128)S(1)}, s32[4,8,128]{2,1,0:T(8,128)S(1)}, u32[]{:S(2)}, u32[]{:S(2)}) collective-permute-start(s32[4,8,128]{2,1,0:T(8,128)S(1)} %pad_add_fusion), channel_id=1, source_target_pairs={{0,16},{4,20},{8,24},{12,28},{16,0},{20,4},{24,8},{28,12},{1,17},{... | collective-permute-start | bytes 49160 | tf_op jit(solution)/shard_map/ppermute | solution.py:314
  11.2 1.0 %copy-start = (bf16[64,4,1024]{2,1,0:T(4,128)(2,1)S(1)}, bf16[64,4,1024]{2,1,0:T(4,128)(2,1)}, u32[]{:S(2)}) copy-start(bf16[64,4,1024]{2,1,0:T(4,128)(2,1)} %k_ref.2) | copy-start | bytes 1572868
  12.3 1.0 %copy-start.1 = (bf16[64,4,1024]{2,1,0:T(4,128)(2,1)S(1)}, bf16[64,4,1024]{2,1,0:T(4,128)(2,1)}, u32[]{:S(2)}) copy-start(bf16[64,4,1024]{2,1,0:T(4,128)(2,1)} %v_ref.2) | copy-start | bytes 1572868
  13.3 0.9 %copy-start.2 = (bf16[256,256]{1,0:T(8,128)(2,1)S(1)}, bf16[256,256]{1,0:T(8,128)(2,1)}, u32[]{:S(2)}) copy-start(bf16[256,256]{1,0:T(8,128)(2,1)} %k_ref.3) | copy-start | bytes 393220
  15.9 21.3 %copy-start.9 = (bf16[256,1024]{1,0:T(8,128)(2,1)S(1)}, bf16[256,1024]{1,0:T(8,128)(2,1)}, u32[]{:S(2)}) copy-start(bf16[256,1024]{1,0:T(8,128)(2,1)} %do_ref.3) | copy-start | bytes 1572868
  16.2 20.9 %copy-start.8 = (bf16[256,1024]{1,0:T(8,128)(2,1)S(1)}, bf16[256,1024]{1,0:T(8,128)(2,1)}, u32[]{:S(2)}) copy-start(bf16[256,1024]{1,0:T(8,128)(2,1)} %q_ref.3) | copy-start | bytes 1572868
  16.3 3.6 %collective-permute-start.3 = (bf16[16,2048]{1,0:T(8,128)(2,1)S(1)}, bf16[16,2048]{1,0:T(8,128)(2,1)S(1)}, u32[]{:S(2)}, u32[]{:S(2)}) collective-permute-start(bf16[16,2048]{1,0:T(8,128)(2,1)S(1)} %get-tuple-element.73), channel_id=1, source_target_pairs={{0,4},{4,0},{8,12},{12,8},{16,20},{20,16},{24,28},{28,24},{1,5},{5... | collective-permute-start | bytes 196616 | tf_op jit(solution)/shard_map/ppermute | solution.py:314
  16.3 5.0 %collective-permute-start.4 = (bf16[16,2048]{1,0:T(8,128)(2,1)S(1)}, bf16[16,2048]{1,0:T(8,128)(2,1)S(1)}, u32[]{:S(2)}, u32[]{:S(2)}) collective-permute-start(bf16[16,2048]{1,0:T(8,128)(2,1)S(1)} %get-tuple-element.74), channel_id=1, source_target_pairs={{0,8},{4,12},{8,0},{12,4},{16,24},{20,28},{24,16},{28,20},{1,9},{5... | collective-permute-start | bytes 196616 | tf_op jit(solution)/shard_map/ppermute | solution.py:314
  17.9 4.7 %collective-permute-start.5 = (bf16[16,2048]{1,0:T(8,128)(2,1)S(1)}, bf16[16,2048]{1,0:T(8,128)(2,1)S(1)}, u32[]{:S(2)}, u32[]{:S(2)}) collective-permute-start(bf16[16,2048]{1,0:T(8,128)(2,1)S(1)} %get-tuple-element.75), channel_id=1, source_target_pairs={{0,12},{4,8},{8,4},{12,0},{16,28},{20,24},{24,20},{28,16},{1,13},{... | collective-permute-start | bytes 196616 | tf_op jit(solution)/shard_map/ppermute | solution.py:314
  18.2 6.7 %collective-permute-start.6 = (bf16[16,2048]{1,0:T(8,128)(2,1)S(1)}, bf16[16,2048]{1,0:T(8,128)(2,1)S(1)}, u32[]{:S(2)}, u32[]{:S(2)}) collective-permute-start(bf16[16,2048]{1,0:T(8,128)(2,1)S(1)} %get-tuple-element.76), channel_id=1, source_target_pairs={{0,16},{4,20},{8,24},{12,28},{16,0},{20,4},{24,8},{28,12},{1,17},{... | collective-permute-start | bytes 196616 | tf_op jit(solution)/shard_map/ppermute | solution.py:314
  18.5 6.4 %collective-permute-start.7 = (bf16[16,2048]{1,0:T(8,128)(2,1)S(1)}, bf16[16,2048]{1,0:T(8,128)(2,1)S(1)}, u32[]{:S(2)}, u32[]{:S(2)}) collective-permute-start(bf16[16,2048]{1,0:T(8,128)(2,1)S(1)} %get-tuple-element.77), channel_id=1, source_target_pairs={{0,20},{4,16},{8,28},{12,24},{16,4},{20,0},{24,12},{28,8},{1,21},{... | collective-permute-start | bytes 196616 | tf_op jit(solution)/shard_map/ppermute | solution.py:314
  19.9 5.5 %collective-permute-start.8 = (bf16[16,2048]{1,0:T(8,128)(2,1)S(1)}, bf16[16,2048]{1,0:T(8,128)(2,1)S(1)}, u32[]{:S(2)}, u32[]{:S(2)}) collective-permute-start(bf16[16,2048]{1,0:T(8,128)(2,1)S(1)} %get-tuple-element.78), channel_id=1, source_target_pairs={{0,24},{4,28},{8,16},{12,20},{16,8},{20,12},{24,0},{28,4},{1,25},{... | collective-permute-start | bytes 196616 | tf_op jit(solution)/shard_map/ppermute | solution.py:314
  21.3 5.1 %collective-permute-start.9 = (bf16[16,2048]{1,0:T(8,128)(2,1)S(1)}, bf16[16,2048]{1,0:T(8,128)(2,1)S(1)}, u32[]{:S(2)}, u32[]{:S(2)}) collective-permute-start(bf16[16,2048]{1,0:T(8,128)(2,1)S(1)} %get-tuple-element.79), channel_id=1, source_target_pairs={{0,28},{4,24},{8,20},{12,16},{16,12},{20,8},{24,4},{28,0},{1,29},{... | collective-permute-start | bytes 196616 | tf_op jit(solution)/shard_map/ppermute | solution.py:314
  22.6 19.8 %collective-permute-start.13 = (bf16[128,512]{1,0:T(8,128)(2,1)S(1)}, bf16[128,512]{1,0:T(8,128)(2,1)S(1)}, u32[]{:S(2)}, u32[]{:S(2)}) collective-permute-start(bf16[128,512]{1,0:T(8,128)(2,1)S(1)} %get-tuple-element.86), channel_id=1, source_target_pairs={{0,4},{4,8},{8,12},{12,16},{16,20},{20,24},{24,28},{1,5},{5,9},{9,... | collective-permute-start | bytes 393224 | tf_op jit(solution)/shard_map/ppermute | solution.py:396
  26.8 4.5 %collective-permute-start.10 = (bf16[64,512]{1,0:T(8,128)(2,1)S(1)}, bf16[64,512]{1,0:T(8,128)(2,1)S(1)}, u32[]{:S(2)}, u32[]{:S(2)}) collective-permute-start(bf16[64,512]{1,0:T(8,128)(2,1)S(1)} %get-tuple-element.81), channel_id=1, source_target_pairs={{0,1},{1,0},{2,3},{3,2},{4,5},{5,4},{6,7},{7,6},{8,9},{9,8},{10,11... | collective-permute-start | bytes 196616 | tf_op jit(solution)/shard_map/ppermute | solution.py:314
  28.4 7.5 %collective-permute-start.11 = (bf16[64,512]{1,0:T(8,128)(2,1)S(1)}, bf16[64,512]{1,0:T(8,128)(2,1)S(1)}, u32[]{:S(2)}, u32[]{:S(2)}) collective-permute-start(bf16[64,512]{1,0:T(8,128)(2,1)S(1)} %get-tuple-element.82), channel_id=1, source_target_pairs={{0,2},{1,3},{2,0},{3,1},{4,6},{5,7},{6,4},{7,5},{8,10},{9,11},{10,... | collective-permute-start | bytes 196616 | tf_op jit(solution)/shard_map/ppermute | solution.py:314
  31.0 6.2 %collective-permute-start.12 = (bf16[64,512]{1,0:T(8,128)(2,1)S(1)}, bf16[64,512]{1,0:T(8,128)(2,1)S(1)}, u32[]{:S(2)}, u32[]{:S(2)}) collective-permute-start(bf16[64,512]{1,0:T(8,128)(2,1)S(1)} %get-tuple-element.83), channel_id=1, source_target_pairs={{0,3},{1,2},{2,1},{3,0},{4,7},{5,6},{6,5},{7,4},{8,11},{9,10},{10,... | collective-permute-start | bytes 196616 | tf_op jit(solution)/shard_map/ppermute | solution.py:314
  37.1 5.2 %copy-start.3 = (bf16[256,256]{1,0:T(8,128)(2,1)S(1)}, bf16[256,256]{1,0:T(8,128)(2,1)}, u32[]{:S(2)}) copy-start(bf16[256,256]{1,0:T(8,128)(2,1)} %k_ref.3) | copy-start | bytes 393220
  37.1 5.2 %copy-start.5 = (bf16[256,256]{1,0:T(8,128)(2,1)S(1)}, bf16[256,256]{1,0:T(8,128)(2,1)}, u32[]{:S(2)}) copy-start(bf16[256,256]{1,0:T(8,128)(2,1)} %v_ref.3) | copy-start | bytes 393220
  37.9 8.7 %collective-permute-start.15 = (bf16[64,512]{1,0:T(8,128)(2,1)S(1)}, bf16[64,512]{1,0:T(8,128)(2,1)S(1)}, u32[]{:S(2)}, u32[]{:S(2)}) collective-permute-start(bf16[64,512]{1,0:T(8,128)(2,1)S(1)} %get-tuple-element.97), channel_id=1, source_target_pairs={{0,1},{1,0},{2,3},{3,2},{4,5},{5,4},{6,7},{7,6},{8,9},{9,8},{10,11... | collective-permute-start | bytes 196616 | tf_op jit(solution)/shard_map/ppermute | solution.py:314
  38.8 7.8 %collective-permute-start.16 = (bf16[64,512]{1,0:T(8,128)(2,1)S(1)}, bf16[64,512]{1,0:T(8,128)(2,1)S(1)}, u32[]{:S(2)}, u32[]{:S(2)}) collective-permute-start(bf16[64,512]{1,0:T(8,128)(2,1)S(1)} %get-tuple-element.98), channel_id=1, source_target_pairs={{0,2},{1,3},{2,0},{3,1},{4,6},{5,7},{6,4},{7,5},{8,10},{9,11},{10,... | collective-permute-start | bytes 196616 | tf_op jit(solution)/shard_map/ppermute | solution.py:314
  40.5 6.1 %collective-permute-start.17 = (bf16[64,512]{1,0:T(8,128)(2,1)S(1)}, bf16[64,512]{1,0:T(8,128)(2,1)S(1)}, u32[]{:S(2)}, u32[]{:S(2)}) collective-permute-start(bf16[64,512]{1,0:T(8,128)(2,1)S(1)} %get-tuple-element.99), channel_id=1, source_target_pairs={{0,3},{1,2},{2,1},{3,0},{4,7},{5,6},{6,5},{7,4},{8,11},{9,10},{10,... | collective-permute-start | bytes 196616 | tf_op jit(solution)/shard_map/ppermute | solution.py:314
  45.3 5.6 %collective-permute-start.14 = (bf16[128,512]{1,0:T(8,128)(2,1)S(1)}, bf16[128,512]{1,0:T(8,128)(2,1)S(1)}, u32[]{:S(2)}, u32[]{:S(2)}) collective-permute-start(bf16[128,512]{1,0:T(8,128)(2,1)S(1)} %get-tuple-element.90), channel_id=1, source_target_pairs={{4,0},{8,4},{12,8},{16,12},{20,16},{24,20},{28,24},{5,1},{9,5},{13... | collective-permute-start | bytes 393224 | tf_op jit(solution)/shard_map/ppermute | solution.py:437
  46.9 4.7 %collective-permute-start.18 = (bf16[16,2048]{1,0:T(8,128)(2,1)S(1)}, bf16[16,2048]{1,0:T(8,128)(2,1)S(1)}, u32[]{:S(2)}, u32[]{:S(2)}) collective-permute-start(bf16[16,2048]{1,0:T(8,128)(2,1)S(1)} %get-tuple-element.101), channel_id=1, source_target_pairs={{0,4},{4,0},{8,12},{12,8},{16,20},{20,16},{24,28},{28,24},{1,5},{5... | collective-permute-start | bytes 196616 | tf_op jit(solution)/shard_map/ppermute | solution.py:314
  48.1 6.4 %collective-permute-start.19 = (bf16[16,2048]{1,0:T(8,128)(2,1)S(1)}, bf16[16,2048]{1,0:T(8,128)(2,1)S(1)}, u32[]{:S(2)}, u32[]{:S(2)}) collective-permute-start(bf16[16,2048]{1,0:T(8,128)(2,1)S(1)} %get-tuple-element.102), channel_id=1, source_target_pairs={{0,8},{4,12},{8,0},{12,4},{16,24},{20,28},{24,16},{28,20},{1,9},{5... | collective-permute-start | bytes 196616 | tf_op jit(solution)/shard_map/ppermute | solution.py:314
  49.7 6.4 %collective-permute-start.20 = (bf16[16,2048]{1,0:T(8,128)(2,1)S(1)}, bf16[16,2048]{1,0:T(8,128)(2,1)S(1)}, u32[]{:S(2)}, u32[]{:S(2)}) collective-permute-start(bf16[16,2048]{1,0:T(8,128)(2,1)S(1)} %get-tuple-element.103), channel_id=1, source_target_pairs={{0,12},{4,8},{8,4},{12,0},{16,28},{20,24},{24,20},{28,16},{1,13},{... | collective-permute-start | bytes 196616 | tf_op jit(solution)/shard_map/ppermute | solution.py:314
  49.7 6.4 %collective-permute-start.21 = (bf16[16,2048]{1,0:T(8,128)(2,1)S(1)}, bf16[16,2048]{1,0:T(8,128)(2,1)S(1)}, u32[]{:S(2)}, u32[]{:S(2)}) collective-permute-start(bf16[16,2048]{1,0:T(8,128)(2,1)S(1)} %get-tuple-element.104), channel_id=1, source_target_pairs={{0,16},{4,20},{8,24},{12,28},{16,0},{20,4},{24,8},{28,12},{1,17},{... | collective-permute-start | bytes 196616 | tf_op jit(solution)/shard_map/ppermute | solution.py:314
  50.9 5.3 %collective-permute-start.22 = (bf16[16,2048]{1,0:T(8,128)(2,1)S(1)}, bf16[16,2048]{1,0:T(8,128)(2,1)S(1)}, u32[]{:S(2)}, u32[]{:S(2)}) collective-permute-start(bf16[16,2048]{1,0:T(8,128)(2,1)S(1)} %get-tuple-element.105), channel_id=1, source_target_pairs={{0,20},{4,16},{8,28},{12,24},{16,4},{20,0},{24,12},{28,8},{1,21},{... | collective-permute-start | bytes 196616 | tf_op jit(solution)/shard_map/ppermute | solution.py:314
  51.6 5.7 %collective-permute-start.23 = (bf16[16,2048]{1,0:T(8,128)(2,1)S(1)}, bf16[16,2048]{1,0:T(8,128)(2,1)S(1)}, u32[]{:S(2)}, u32[]{:S(2)}) collective-permute-start(bf16[16,2048]{1,0:T(8,128)(2,1)S(1)} %get-tuple-element.106), channel_id=1, source_target_pairs={{0,24},{4,28},{8,16},{12,20},{16,8},{20,12},{24,0},{28,4},{1,25},{... | collective-permute-start | bytes 196616 | tf_op jit(solution)/shard_map/ppermute | solution.py:314
  54.5 4.6 %collective-permute-start.24 = (bf16[16,2048]{1,0:T(8,128)(2,1)S(1)}, bf16[16,2048]{1,0:T(8,128)(2,1)S(1)}, u32[]{:S(2)}, u32[]{:S(2)}) collective-permute-start(bf16[16,2048]{1,0:T(8,128)(2,1)S(1)} %get-tuple-element.107), channel_id=1, source_target_pairs={{0,28},{4,24},{8,20},{12,16},{16,12},{20,8},{24,4},{28,0},{1,29},{... | collective-permute-start | bytes 196616 | tf_op jit(solution)/shard_map/ppermute | solution.py:314
  (3 other events, 2.3 us)
where the time goes:
time: 60.8 us; the launch traced here: 60.5 us
  starting transfers between devices  31.8 us (52%)
  waiting for transfers between devices  13 us (21%)
  Pallas kernels  9.62 us (16%)
  local copies, waits for them, and re-layouts  5.27 us (9%)
  between operations  0.82 us (1%)
    ppermute x23, starting transfers between devices, swapped(): lax.ppermute(block, axis, [(i, i ^ apart) for i in range(lax.axis_size(ax...  28.3 us
    ppermute x23, waiting for transfers between devices, swapped(): lax.ppermute(block, axis, [(i, i ^ apart) for i in range(lax.axis_size(ax...  13 us
    pallas_call x9, Pallas kernels, call(): pl.pallas_call(kernel, out_shape=tuple(outs), in_specs=places or [SMEM] *...  9.62 us
    unnamed x20, local copies, waits for them, and re-layouts  5.27 us
    ppermute x1, starting transfers between devices, body(): halo = lax.ppermute(halo, 'seq', [(i, i + 1) for i in range(devices - 1)])  2.23 us
    ppermute x1, starting transfers between devices, body(): back = lax.ppermute(back, 'seq', [(i + 1, i) for i in range(devices - 1)])  1.29 us
  transfers between devices with their start and end apart: 25, of which 8 were waited for; matrix products, arithmetic and copies ran while one was open for 0% of the time, Pallas kernels for 11%

commit v1 on v0

--- a/solution.py
+++ b/solution.py
@@ -23,9 +23,8 @@
 BF16 = jnp.bfloat16
 VMEM = pl.BlockSpec(memory_space=pltpu.VMEM)
 SMEM = pl.BlockSpec(memory_space=pltpu.SMEM)
-HBM = pl.BlockSpec(memory_space=pltpu.HBM)
+ANY = pl.BlockSpec(memory_space=pl.ANY)
 LANES = 128
-PARAMS = pltpu.CompilerParams(vmem_limit_bytes=16 * 1024 * 1024)
 
 
 def dot_nn(a, b):
@@ -64,16 +63,13 @@
     return probs.astype(BF16), grad_scores
 
 
-def plan_kernel(
-    tokens, cap, owner_hbm, slot_hbm, want_ref, owner_out, rank_out, owner_ref, slot_ref, sems
-):
+def plan_kernel(tokens, cap, owner_any, slot_any, want_ref, owner_ref, slot_ref, sems):
     copies = [
-        pltpu.make_async_copy(owner_hbm, owner_ref, sems.at[0]),
-        pltpu.make_async_copy(slot_hbm, slot_ref, sems.at[1]),
+        pltpu.make_async_copy(owner_any, owner_ref, sems.at[0]),
+        pltpu.make_async_copy(slot_any, slot_ref, sems.at[1]),
     ]
     for copy in copies:
         copy.start()
-    spans, per_span = owner_ref.shape
     row = lax.broadcasted_iota(jnp.int32, want_ref.shape, 0)
     lane = lax.broadcasted_iota(jnp.int32, want_ref.shape, 1)
     place = row * cap + (lane // tokens) % cap
@@ -81,7 +77,14 @@
     want = jnp.full(want_ref.shape, -1, jnp.int32)
     for copy in copies:
         copy.wait()
-    owners = []
+    for i, j, owner, rank in ranked(owner_ref):
+        want = jnp.where(place == owner * cap + rank, slot_ref[i, j] * tokens + token, want)
+    want_ref[...] = want
+
+
+def ranked(owner_ref):
+    spans, per_span = owner_ref.shape
+    owners, found = [], []
     for i in range(spans):
         for j in range(per_span):
             owner = owner_ref[i, j]
@@ -89,81 +92,109 @@
             for earlier in owners:
                 rank = rank + jnp.where(earlier == owner, 1, 0)
             owners.append(owner)
-            want = jnp.where(place == owner * cap + rank, slot_ref[i, j] * tokens + token, want)
-            owner_out[i * per_span + j] = owner
-            rank_out[i * per_span + j] = rank
-    want_ref[...] = want
+            found.append((i, j, owner, rank))
+    return found
 
 
 def stage_kernel(
-    rows_each, me_ref, owner_ref, rank_ref, k_ref, v_ref, sk_ref, sv_ref, store_ref, halo_ref, placed_ref
+    rows_each,
+    chunks,
+    owner_any,
+    k_any,
+    v_any,
+    sk_any,
+    sv_any,
+    store_ref,
+    halo_ref,
+    placed_ref,
+    owner_ref,
+    k_ref,
+    v_ref,
+    sems,
 ):
     slots, tokens, features = k_ref.shape
-    rows, columns = store_ref.shape
-    kv_width = sk_ref.shape[1]
-    for z in range(features // kv_width):
-        cols = slice(z * kv_width, (z + 1) * kv_width)
-        at = 2 * z * kv_width
-        store_ref[:, at : at + kv_width] = k_ref[:, :, cols].reshape(rows, kv_width)
-        store_ref[:, at + kv_width : at + 2 * kv_width] = v_ref[:, :, cols].reshape(rows, kv_width)
-    halo_ref[:, :kv_width] = sk_ref[sk_ref.shape[0] - halo_ref.shape[0] :]
-    halo_ref[:, kv_width:] = sv_ref[sv_ref.shape[0] - halo_ref.shape[0] :]
+    kv_width = sk_any.shape[1]
+    window = halo_ref.shape[0]
+    tail = slice(sk_any.shape[0] - window, sk_any.shape[0])
+    step = slots // chunks
+    fetch_owner = pltpu.make_async_copy(owner_any, owner_ref, sems.at[2 * chunks + 2])
+    fetch_owner.start()
+    copies = []
+    for i in range(chunks):
+        part = slice(i * step, (i + 1) * step)
+        copies.append(pltpu.make_async_copy(k_any.at[part], k_ref.at[part], sems.at[2 * i]))
+        copies.append(pltpu.make_async_copy(v_any.at[part], v_ref.at[part], sems.at[2 * i + 1]))
+    left, right = slice(0, kv_width), slice(kv_width, 2 * kv_width)
+    copies.append(pltpu.make_async_copy(sk_any.at[tail], halo_ref.at[:, left], sems.at[2 * chunks]))
+    copies.append(
+        pltpu.make_async_copy(sv_any.at[tail], halo_ref.at[:, right], sems.at[2 * chunks + 1])
+    )
+    for copy in copies:
+        copy.start()
+    fetch_owner.wait()
     lanes, used = placed_ref.shape
-    me = me_ref[0]
     lane = lax.broadcasted_iota(jnp.int32, (1, used), 1)
     place = lane % tokens
-    for r in range(used // tokens):
-        first = (owner_ref[r] ^ me) * rows_each + rank_ref[r] * tokens
-        place = place + jnp.where(lane // tokens == r, first, 0)
+    for r, (_, _, owner, rank) in enumerate(ranked(owner_ref)):
+        place = place + jnp.where(lane // tokens == r, owner * rows_each + rank * tokens, 0)
     row = lax.broadcasted_iota(jnp.int32, (lanes, used), 0)
     placed_ref[...] = jnp.where(row == place, 1.0, 0.0).astype(BF16)
-
-
-def pack_kernel(pieces, me_ref, store_ref, *refs):
-    wanted_refs, send_refs, owned_ref = refs[:pieces], refs[pieces:-1], refs[-1]
-    rows_each = send_refs[0].shape[0]
+    for i in range(chunks):
+        copies[2 * i].wait()
+        copies[2 * i + 1].wait()
+        part = slice(i * step, (i + 1) * step)
+        rows = slice(i * step * tokens, (i + 1) * step * tokens)
+        for z in range(features // kv_width):
+            cols = slice(z * kv_width, (z + 1) * kv_width)
+            at = 2 * z * kv_width
+            for ref in (k_ref, v_ref):
+                store_ref[rows, at : at + kv_width] = ref[part, :, cols].reshape(
+                    step * tokens, kv_width
+                )
+                at += kv_width
+    for copy in copies[2 * chunks :]:
+        copy.wait()
+
+
+def pack_kernel(sources, me_ref, store_ref, *refs):
+    *wanted_refs, send_ref, owned_ref = refs
+    devices, rows_each, columns = send_ref.shape
     rows, lanes = owned_ref.shape
     me = me_ref[0]
     width = wanted_refs[0].shape[2]
-    lane = lax.broadcasted_iota(jnp.int32, (1, width), 1)
+    lane = lax.broadcasted_iota(jnp.int32, (1, width), 1) // rows_each
     parts = [jnp.full((1, width), -1, jnp.int32) for _ in range(lanes // width)]
-    apart = 0
-    for wanted_ref in wanted_refs:
-        for i in range(wanted_ref.shape[0]):
-            part, at = divmod(apart * rows_each, width)
-            from_there = wanted_ref[i, pl.ds(me, 1), :]
-            here = (lane >= at) & (lane < at + rows_each)
-            parts[part] = jnp.where(here, from_there, parts[part])
-            apart += 1
+    entries = [(ref, i) for ref in wanted_refs for i in range(ref.shape[0])]
+    for apart, (wanted_ref, i) in zip(sources, entries):
+        from_there = wanted_ref[i, pl.ds(me, 1), :]
+        for p in range(len(parts)):
+            here = lane + p * (width // rows_each) == me ^ apart
+            parts[p] = jnp.where(here, from_there, parts[p])
     target = jnp.concatenate(parts, axis=1)
     row = lax.broadcasted_iota(jnp.int32, (rows, lanes), 0)
     owned = jnp.where(row == target, 1.0, 0.0).astype(BF16)
     owned_ref[...] = owned
     picked = dot_tn(owned, store_ref[...]).astype(BF16)
-    for at, send_ref in enumerate(send_refs):
-        send_ref[...] = picked[at * rows_each : (at + 1) * rows_each]
-
-
-def spread_kernel(tp, z_ref, placed_ref, *refs):
-    got_refs, send_refs, near_ref = refs[: -tp - 1], refs[-tp - 1 : -1], refs[-1]
+    send_ref[...] = picked.reshape(devices, rows_each, columns)
+
+
+def spread_kernel(tp, z_ref, placed_ref, got_ref, *refs):
+    send_refs, near_ref = refs[:-1], refs[-1]
     both = send_refs[0].shape[1]
-    got = jnp.concatenate([ref[...] for ref in got_refs], axis=0)
+    got = got_ref[...].reshape(placed_ref.shape[0], tp * both)
     near_ref[...] = dot_tn(placed_ref[...], got).astype(BF16)
-    for apart, send_ref in enumerate(send_refs):
+    for apart, send_ref in zip(distances(tp), send_refs):
         start = pl.multiple_of((z_ref[0] ^ apart) * both, both)
         send_ref[...] = near_ref[:, pl.ds(start, both)]
 
 
 def scatter_kernel(tp, z_ref, placed_ref, *refs):
-    grad_refs, send_refs, all_ref = refs[:tp], refs[tp:-1], refs[-1]
+    grad_refs, (send_ref, all_ref) = refs[:tp], refs[tp:]
     both = grad_refs[0].shape[1]
-    rows_each = send_refs[0].shape[0]
-    for apart, grad_ref in enumerate(grad_refs):
+    for apart, grad_ref in zip(distances(tp), grad_refs):
         start = pl.multiple_of((z_ref[0] ^ apart) * both, both)
         all_ref[:, pl.ds(start, both)] = grad_ref[...]
-    rows = dot_nn(placed_ref[...], all_ref[...]).astype(BF16)
-    for at, send_ref in enumerate(send_refs):
-        send_ref[...] = rows[at * rows_each : (at + 1) * rows_each]
+    send_ref[...] = dot_nn(placed_ref[...], all_ref[...]).astype(BF16).reshape(send_ref.shape)
 
 
 def self_kernel(
@@ -248,9 +279,9 @@
         ds_ref[at] = grad_scores[:, part]
         dk = dot_nn(grad_scores[:, part], queries[at]).astype(BF16)
         dv = dot_nn(weights[:, part], grads[at]).astype(BF16)
-        for apart, grad_ref in enumerate(grad_refs):
-            grad_ref[here, cols] = dk[apart * rows : (apart + 1) * rows]
-            grad_ref[here, vcols] = dv[apart * rows : (apart + 1) * rows]
+        for i, grad_ref in enumerate(grad_refs):
+            grad_ref[here, cols] = dk[i * rows : (i + 1) * rows]
+            grad_ref[here, vcols] = dv[i * rows : (i + 1) * rows]
 
 
 def join_kernel(tp, w_ref, ds_ref, out_ref, dq_ref, dkv_ref, back_ref, *refs):
@@ -282,12 +313,11 @@
     ).astype(BF16)
 
 
-def sum_kernel(tp, owned_ref, *refs):
-    got_refs, (kg_ref, vg_ref) = refs[:-2], refs[-2:]
+def sum_kernel(tp, owned_ref, got_ref, kg_ref, vg_ref):
     store_rows, tokens, features = kg_ref.shape
     width = features // tp
     owned = owned_ref[...]
-    got = jnp.concatenate([ref[...] for ref in got_refs], axis=0)
+    got = got_ref[...].reshape(owned.shape[1], 2 * features)
     for z in range(tp):
         total = dot_nn(owned, got[:, 2 * z * width : 2 * (z + 1) * width]).astype(BF16)
         cols = slice(z * width, (z + 1) * width)
@@ -295,14 +325,18 @@
         vg_ref[:, :, cols] = total[:, width:].reshape(store_rows, tokens, width)
 
 
-def call(kernel, name, ins, outs, flops, bytes_accessed, scratch=(), scalars=0, places=None):
+def call(kernel, name, ins, outs, flops, bytes_accessed, scratch=(), scalars=0, fetched=0):
+    direct = len(ins) - fetched
+    ins = ins[:direct] + tuple(
+        pltpu.with_memory_space_constraint(each, pltpu.HBM) for each in ins[direct:]
+    )
     return pl.pallas_call(
         kernel,
         out_shape=tuple(outs),
-        in_specs=places or [SMEM] * scalars + [VMEM] * (len(ins) - scalars),
+        in_specs=[SMEM] * scalars + [VMEM] * (direct - scalars) + [ANY] * fetched,
         out_specs=tuple(SMEM if len(out.shape) == 1 else VMEM for out in outs),
         scratch_shapes=list(scratch),
-        compiler_params=PARAMS,
+        compiler_params=pltpu.CompilerParams(vmem_limit_bytes=16 * 1024 * 1024),
         cost_estimate=pl.CostEstimate(
             flops=flops, bytes_accessed=bytes_accessed, transcendentals=0
         ),
@@ -312,6 +346,15 @@
 
 def swapped(block, axis, apart):
     return lax.ppermute(block, axis, [(i, i ^ apart) for i in range(lax.axis_size(axis))])
+
+
+def distances(tp):
+    return [0] + sorted(range(1, tp), key=lambda j: (j < 2, j))
+
+
+def exchanged(blocks):
+    apart = distances(len(blocks))
+    return [blocks[0]] + [swapped(b, "tp", j) for b, j in zip(blocks[1:], apart[1:])]
 
 
 def body(
@@ -344,35 +387,32 @@
     rank = lax.axis_index("seq").astype(int32).reshape(1)
     z_rank = lax.axis_index("tp").astype(int32).reshape(1)
 
-    want, owner_of, rank_of = call(
+    (want,) = call(
         functools.partial(plan_kernel, tokens, cap),
         "plan_requests",
         (nbr_owner, nbr_slot),
-        (
-            struct((devices, min(lanes, LANES)), int32),
-            struct((requests,), int32),
-            struct((requests,), int32),
-        ),
+        (struct((devices, min(lanes, LANES)), int32),),
         0,
-        10_000,
+        100_000,
         scratch=[
             pltpu.SMEM(nbr_owner.shape, int32),
             pltpu.SMEM(nbr_slot.shape, int32),
             pltpu.SemaphoreType.DMA((2,)),
         ],
-        places=[HBM, HBM],
-    )
-    pieces = [want[None]]
-    step = 1
-    while step < devices:
-        known = jnp.concatenate(pieces, axis=0) if step > 1 else pieces[0]
-        pieces.append(swapped(known, "seq", step))
+        fetched=2,
+    )
+    known, step = want[None], 1
+    while devices // step > 4:
+        known = jnp.concatenate([known, swapped(known, "seq", step)], axis=0)
         step *= 2
-
+    pieces = [known] + [swapped(known, "seq", far) for far in range(step, devices, step)]
+    sources = list(range(devices))
+
+    chunks = 4
     store, halo, placed = call(
-        functools.partial(stage_kernel, rows_each),
+        functools.partial(stage_kernel, rows_each, chunks),
         "stage_store",
-        (rank, owner_of, rank_of, enc_keys, encoded_values, sequence_keys, sequence_values),
+        (nbr_owner, enc_keys, encoded_values, sequence_keys, sequence_values),
         (
             struct((store_rows, 2 * enc_keys.shape[2]), BF16),
             struct((window, both), BF16),
@@ -380,19 +420,25 @@
         ),
         0,
         3_000_000,
-        scalars=3,
-    )
-    *sent, owned = call(
-        functools.partial(pack_kernel, len(pieces)),
+        scratch=[
+            pltpu.SMEM(nbr_owner.shape, int32),
+            pltpu.VMEM(enc_keys.shape, BF16),
+            pltpu.VMEM(encoded_values.shape, BF16),
+            pltpu.SemaphoreType.DMA((2 * chunks + 3,)),
+        ],
+        fetched=5,
+    )
+    sent, owned = call(
+        functools.partial(pack_kernel, sources),
         "pack_requests",
         (rank, store, *pieces),
-        [struct((rows_each, tp * both), BF16)] * devices + [struct((store_rows, lanes), BF16)],
+        (struct((devices, rows_each, tp * both), BF16), struct((store_rows, lanes), BF16)),
         200_000_000,
         2_000_000,
         scalars=1,
     )
     sent, halo = lax.optimization_barrier((sent, halo))
-    got = [sent[0]] + [swapped(sent[j], "seq", j) for j in range(1, devices)]
+    got = lax.all_to_all(sent, "seq", split_axis=0, concat_axis=0, tiled=True)
     halo = lax.ppermute(halo, "seq", [(i, i + 1) for i in range(devices - 1)])
 
     self_out, self_dq, self_dkv, back = call(
@@ -410,17 +456,20 @@
         scalars=1,
     )
 
+    got, self_out, self_dq, self_dkv, back = lax.optimization_barrier(
+        (got, self_out, self_dq, self_dkv, back)
+    )
     spread = call(
         functools.partial(spread_kernel, tp),
         "spread_rows",
-        (z_rank, placed, *got),
+        (z_rank, placed, got),
         [struct((used, both), BF16)] * tp,
         50_000_000,
         1_000_000,
         scratch=[pltpu.VMEM((used, tp * both), BF16)],
         scalars=1,
     )
-    near = [spread[0]] + [swapped(spread[j], "tp", j) for j in range(1, tp)]
+    near = exchanged(spread)
 
     blocks = spans * groups
     rows_span = per_span * NEIGHBOUR_LENGTH
@@ -433,20 +482,21 @@
         600_000_000,
         3_000_000,
     )
-    grads = [grads[0]] + [swapped(grads[j], "tp", j) for j in range(1, tp)]
+    grads = exchanged(grads)
     back = lax.ppermute(back, "seq", [(i + 1, i) for i in range(devices - 1)])
 
-    returned = call(
+    (returned,) = call(
         functools.partial(scatter_kernel, tp),
         "scatter_gradients",
         (z_rank, placed, *grads),
-        [struct((rows_each, tp * both), BF16)] * devices,
+        (struct((devices, rows_each, tp * both), BF16),),
         50_000_000,
         1_000_000,
         scratch=[pltpu.VMEM((used, tp * both), BF16)],
         scalars=1,
     )
-    returned = [returned[0]] + [swapped(returned[j], "seq", j) for j in range(1, devices)]
+    returned, weights = lax.optimization_barrier((returned, weights))
+    returned = lax.all_to_all(returned, "seq", split_axis=0, concat_axis=0, tiled=True)
 
     attended, query_gradient, key_gradient, value_gradient = call(
         functools.partial(join_kernel, tp),
@@ -464,7 +514,7 @@
     store_kgrad, store_vgrad = call(
         functools.partial(sum_kernel, tp),
         "sum_store_gradients",
-        (owned, *returned),
+        (owned, returned),
         (struct(enc_keys.shape, BF16), struct(encoded_values.shape, BF16)),
         200_000_000,
         2_000_000,

time: 60.8 us -> 75.8 us (1.25)
  the two profiles are of different devices: /device:TPU:0 before, /device:TPU:1 now
where the time goes in v1:
time: 75.8 us; the launch traced here: 75 us
  starting transfers between devices  30.9 us (41%)
  waiting for transfers between devices  21.6 us (28%)
  Pallas kernels  11.4 us (15%)
  local copies, waits for them, and re-layouts  10.3 us (14%)
  between operations  0.77 us (1%)
    pallas_call x9, Pallas kernels, call(): pl.pallas_call(kernel, out_shape=tuple(outs), in_specs=[SMEM] * scalars +...  11.4 us
    unnamed x38, local copies, waits for them, and re-layouts  10.3 us
    ppermute x10, starting transfers between devices, swapped(): lax.ppermute(block, axis, [(i, i ^ apart) for i in range(lax.axis_size(ax...  10.1 us
    all_to_all x1, starting transfers between devices, body(): lax.all_to_all(returned, 'seq', split_axis=0, concat_axis=0, tiled=True)  9.77 us
    ppermute x10, waiting for transfers between devices, swapped(): lax.ppermute(block, axis, [(i, i ^ apart) for i in range(lax.axis_size(ax...  9.73 us
    ppermute x1, waiting for transfers between devices, body(): back = lax.ppermute(back, 'seq', [(i + 1, i) for i in range(devices - 1)])  7.65 us
    all_to_all x1, starting transfers between devices, body(): got = lax.all_to_all(sent, 'seq', split_axis=0, concat_axis=0, tiled=True)  5.58 us
    ppermute x1, waiting for transfers between devices, body(): halo = lax.ppermute(halo, 'seq', [(i, i + 1) for i in range(devices - 1)])  4.21 us
  transfers between devices with their start and end apart: 14, of which 10 were waited for; matrix products, arithmetic and copies ran while one was open for 0% of the time, Pallas kernels for 8%

profile of v1, /device:TPU:1, one launch (start us, length us, event | category | flops | bytes accessed | tf_op | source)
XLA Modules:
  0.0 75.0 jit_solution(5242741894818308797)
XLA Ops:
  0.6 0.9 %plan_requests.1 = s32[8,128]{1,0:T(8,128)S(1)} custom-call(s32[4,4]{1,0:T(4,128)} %owner_any.3, s32[4,4]{1,0:T(4,128)} %slot_any.1), custom_call_target="tpu_custom_call" | custom-call | bytes 100000 | tf_op jit(solution)/shard_map/plan_requests/pallas_call | solution.py:333
  1.7 1.1 %collective-permute-done = s32[1,8,128]{2,1,0:T(8,128)S(1)} collective-permute-done((s32[1,8,128]{2,1,0:T(8,128)S(1)}, s32[1,8,128]{2,1,0:T(8,128)S(1)}, u32[]{:S(2)}, u32[]{:S(2)}) %collective-permute-start) | collective-permute-done | bytes 4128 | tf_op jit(solution)/shard_map/ppermute | solution.py:348
  2.8 3.3 %collective-permute-start.3 = (s32[2,8,128]{2,1,0:T(8,128)S(1)}, s32[2,8,128]{2,1,0:T(8,128)S(1)}, u32[]{:S(2)}, u32[]{:S(2)}) collective-permute-start(s32[2,8,128]{2,1,0:T(8,128)S(1)} %pad_add_fusion.refs_0_), channel_id=1, source_target_pairs={{0,24},{4,28},{8,16},{12,20},{16,8},{20,12},{24,0},{28,4},{1,25},{... | collective-permute-start | bytes 24584 | tf_op jit(solution)/shard_map/ppermute | solution.py:348
  6.4 1.4 %stage_store.1 = (bf16[256,2048]{1,0:T(8,128)(2,1)S(1)}, bf16[128,512]{1,0:T(8,128)(2,1)S(1)}, bf16[128,64]{1,0:T(8,128)(2,1)S(1)}) custom-call(s32[4,4]{1,0:T(4,128)} %owner_any.3, bf16[64,4,1024]{2,1,0:T(4,128)(2,1)} %k_any.1, bf16[64,4,1024]{2,1,0:T(4,128)(2,1)} %v_any.1, bf16[256,256]{1,0:T(8,128)(2,1)} %k_ref.1, bf16[256,256]{1,0:T(8,128)(2,1)} %v_ref.1), custom_call_target="tpu_custom_call" | custom-call | bytes 3000000 | tf_op jit(solution)/shard_map/stage_store/pallas_call | solution.py:333
  7.8 0.8 %collective-permute-done.2.refs_2_ = s32[2,8,128]{2,1,0:T(8,128)S(1)} collective-permute-done((s32[2,8,128]{2,1,0:T(8,128)S(1)}, s32[2,8,128]{2,1,0:T(8,128)S(1)}, u32[]{:S(2)}, u32[]{:S(2)}) %collective-permute-start.2) | collective-permute-done | bytes 8224 | tf_op jit(solution)/shard_map/ppermute | solution.py:348
  8.9 1.1 %pack_requests.1 = (bf16[8,16,2048]{2,1,0:T(8,128)(2,1)}, bf16[256,128]{1,0:T(8,128)(2,1)S(1)}) custom-call(s32[1]{0:T(128)} %bitcast.1.me_ref.rank_ref, bf16[256,2048]{1,0:T(8,128)(2,1)S(1)} %get-tuple-element.41.store_ref, s32[2,8,128]{2,1,0:T(8,128)S(1)} %pad_add_fusion.refs_0_, s32[2,8,128]{2,1,0:T(8,128)S(1)} %collective-permute-done.1.refs_1_, ...), custom_call_target="tpu_custom_call" | custom-call | flops 200000000 | bytes 2000000 | tf_op jit(solution)/shard_map/pack_requests/pallas_call | solution.py:333
  10.6 5.6 %all-to-all-start = ((bf16[8,16,2048]{2,1,0:T(8,128)(2,1)}), bf16[8,16,2048]{2,1,0:T(8,128)(2,1)S(1)}, u32[]{:S(2)}, u32[]{:S(2)}) async-start(bf16[8,16,2048]{2,1,0:T(8,128)(2,1)} %get-tuple-element.44), calls=%async_computation | async-start | bytes 1048576 | tf_op jit(solution)/shard_map/all_to_all | solution.py:441
  16.2 3.5 %collective-permute-start.4 = (bf16[128,512]{1,0:T(8,128)(2,1)S(1)}, bf16[128,512]{1,0:T(8,128)(2,1)S(1)}, u32[]{:S(2)}, u32[]{:S(2)}) collective-permute-start(bf16[128,512]{1,0:T(8,128)(2,1)S(1)} %get-tuple-element.45), channel_id=1, source_target_pairs={{0,4},{4,8},{8,12},{12,16},{16,20},{20,24},{24,28},{1,5},{5,9},{9,... | collective-permute-start | bytes 393224 | tf_op jit(solution)/shard_map/ppermute | solution.py:442
  19.7 4.2 %collective-permute-done.4.halo_ref = bf16[128,512]{1,0:T(8,128)(2,1)S(1)} collective-permute-done((bf16[128,512]{1,0:T(8,128)(2,1)S(1)}, bf16[128,512]{1,0:T(8,128)(2,1)S(1)}, u32[]{:S(2)}, u32[]{:S(2)}) %collective-permute-start.4) | collective-permute-done | bytes 131104 | tf_op jit(solution)/shard_map/ppermute | solution.py:442
  24.6 1.0 %copy-done.10 = bf16[256,1024]{1,0:T(8,128)(2,1)S(1)} copy-done((bf16[256,1024]{1,0:T(8,128)(2,1)S(1)}, bf16[256,1024]{1,0:T(8,128)(2,1)}, u32[]{:S(2)}) %copy-start.10) | copy-done | bytes 524312
  25.7 1.0 %copy-done.12 = bf16[256,1024]{1,0:T(8,128)(2,1)S(1)} copy-done((bf16[256,1024]{1,0:T(8,128)(2,1)S(1)}, bf16[256,1024]{1,0:T(8,128)(2,1)}, u32[]{:S(2)}) %copy-start.12) | copy-done | bytes 524312
  26.7 0.9 %copy-done.16 = bf16[128,512]{1,0:T(8,128)(2,1)S(1)} copy-done((bf16[128,512]{1,0:T(8,128)(2,1)S(1)}, bf16[128,512]{1,0:T(8,128)(2,1)}, u32[]{:S(2)}) %copy-start.16) | copy-done | bytes 131096
  27.6 2.9 %self_attention.1 = (f32[256,1024]{1,0:T(8,128)S(1)}, f32[256,1024]{1,0:T(8,128)S(1)}, f32[256,512]{1,0:T(8,128)S(1)}, bf16[128,512]{1,0:T(8,128)(2,1)S(1)}) custom-call(s32[1]{0:T(128)} %bitcast.1.me_ref.rank_ref, bf16[256,1024]{1,0:T(8,128)(2,1)S(1)} %copy-done.10, bf16[256,256]{1,0:T(8,128)(2,1)S(1)} %copy-done.2, bf16[256,256]{1,0:T(8,128)(2,1)S(1)} %copy-done.3, ...), custom_call_target="tpu_custom_call" | custom-call | flops 1600000000 | bytes 6000000 | tf_op jit(solution)/shard_map/self_attention/pallas_call | solution.py:333
  31.4 2.4 %collective-permute-start.5 = (bf16[64,512]{1,0:T(8,128)(2,1)S(1)}, bf16[64,512]{1,0:T(8,128)(2,1)S(1)}, u32[]{:S(2)}, u32[]{:S(2)}) collective-permute-start(bf16[64,512]{1,0:T(8,128)(2,1)S(1)} %get-tuple-element.52), channel_id=1, source_target_pairs={{0,2},{1,3},{2,0},{3,1},{4,6},{5,7},{6,4},{7,5},{8,10},{9,11},{10,... | collective-permute-start | bytes 196616 | tf_op jit(solution)/shard_map/ppermute | solution.py:348
  33.8 1.1 %collective-permute-start.6 = (bf16[64,512]{1,0:T(8,128)(2,1)S(1)}, bf16[64,512]{1,0:T(8,128)(2,1)S(1)}, u32[]{:S(2)}, u32[]{:S(2)}) collective-permute-start(bf16[64,512]{1,0:T(8,128)(2,1)S(1)} %get-tuple-element.53), channel_id=1, source_target_pairs={{0,3},{1,2},{2,1},{3,0},{4,7},{5,6},{6,5},{7,4},{8,11},{9,10},{10,... | collective-permute-start | bytes 196616 | tf_op jit(solution)/shard_map/ppermute | solution.py:348
  35.9 2.8 %collective-permute-done.6.refs_2_ = bf16[64,512]{1,0:T(8,128)(2,1)S(1)} collective-permute-done((bf16[64,512]{1,0:T(8,128)(2,1)S(1)}, bf16[64,512]{1,0:T(8,128)(2,1)S(1)}, u32[]{:S(2)}, u32[]{:S(2)}) %collective-permute-start.6) | collective-permute-done | bytes 65568 | tf_op jit(solution)/shard_map/ppermute | solution.py:348
  38.7 1.1 %copy-done.13 = bf16[256,1024]{1,0:T(8,128)(2,1)S(1)} copy-done((bf16[256,1024]{1,0:T(8,128)(2,1)S(1)}, bf16[256,1024]{1,0:T(8,128)(2,1)}, u32[]{:S(2)}) %copy-start.13) | copy-done | bytes 524312
  40.6 1.3 %collective-permute-start.8 = (bf16[64,512]{1,0:T(8,128)(2,1)S(1)}, bf16[64,512]{1,0:T(8,128)(2,1)S(1)}, u32[]{:S(2)}, u32[]{:S(2)}) collective-permute-start(bf16[64,512]{1,0:T(8,128)(2,1)S(1)} %get-tuple-element.56), channel_id=1, source_target_pairs={{0,2},{1,3},{2,0},{3,1},{4,6},{5,7},{6,4},{7,5},{8,10},{9,11},{10,... | collective-permute-start | bytes 196616 | tf_op jit(solution)/shard_map/ppermute | solution.py:348
  41.9 0.9 %collective-permute-start.9 = (bf16[64,512]{1,0:T(8,128)(2,1)S(1)}, bf16[64,512]{1,0:T(8,128)(2,1)S(1)}, u32[]{:S(2)}, u32[]{:S(2)}) collective-permute-start(bf16[64,512]{1,0:T(8,128)(2,1)S(1)} %get-tuple-element.57), channel_id=1, source_target_pairs={{0,3},{1,2},{2,1},{3,0},{4,7},{5,6},{6,5},{7,4},{8,11},{9,10},{10,... | collective-permute-start | bytes 196616 | tf_op jit(solution)/shard_map/ppermute | solution.py:348
  43.3 2.7 %collective-permute-done.8.refs_1_ = bf16[64,512]{1,0:T(8,128)(2,1)S(1)} collective-permute-done((bf16[64,512]{1,0:T(8,128)(2,1)S(1)}, bf16[64,512]{1,0:T(8,128)(2,1)S(1)}, u32[]{:S(2)}, u32[]{:S(2)}) %collective-permute-start.8) | collective-permute-done | bytes 65568 | tf_op jit(solution)/shard_map/ppermute | solution.py:348
  46.0 1.0 %collective-permute-done.9.refs_2_ = bf16[64,512]{1,0:T(8,128)(2,1)S(1)} collective-permute-done((bf16[64,512]{1,0:T(8,128)(2,1)S(1)}, bf16[64,512]{1,0:T(8,128)(2,1)S(1)}, u32[]{:S(2)}, u32[]{:S(2)}) %collective-permute-start.9) | collective-permute-done | bytes 65568 | tf_op jit(solution)/shard_map/ppermute | solution.py:348
  47.3 1.1 %scatter_gradients.1 = bf16[8,16,2048]{2,1,0:T(8,128)(2,1)} custom-call(s32[1]{0:T(128)} %bitcast.z_ref, bf16[128,64]{1,0:T(8,128)(2,1)S(1)} %get-tuple-element.40.placed_ref, bf16[64,512]{1,0:T(8,128)(2,1)S(1)} %get-tuple-element.55.refs_0_, bf16[64,512]{1,0:T(8,128)(2,1)S(1)} %collective-permute-done.8.refs_1_, ...), custom_call_target="tpu_custom_call" | custom-call | flops 50000000 | bytes 1000000 | tf_op jit(solution)/shard_map/scatter_gradients/pallas_call | solution.py:333
  48.4 9.8 %all-to-all-start.1 = ((bf16[8,16,2048]{2,1,0:T(8,128)(2,1)}), bf16[8,16,2048]{2,1,0:T(8,128)(2,1)S(1)}, u32[]{:S(2)}, u32[]{:S(2)}) async-start(bf16[8,16,2048]{2,1,0:T(8,128)(2,1)} %scatter_gradients.1), calls=%async_computation.1 | async-start | bytes 1048576 | tf_op jit(solution)/shard_map/all_to_all | solution.py:499
  58.2 1.9 %collective-permute-start.11 = (bf16[128,512]{1,0:T(8,128)(2,1)}, bf16[128,512]{1,0:T(8,128)(2,1)S(1)}, u32[]{:S(2)}, u32[]{:S(2)}) collective-permute-start(bf16[128,512]{1,0:T(8,128)(2,1)} %copy-done.14), channel_id=1, source_target_pairs={{4,0},{8,4},{12,8},{16,12},{20,16},{24,20},{28,24},{5,1},{9,5},{13... | collective-permute-start | bytes 393224 | tf_op jit(solution)/shard_map/ppermute | solution.py:486
  60.1 7.6 %collective-permute-done.11.back_ref = bf16[128,512]{1,0:T(8,128)(2,1)S(1)} collective-permute-done((bf16[128,512]{1,0:T(8,128)(2,1)}, bf16[128,512]{1,0:T(8,128)(2,1)S(1)}, u32[]{:S(2)}, u32[]{:S(2)}) %collective-permute-start.11) | collective-permute-done | bytes 131104 | tf_op jit(solution)/shard_map/ppermute | solution.py:486
  67.8 0.9 %copy-done.1 = bf16[8,64,256]{2,1,0:T(8,128)(2,1)S(1)} copy-done((bf16[8,64,256]{2,1,0:T(8,128)(2,1)S(1)}, bf16[8,64,256]{2,1,0:T(8,128)(2,1)}, u32[]{:S(2)}) %copy-start.1) | copy-done | bytes 262168
  68.7 0.8 %copy-done.5 = bf16[64,512]{1,0:T(8,128)(2,1)S(1)} copy-done((bf16[64,512]{1,0:T(8,128)(2,1)S(1)}, bf16[64,512]{1,0:T(8,128)(2,1)}, u32[]{:S(2)}) %copy-start.5) | copy-done | bytes 65560
  69.5 0.8 %copy-done.7 = bf16[64,512]{1,0:T(8,128)(2,1)S(1)} copy-done((bf16[64,512]{1,0:T(8,128)(2,1)S(1)}, bf16[64,512]{1,0:T(8,128)(2,1)}, u32[]{:S(2)}) %copy-start.7) | copy-done | bytes 65560
  70.4 0.8 %copy-done.9 = bf16[64,512]{1,0:T(8,128)(2,1)S(1)} copy-done((bf16[64,512]{1,0:T(8,128)(2,1)S(1)}, bf16[64,512]{1,0:T(8,128)(2,1)}, u32[]{:S(2)}) %copy-start.9) | copy-done | bytes 65560
  71.2 1.6 %join_outputs.1 = (bf16[256,1024]{1,0:T(8,128)(2,1)}, bf16[256,1024]{1,0:T(8,128)(2,1)}, bf16[256,256]{1,0:T(8,128)(2,1)}, bf16[256,256]{1,0:T(8,128)(2,1)}) custom-call(bf16[8,64,256]{2,1,0:T(8,128)(2,1)S(1)} %get-tuple-element.60.w_ref, bf16[8,64,256]{2,1,0:T(8,128)(2,1)S(1)} %copy-done.1, f32[256,1024]{1,0:T(8,128)S(1)} %get-tuple-element.62.out_ref, ...), custom_call_target="tpu_custom_call" | custom-call | flops 300000000 | bytes 5000000 | tf_op jit(solution)/shard_map/join_outputs/pallas_call | solution.py:333
  72.8 0.8 %copy-done.18 = bf16[256,128]{1,0:T(8,128)(2,1)S(1)} copy-done((bf16[256,128]{1,0:T(8,128)(2,1)S(1)}, bf16[256,128]{1,0:T(8,128)(2,1)}, u32[]{:S(2)}) %copy-start.18) | copy-done | bytes 65560
  73.6 1.4 %sum_store_gradients.1 = (bf16[64,4,1024]{2,1,0:T(4,128)(2,1)}, bf16[64,4,1024]{2,1,0:T(4,128)(2,1)}) custom-call(bf16[256,128]{1,0:T(8,128)(2,1)S(1)} %copy-done.18, bf16[8,16,2048]{2,1,0:T(8,128)(2,1)S(1)} %all-to-all-done.1.got_ref), custom_call_target="tpu_custom_call" | custom-call | flops 200000000 | bytes 2000000 | tf_op jit(solution)/shard_map/sum_store_gradients/pallas_call | solution.py:333
  (44 shorter events, 5.5 us)
Async XLA Ops:
  1.6 1.2 %collective-permute-start = (s32[1,8,128]{2,1,0:T(8,128)S(1)}, s32[1,8,128]{2,1,0:T(8,128)S(1)}, u32[]{:S(2)}, u32[]{:S(2)}) collective-permute-start(s32[1,8,128]{2,1,0:T(8,128)S(1)} %bitcast.3), channel_id=1, source_target_pairs={{0,4},{4,0},{8,12},{12,8},{16,20},{20,16},{24,28},{28,24},{1,5},{5... | collective-permute-start | bytes 12296 | tf_op jit(solution)/shard_map/ppermute | solution.py:348
  2.8 5.0 %collective-permute-start.3 = (s32[2,8,128]{2,1,0:T(8,128)S(1)}, s32[2,8,128]{2,1,0:T(8,128)S(1)}, u32[]{:S(2)}, u32[]{:S(2)}) collective-permute-start(s32[2,8,128]{2,1,0:T(8,128)S(1)} %pad_add_fusion.refs_0_), channel_id=1, source_target_pairs={{0,24},{4,28},{8,16},{12,20},{16,8},{20,12},{24,0},{28,4},{1,25},{... | collective-permute-start | bytes 24584 | tf_op jit(solution)/shard_map/ppermute | solution.py:348
  6.1 2.5 %collective-permute-start.2 = (s32[2,8,128]{2,1,0:T(8,128)S(1)}, s32[2,8,128]{2,1,0:T(8,128)S(1)}, u32[]{:S(2)}, u32[]{:S(2)}) collective-permute-start(s32[2,8,128]{2,1,0:T(8,128)S(1)} %pad_add_fusion.refs_0_), channel_id=1, source_target_pairs={{0,16},{4,20},{8,24},{12,28},{16,0},{20,4},{24,8},{28,12},{1,17},{... | collective-permute-start | bytes 24584 | tf_op jit(solution)/shard_map/ppermute | solution.py:348
  6.4 2.5 %collective-permute-start.1 = (s32[2,8,128]{2,1,0:T(8,128)S(1)}, s32[2,8,128]{2,1,0:T(8,128)S(1)}, u32[]{:S(2)}, u32[]{:S(2)}) collective-permute-start(s32[2,8,128]{2,1,0:T(8,128)S(1)} %pad_add_fusion.refs_0_), channel_id=1, source_target_pairs={{0,8},{4,12},{8,0},{12,4},{16,24},{20,28},{24,16},{28,20},{1,9},{5... | collective-permute-start | bytes 24584 | tf_op jit(solution)/shard_map/ppermute | solution.py:348
  10.6 14.0 %copy-start.2 = (bf16[256,256]{1,0:T(8,128)(2,1)S(1)}, bf16[256,256]{1,0:T(8,128)(2,1)}, u32[]{:S(2)}) copy-start(bf16[256,256]{1,0:T(8,128)(2,1)} %k_ref.1) | copy-start | bytes 393220
  10.6 14.0 %copy-start.3 = (bf16[256,256]{1,0:T(8,128)(2,1)S(1)}, bf16[256,256]{1,0:T(8,128)(2,1)}, u32[]{:S(2)}) copy-start(bf16[256,256]{1,0:T(8,128)(2,1)} %v_ref.1) | copy-start | bytes 393220
  10.6 20.5 %all-to-all-start = ((bf16[8,16,2048]{2,1,0:T(8,128)(2,1)}), bf16[8,16,2048]{2,1,0:T(8,128)(2,1)S(1)}, u32[]{:S(2)}, u32[]{:S(2)}) async-start(bf16[8,16,2048]{2,1,0:T(8,128)(2,1)} %get-tuple-element.44), calls=%async_computation | async-start | bytes 1048576 | tf_op jit(solution)/shard_map/all_to_all | solution.py:441
  16.2 7.8 %collective-permute-start.4 = (bf16[128,512]{1,0:T(8,128)(2,1)S(1)}, bf16[128,512]{1,0:T(8,128)(2,1)S(1)}, u32[]{:S(2)}, u32[]{:S(2)}) collective-permute-start(bf16[128,512]{1,0:T(8,128)(2,1)S(1)} %get-tuple-element.45), channel_id=1, source_target_pairs={{0,4},{4,8},{8,12},{12,16},{16,20},{20,24},{24,28},{1,5},{5,9},{9,... | collective-permute-start | bytes 393224 | tf_op jit(solution)/shard_map/ppermute | solution.py:442
  24.0 0.7 copy-start.15
  24.6 1.0 %copy-start.10 = (bf16[256,1024]{1,0:T(8,128)(2,1)S(1)}, bf16[256,1024]{1,0:T(8,128)(2,1)}, u32[]{:S(2)}) copy-start(bf16[256,1024]{1,0:T(8,128)(2,1)} %q_ref.3) | copy-start | bytes 1572868
  25.7 1.0 %copy-start.12 = (bf16[256,1024]{1,0:T(8,128)(2,1)S(1)}, bf16[256,1024]{1,0:T(8,128)(2,1)}, u32[]{:S(2)}) copy-start(bf16[256,1024]{1,0:T(8,128)(2,1)} %do_ref.3) | copy-start | bytes 1572868
  26.7 0.9 %copy-start.16 = (bf16[128,512]{1,0:T(8,128)(2,1)S(1)}, bf16[128,512]{1,0:T(8,128)(2,1)}, u32[]{:S(2)}) copy-start(bf16[128,512]{1,0:T(8,128)(2,1)} %copy-done.15) | copy-start | bytes 393220
  30.5 0.7 copy-start.14
  31.2 7.6 %copy-start.11 = (bf16[256,1024]{1,0:T(8,128)(2,1)S(1)}, bf16[256,1024]{1,0:T(8,128)(2,1)}, u32[]{:S(2)}) copy-start(bf16[256,1024]{1,0:T(8,128)(2,1)} %q_ref.3) | copy-start | bytes 1572868
  31.4 4.5 %collective-permute-start.5 = (bf16[64,512]{1,0:T(8,128)(2,1)S(1)}, bf16[64,512]{1,0:T(8,128)(2,1)S(1)}, u32[]{:S(2)}, u32[]{:S(2)}) collective-permute-start(bf16[64,512]{1,0:T(8,128)(2,1)S(1)} %get-tuple-element.52), channel_id=1, source_target_pairs={{0,2},{1,3},{2,0},{3,1},{4,6},{5,7},{6,4},{7,5},{8,10},{9,11},{10,... | collective-permute-start | bytes 196616 | tf_op jit(solution)/shard_map/ppermute | solution.py:348
  33.8 4.9 %collective-permute-start.6 = (bf16[64,512]{1,0:T(8,128)(2,1)S(1)}, bf16[64,512]{1,0:T(8,128)(2,1)S(1)}, u32[]{:S(2)}, u32[]{:S(2)}) collective-permute-start(bf16[64,512]{1,0:T(8,128)(2,1)S(1)} %get-tuple-element.53), channel_id=1, source_target_pairs={{0,3},{1,2},{2,1},{3,0},{4,7},{5,6},{6,5},{7,4},{8,11},{9,10},{10,... | collective-permute-start | bytes 196616 | tf_op jit(solution)/shard_map/ppermute | solution.py:348
  34.9 3.8 %collective-permute-start.7 = (bf16[64,512]{1,0:T(8,128)(2,1)S(1)}, bf16[64,512]{1,0:T(8,128)(2,1)S(1)}, u32[]{:S(2)}, u32[]{:S(2)}) collective-permute-start(bf16[64,512]{1,0:T(8,128)(2,1)S(1)} %get-tuple-element.54), channel_id=1, source_target_pairs={{0,1},{1,0},{2,3},{3,2},{4,5},{5,4},{6,7},{7,6},{8,9},{9,8},{10,11... | collective-permute-start | bytes 196616 | tf_op jit(solution)/shard_map/ppermute | solution.py:348
  35.9 4.7 %copy-start.4 = (bf16[64,512]{1,0:T(8,128)(2,1)}, bf16[64,512]{1,0:T(8,128)(2,1)S(1)}, u32[]{:S(2)}) copy-start(bf16[64,512]{1,0:T(8,128)(2,1)S(1)} %collective-permute-done.5.refs_1_) | copy-start | bytes 196612
  38.7 1.9 %copy-start.6 = (bf16[64,512]{1,0:T(8,128)(2,1)}, bf16[64,512]{1,0:T(8,128)(2,1)S(1)}, u32[]{:S(2)}) copy-start(bf16[64,512]{1,0:T(8,128)(2,1)S(1)} %collective-permute-done.6.refs_2_) | copy-start | bytes 196612
  38.7 1.9 %copy-start.8 = (bf16[64,512]{1,0:T(8,128)(2,1)}, bf16[64,512]{1,0:T(8,128)(2,1)S(1)}, u32[]{:S(2)}) copy-start(bf16[64,512]{1,0:T(8,128)(2,1)S(1)} %collective-permute-done.7.refs_3_) | copy-start | bytes 196612
  38.7 1.1 %copy-start.13 = (bf16[256,1024]{1,0:T(8,128)(2,1)S(1)}, bf16[256,1024]{1,0:T(8,128)(2,1)}, u32[]{:S(2)}) copy-start(bf16[256,1024]{1,0:T(8,128)(2,1)} %do_ref.3) | copy-start | bytes 1572868
  40.6 7.8 %copy-start = (bf16[8,64,256]{2,1,0:T(8,128)(2,1)}, bf16[8,64,256]{2,1,0:T(8,128)(2,1)S(1)}, u32[]{:S(2)}) copy-start(bf16[8,64,256]{2,1,0:T(8,128)(2,1)S(1)} %get-tuple-element.61.ds_ref) | copy-start | bytes 786436
  40.6 5.4 %collective-permute-start.8 = (bf16[64,512]{1,0:T(8,128)(2,1)S(1)}, bf16[64,512]{1,0:T(8,128)(2,1)S(1)}, u32[]{:S(2)}, u32[]{:S(2)}) collective-permute-start(bf16[64,512]{1,0:T(8,128)(2,1)S(1)} %get-tuple-element.56), channel_id=1, source_target_pairs={{0,2},{1,3},{2,0},{3,1},{4,6},{5,7},{6,4},{7,5},{8,10},{9,11},{10,... | collective-permute-start | bytes 196616 | tf_op jit(solution)/shard_map/ppermute | solution.py:348
  41.9 5.1 %collective-permute-start.9 = (bf16[64,512]{1,0:T(8,128)(2,1)S(1)}, bf16[64,512]{1,0:T(8,128)(2,1)S(1)}, u32[]{:S(2)}, u32[]{:S(2)}) collective-permute-start(bf16[64,512]{1,0:T(8,128)(2,1)S(1)} %get-tuple-element.57), channel_id=1, source_target_pairs={{0,3},{1,2},{2,1},{3,0},{4,7},{5,6},{6,5},{7,4},{8,11},{9,10},{10,... | collective-permute-start | bytes 196616 | tf_op jit(solution)/shard_map/ppermute | solution.py:348
  42.8 4.5 %collective-permute-start.10 = (bf16[64,512]{1,0:T(8,128)(2,1)S(1)}, bf16[64,512]{1,0:T(8,128)(2,1)S(1)}, u32[]{:S(2)}, u32[]{:S(2)}) collective-permute-start(bf16[64,512]{1,0:T(8,128)(2,1)S(1)} %get-tuple-element.58), channel_id=1, source_target_pairs={{0,1},{1,0},{2,3},{3,2},{4,5},{5,4},{6,7},{7,6},{8,9},{9,8},{10,11... | collective-permute-start | bytes 196616 | tf_op jit(solution)/shard_map/ppermute | solution.py:348
  48.4 24.4 %all-to-all-start.1 = ((bf16[8,16,2048]{2,1,0:T(8,128)(2,1)}), bf16[8,16,2048]{2,1,0:T(8,128)(2,1)S(1)}, u32[]{:S(2)}, u32[]{:S(2)}) async-start(bf16[8,16,2048]{2,1,0:T(8,128)(2,1)} %scatter_gradients.1), calls=%async_computation.1 | async-start | bytes 1048576 | tf_op jit(solution)/shard_map/all_to_all | solution.py:499
  58.2 9.6 %collective-permute-start.11 = (bf16[128,512]{1,0:T(8,128)(2,1)}, bf16[128,512]{1,0:T(8,128)(2,1)S(1)}, u32[]{:S(2)}, u32[]{:S(2)}) collective-permute-start(bf16[128,512]{1,0:T(8,128)(2,1)} %copy-done.14), channel_id=1, source_target_pairs={{4,0},{8,4},{12,8},{16,12},{20,16},{24,20},{28,24},{5,1},{9,5},{13... | collective-permute-start | bytes 393224 | tf_op jit(solution)/shard_map/ppermute | solution.py:486
  67.8 1.0 %copy-start.1 = (bf16[8,64,256]{2,1,0:T(8,128)(2,1)S(1)}, bf16[8,64,256]{2,1,0:T(8,128)(2,1)}, u32[]{:S(2)}) copy-start(bf16[8,64,256]{2,1,0:T(8,128)(2,1)} %copy-done) | copy-start | bytes 786436
  68.7 0.8 %copy-start.5 = (bf16[64,512]{1,0:T(8,128)(2,1)S(1)}, bf16[64,512]{1,0:T(8,128)(2,1)}, u32[]{:S(2)}) copy-start(bf16[64,512]{1,0:T(8,128)(2,1)} %copy-done.4) | copy-start | bytes 196612
  69.5 0.8 %copy-start.7 = (bf16[64,512]{1,0:T(8,128)(2,1)S(1)}, bf16[64,512]{1,0:T(8,128)(2,1)}, u32[]{:S(2)}) copy-start(bf16[64,512]{1,0:T(8,128)(2,1)} %copy-done.6) | copy-start | bytes 196612
  70.4 0.8 %copy-start.9 = (bf16[64,512]{1,0:T(8,128)(2,1)S(1)}, bf16[64,512]{1,0:T(8,128)(2,1)}, u32[]{:S(2)}) copy-start(bf16[64,512]{1,0:T(8,128)(2,1)} %copy-done.8) | copy-start | bytes 196612
  72.8 0.8 %copy-start.18 = (bf16[256,128]{1,0:T(8,128)(2,1)S(1)}, bf16[256,128]{1,0:T(8,128)(2,1)}, u32[]{:S(2)}) copy-start(bf16[256,128]{1,0:T(8,128)(2,1)} %copy-done.17) | copy-start | bytes 196612
  (1 other events, 0.6 us)

commit v2 on v1

--- a/solution.py
+++ b/solution.py
@@ -99,6 +99,7 @@
 def stage_kernel(
     rows_each,
     chunks,
+    me_ref,
     owner_any,
     k_any,
     v_any,
@@ -132,11 +133,12 @@
     for copy in copies:
         copy.start()
     fetch_owner.wait()
+    me = me_ref[0]
     lanes, used = placed_ref.shape
     lane = lax.broadcasted_iota(jnp.int32, (1, used), 1)
     place = lane % tokens
     for r, (_, _, owner, rank) in enumerate(ranked(owner_ref)):
-        place = place + jnp.where(lane // tokens == r, owner * rows_each + rank * tokens, 0)
+        place = place + jnp.where(lane // tokens == r, (owner ^ me) * rows_each + rank * tokens, 0)
     row = lax.broadcasted_iota(jnp.int32, (lanes, used), 0)
     placed_ref[...] = jnp.where(row == place, 1.0, 0.0).astype(BF16)
     for i in range(chunks):
@@ -156,32 +158,33 @@
         copy.wait()
 
 
-def pack_kernel(sources, me_ref, store_ref, *refs):
-    *wanted_refs, send_ref, owned_ref = refs
-    devices, rows_each, columns = send_ref.shape
+def pack_kernel(pieces, me_ref, store_ref, *refs):
+    wanted_refs, send_refs, owned_ref = refs[:pieces], refs[pieces:-1], refs[-1]
+    rows_each = send_refs[0].shape[0]
     rows, lanes = owned_ref.shape
     me = me_ref[0]
     width = wanted_refs[0].shape[2]
-    lane = lax.broadcasted_iota(jnp.int32, (1, width), 1) // rows_each
+    lane = lax.broadcasted_iota(jnp.int32, (1, width), 1)
     parts = [jnp.full((1, width), -1, jnp.int32) for _ in range(lanes // width)]
     entries = [(ref, i) for ref in wanted_refs for i in range(ref.shape[0])]
-    for apart, (wanted_ref, i) in zip(sources, entries):
+    for apart, (wanted_ref, i) in enumerate(entries):
+        part, at = divmod(apart * rows_each, width)
         from_there = wanted_ref[i, pl.ds(me, 1), :]
-        for p in range(len(parts)):
-            here = lane + p * (width // rows_each) == me ^ apart
-            parts[p] = jnp.where(here, from_there, parts[p])
+        here = (lane >= at) & (lane < at + rows_each)
+        parts[part] = jnp.where(here, from_there, parts[part])
     target = jnp.concatenate(parts, axis=1)
     row = lax.broadcasted_iota(jnp.int32, (rows, lanes), 0)
     owned = jnp.where(row == target, 1.0, 0.0).astype(BF16)
     owned_ref[...] = owned
     picked = dot_tn(owned, store_ref[...]).astype(BF16)
-    send_ref[...] = picked.reshape(devices, rows_each, columns)
-
-
-def spread_kernel(tp, z_ref, placed_ref, got_ref, *refs):
-    send_refs, near_ref = refs[:-1], refs[-1]
+    for at, send_ref in enumerate(send_refs):
+        send_ref[...] = picked[at * rows_each : (at + 1) * rows_each]
+
+
+def spread_kernel(tp, z_ref, placed_ref, *refs):
+    got_refs, send_refs, near_ref = refs[: -tp - 1], refs[-tp - 1 : -1], refs[-1]
     both = send_refs[0].shape[1]
-    got = got_ref[...].reshape(placed_ref.shape[0], tp * both)
+    got = jnp.concatenate([ref[...] for ref in got_refs], axis=0)
     near_ref[...] = dot_tn(placed_ref[...], got).astype(BF16)
     for apart, send_ref in zip(distances(tp), send_refs):
         start = pl.multiple_of((z_ref[0] ^ apart) * both, both)
@@ -189,12 +192,15 @@
 
 
 def scatter_kernel(tp, z_ref, placed_ref, *refs):
-    grad_refs, (send_ref, all_ref) = refs[:tp], refs[tp:]
+    grad_refs, send_refs, all_ref = refs[:tp], refs[tp:-1], refs[-1]
     both = grad_refs[0].shape[1]
+    rows_each = send_refs[0].shape[0]
     for apart, grad_ref in zip(distances(tp), grad_refs):
         start = pl.multiple_of((z_ref[0] ^ apart) * both, both)
         all_ref[:, pl.ds(start, both)] = grad_ref[...]
-    send_ref[...] = dot_nn(placed_ref[...], all_ref[...]).astype(BF16).reshape(send_ref.shape)
+    rows = dot_nn(placed_ref[...], all_ref[...]).astype(BF16)
+    for at, send_ref in enumerate(send_refs):
+        send_ref[...] = rows[at * rows_each : (at + 1) * rows_each]
 
 
 def self_kernel(
@@ -313,19 +319,32 @@
     ).astype(BF16)
 
 
-def sum_kernel(tp, owned_ref, got_ref, kg_ref, vg_ref):
-    store_rows, tokens, features = kg_ref.shape
+def sum_kernel(chunks, owned_ref, *refs):
+    got_refs, (kg_any, vg_any, kg_ref, vg_ref, sems) = refs[:-5], refs[-5:]
+    slots, tokens, features = kg_ref.shape
+    tp = NEIGHBOUR_LENGTH // tokens
     width = features // tp
-    owned = owned_ref[...]
-    got = got_ref[...].reshape(owned.shape[1], 2 * features)
-    for z in range(tp):
-        total = dot_nn(owned, got[:, 2 * z * width : 2 * (z + 1) * width]).astype(BF16)
-        cols = slice(z * width, (z + 1) * width)
-        kg_ref[:, :, cols] = total[:, :width].reshape(store_rows, tokens, width)
-        vg_ref[:, :, cols] = total[:, width:].reshape(store_rows, tokens, width)
-
-
-def call(kernel, name, ins, outs, flops, bytes_accessed, scratch=(), scalars=0, fetched=0):
+    got = jnp.concatenate([ref[...] for ref in got_refs], axis=0)
+    step = slots // chunks
+    copies = []
+    for i in range(chunks):
+        part = slice(i * step, (i + 1) * step)
+        total = dot_nn(owned_ref[i * step * tokens : (i + 1) * step * tokens], got).astype(BF16)
+        for z in range(tp):
+            cols = slice(z * width, (z + 1) * width)
+            at = 2 * z * width
+            kg_ref[part, :, cols] = total[:, at : at + width].reshape(step, tokens, width)
+            vg_ref[part, :, cols] = total[:, at + width : at + 2 * width].reshape(
+                step, tokens, width
+            )
+        for j, (ref, out) in enumerate(((kg_ref, kg_any), (vg_ref, vg_any))):
+            copies.append(pltpu.make_async_copy(ref.at[part], out.at[part], sems.at[2 * i + j]))
+            copies[-1].start()
+    for copy in copies:
+        copy.wait()
+
+
+def call(kernel, name, ins, outs, flops, bytes_accessed, scratch=(), scalars=0, fetched=0, stores=False):
     direct = len(ins) - fetched
     ins = ins[:direct] + tuple(
         pltpu.with_memory_space_constraint(each, pltpu.HBM) for each in ins[direct:]
@@ -334,7 +353,7 @@
         kernel,
         out_shape=tuple(outs),
         in_specs=[SMEM] * scalars + [VMEM] * (direct - scalars) + [ANY] * fetched,
-        out_specs=tuple(SMEM if len(out.shape) == 1 else VMEM for out in outs),
+        out_specs=(ANY if stores else VMEM,) * len(outs),
         scratch_shapes=list(scratch),
         compiler_params=pltpu.CompilerParams(vmem_limit_bytes=16 * 1024 * 1024),
         cost_estimate=pl.CostEstimate(
@@ -406,13 +425,12 @@
         known = jnp.concatenate([known, swapped(known, "seq", step)], axis=0)
         step *= 2
     pieces = [known] + [swapped(known, "seq", far) for far in range(step, devices, step)]
-    sources = list(range(devices))
 
     chunks = 4
     store, halo, placed = call(
         functools.partial(stage_kernel, rows_each, chunks),
         "stage_store",
-        (nbr_owner, enc_keys, encoded_values, sequence_keys, sequence_values),
+        (rank, nbr_owner, enc_keys, encoded_values, sequence_keys, sequence_values),
         (
             struct((store_rows, 2 * enc_keys.shape[2]), BF16),
             struct((window, both), BF16),
@@ -426,21 +444,46 @@
             pltpu.VMEM(encoded_values.shape, BF16),
             pltpu.SemaphoreType.DMA((2 * chunks + 3,)),
         ],
+        scalars=1,
         fetched=5,
     )
-    sent, owned = call(
-        functools.partial(pack_kernel, sources),
+    *sent, owned = call(
+        functools.partial(pack_kernel, len(pieces)),
         "pack_requests",
         (rank, store, *pieces),
-        (struct((devices, rows_each, tp * both), BF16), struct((store_rows, lanes), BF16)),
+        [struct((rows_each, tp * both), BF16)] * devices + [struct((store_rows, lanes), BF16)],
         200_000_000,
         2_000_000,
         scalars=1,
     )
-    sent, halo = lax.optimization_barrier((sent, halo))
-    got = lax.all_to_all(sent, "seq", split_axis=0, concat_axis=0, tiled=True)
+    got = [sent[0]] + [swapped(sent[j], "seq", j) for j in range(1, devices)]
+    spread = call(
+        functools.partial(spread_kernel, tp),
+        "spread_rows",
+        (z_rank, placed, *got),
+        [struct((used, both), BF16)] * tp,
+        50_000_000,
+        1_000_000,
+        scratch=[pltpu.VMEM((used, tp * both), BF16)],
+        scalars=1,
+    )
+    near = exchanged(spread)
+    near[1], halo = lax.optimization_barrier((near[1], halo))
     halo = lax.ppermute(halo, "seq", [(i, i + 1) for i in range(devices - 1)])
 
+    blocks = spans * groups
+    rows_span = per_span * NEIGHBOUR_LENGTH
+    *grads, weights, grad_scores = call(
+        functools.partial(cross_kernel, tp),
+        "cross_attention",
+        (queries, output_gradient, *near),
+        [struct((used, both), BF16)] * tp
+        + [struct((blocks, rows_span, GROUP * SPAN_TOKENS), BF16)] * 2,
+        600_000_000,
+        3_000_000,
+    )
+    grads, halo = lax.optimization_barrier((grads, halo))
+    grads = exchanged(grads)
     self_out, self_dq, self_dkv, back = call(
         self_kernel,
         "self_attention",
@@ -455,48 +498,21 @@
         6_000_000,
         scalars=1,
     )
-
-    got, self_out, self_dq, self_dkv, back = lax.optimization_barrier(
-        (got, self_out, self_dq, self_dkv, back)
-    )
-    spread = call(
-        functools.partial(spread_kernel, tp),
-        "spread_rows",
-        (z_rank, placed, got),
-        [struct((used, both), BF16)] * tp,
+    back = lax.ppermute(back, "seq", [(i + 1, i) for i in range(devices - 1)])
+    grads, self_out = lax.optimization_barrier((grads, self_out))
+
+    returned = call(
+        functools.partial(scatter_kernel, tp),
+        "scatter_gradients",
+        (z_rank, placed, *grads),
+        [struct((rows_each, tp * both), BF16)] * devices,
         50_000_000,
         1_000_000,
         scratch=[pltpu.VMEM((used, tp * both), BF16)],
         scalars=1,
     )
-    near = exchanged(spread)
-
-    blocks = spans * groups
-    rows_span = per_span * NEIGHBOUR_LENGTH
-    *grads, weights, grad_scores = call(
-        functools.partial(cross_kernel, tp),
-        "cross_attention",
-        (queries, output_gradient, *near),
-        [struct((used, both), BF16)] * tp
-        + [struct((blocks, rows_span, GROUP * SPAN_TOKENS), BF16)] * 2,
-        600_000_000,
-        3_000_000,
-    )
-    grads = exchanged(grads)
-    back = lax.ppermute(back, "seq", [(i + 1, i) for i in range(devices - 1)])
-
-    (returned,) = call(
-        functools.partial(scatter_kernel, tp),
-        "scatter_gradients",
-        (z_rank, placed, *grads),
-        (struct((devices, rows_each, tp * both), BF16),),
-        50_000_000,
-        1_000_000,
-        scratch=[pltpu.VMEM((used, tp * both), BF16)],
-        scalars=1,
-    )
     returned, weights = lax.optimization_barrier((returned, weights))
-    returned = lax.all_to_all(returned, "seq", split_axis=0, concat_axis=0, tiled=True)
+    returned = [returned[0]] + [swapped(returned[j], "seq", j) for j in range(1, devices)]
 
     attended, query_gradient, key_gradient, value_gradient = call(
         functools.partial(join_kernel, tp),
@@ -511,13 +527,20 @@
         300_000_000,
         5_000_000,
     )
+    returned, attended = lax.optimization_barrier((returned, attended))
     store_kgrad, store_vgrad = call(
-        functools.partial(sum_kernel, tp),
+        functools.partial(sum_kernel, chunks),
         "sum_store_gradients",
-        (owned, returned),
+        (owned, *returned),
         (struct(enc_keys.shape, BF16), struct(encoded_values.shape, BF16)),
         200_000_000,
         2_000_000,
+        scratch=[
+            pltpu.VMEM(enc_keys.shape, BF16),
+            pltpu.VMEM(encoded_values.shape, BF16),
+            pltpu.SemaphoreType.DMA((2 * chunks,)),
+        ],
+        stores=True,
     )
     return (
         attended,

time: 75.8 us -> 61.9 us (0.82)
  the two profiles are of different devices: /device:TPU:1 before, /device:TPU:0 now
where the time goes in v2:
time: 61.9 us; the launch traced here: 61.7 us
  starting transfers between devices  31.1 us (50%)
  waiting for transfers between devices  20.1 us (32%)
  Pallas kernels  9.7 us (16%)
  between operations  0.78 us (1%)
    ppermute x24, starting transfers between devices, swapped(): lax.ppermute(block, axis, [(i, i ^ apart) for i in range(lax.axis_size(ax...  28.5 us
    ppermute x24, waiting for transfers between devices, swapped(): lax.ppermute(block, axis, [(i, i ^ apart) for i in range(lax.axis_size(ax...  20.1 us
    pallas_call x9, Pallas kernels, call(): pl.pallas_call(kernel, out_shape=tuple(outs), in_specs=[SMEM] * scalars +...  9.7 us
    ppermute x1, starting transfers between devices, body(): back = lax.ppermute(back, 'seq', [(i + 1, i) for i in range(devices - 1)])  1.29 us
    ppermute x1, starting transfers between devices, body(): halo = lax.ppermute(halo, 'seq', [(i, i + 1) for i in range(devices - 1)])  1.29 us
  transfers between devices with their start and end apart: 26, of which 13 were waited for; matrix products, arithmetic and copies ran while one was open for 0% of the time, Pallas kernels for 11%

profile of v2, /device:TPU:0, one launch (start us, length us, event | category | flops | bytes accessed | tf_op | source)
XLA Modules:
  0.0 61.7 jit_solution(11361151918056320118)
XLA Ops:
  0.6 0.9 %plan_requests.1 = s32[8,128]{1,0:T(8,128)S(1)} custom-call(s32[4,4]{1,0:T(4,128)} %owner_any.3, s32[4,4]{1,0:T(4,128)} %slot_any.1), custom_call_target="tpu_custom_call" | custom-call | bytes 100000 | tf_op jit(solution)/shard_map/plan_requests/pallas_call | solution.py:352
  1.6 0.5 collective-permute-start
  2.1 0.8 %collective-permute-done = s32[1,8,128]{2,1,0:T(8,128)S(1)} collective-permute-done((s32[1,8,128]{2,1,0:T(8,128)S(1)}, s32[1,8,128]{2,1,0:T(8,128)S(1)}, u32[]{:S(2)}, u32[]{:S(2)}) %collective-permute-start) | collective-permute-done | bytes 4128 | tf_op jit(solution)/shard_map/ppermute | solution.py:367
  2.9 3.8 %collective-permute-start.3 = (s32[2,8,128]{2,1,0:T(8,128)S(1)}, s32[2,8,128]{2,1,0:T(8,128)S(1)}, u32[]{:S(2)}, u32[]{:S(2)}) collective-permute-start(s32[2,8,128]{2,1,0:T(8,128)S(1)} %pad_add_fusion.refs_0_), channel_id=1, source_target_pairs={{0,24},{4,28},{8,16},{12,20},{16,8},{20,12},{24,0},{28,4},{1,25},{... | collective-permute-start | bytes 24584 | tf_op jit(solution)/shard_map/ppermute | solution.py:367
  6.7 0.5 collective-permute-start.2
  7.3 1.4 %stage_store.1 = (bf16[256,2048]{1,0:T(8,128)(2,1)S(1)}, bf16[128,512]{1,0:T(8,128)(2,1)S(1)}, bf16[128,64]{1,0:T(8,128)(2,1)S(1)}) custom-call(s32[1]{0:T(128)} %bitcast.1.me_ref.rank_ref, s32[4,4]{1,0:T(4,128)} %owner_any.3, bf16[64,4,1024]{2,1,0:T(4,128)(2,1)} %k_any.1, bf16[64,4,1024]{2,1,0:T(4,128)(2,1)} %v_any.1, bf16[256,256]{1,0:T(8,128)(2,1)} %k_ref.1, ...), custom_call_target="tpu_custom_call" | custom-call | bytes 3000000 | tf_op jit(solution)/shard_map/stage_store/pallas_call | solution.py:352
  8.7 1.7 %collective-permute-done.2.refs_2_ = s32[2,8,128]{2,1,0:T(8,128)S(1)} collective-permute-done((s32[2,8,128]{2,1,0:T(8,128)S(1)}, s32[2,8,128]{2,1,0:T(8,128)S(1)}, u32[]{:S(2)}, u32[]{:S(2)}) %collective-permute-start.2) | collective-permute-done | bytes 8224 | tf_op jit(solution)/shard_map/ppermute | solution.py:367
  11.4 1.7 %collective-permute-start.6 = (bf16[16,2048]{1,0:T(8,128)(2,1)S(1)}, bf16[16,2048]{1,0:T(8,128)(2,1)S(1)}, u32[]{:S(2)}, u32[]{:S(2)}) collective-permute-start(bf16[16,2048]{1,0:T(8,128)(2,1)S(1)} %get-tuple-element.81), channel_id=1, source_target_pairs={{0,12},{4,8},{8,4},{12,0},{16,28},{20,24},{24,20},{28,16},{1,13},{... | collective-permute-start | bytes 196616 | tf_op jit(solution)/shard_map/ppermute | solution.py:367
  13.1 1.5 %collective-permute-start.7 = (bf16[16,2048]{1,0:T(8,128)(2,1)S(1)}, bf16[16,2048]{1,0:T(8,128)(2,1)S(1)}, u32[]{:S(2)}, u32[]{:S(2)}) collective-permute-start(bf16[16,2048]{1,0:T(8,128)(2,1)S(1)} %get-tuple-element.82), channel_id=1, source_target_pairs={{0,16},{4,20},{8,24},{12,28},{16,0},{20,4},{24,8},{28,12},{1,17},{... | collective-permute-start | bytes 196616 | tf_op jit(solution)/shard_map/ppermute | solution.py:367
  14.8 1.5 %collective-permute-start.9 = (bf16[16,2048]{1,0:T(8,128)(2,1)S(1)}, bf16[16,2048]{1,0:T(8,128)(2,1)S(1)}, u32[]{:S(2)}, u32[]{:S(2)}) collective-permute-start(bf16[16,2048]{1,0:T(8,128)(2,1)S(1)} %get-tuple-element.84), channel_id=1, source_target_pairs={{0,24},{4,28},{8,16},{12,20},{16,8},{20,12},{24,0},{28,4},{1,25},{... | collective-permute-start | bytes 196616 | tf_op jit(solution)/shard_map/ppermute | solution.py:367
  16.3 1.2 %collective-permute-start.10 = (bf16[16,2048]{1,0:T(8,128)(2,1)S(1)}, bf16[16,2048]{1,0:T(8,128)(2,1)S(1)}, u32[]{:S(2)}, u32[]{:S(2)}) collective-permute-start(bf16[16,2048]{1,0:T(8,128)(2,1)S(1)} %get-tuple-element.85), channel_id=1, source_target_pairs={{0,28},{4,24},{8,20},{12,16},{16,12},{20,8},{24,4},{28,0},{1,29},{... | collective-permute-start | bytes 196616 | tf_op jit(solution)/shard_map/ppermute | solution.py:367
  17.6 1.3 %collective-permute-done.8.refs_5_ = bf16[16,2048]{1,0:T(8,128)(2,1)S(1)} collective-permute-done((bf16[16,2048]{1,0:T(8,128)(2,1)S(1)}, bf16[16,2048]{1,0:T(8,128)(2,1)S(1)}, u32[]{:S(2)}, u32[]{:S(2)}) %collective-permute-start.8) | collective-permute-done | bytes 65568 | tf_op jit(solution)/shard_map/ppermute | solution.py:367
  18.8 1.5 %collective-permute-done.9.refs_6_ = bf16[16,2048]{1,0:T(8,128)(2,1)S(1)} collective-permute-done((bf16[16,2048]{1,0:T(8,128)(2,1)S(1)}, bf16[16,2048]{1,0:T(8,128)(2,1)S(1)}, u32[]{:S(2)}, u32[]{:S(2)}) %collective-permute-start.9) | collective-permute-done | bytes 65568 | tf_op jit(solution)/shard_map/ppermute | solution.py:367
  20.3 1.1 %collective-permute-done.10.refs_7_ = bf16[16,2048]{1,0:T(8,128)(2,1)S(1)} collective-permute-done((bf16[16,2048]{1,0:T(8,128)(2,1)S(1)}, bf16[16,2048]{1,0:T(8,128)(2,1)S(1)}, u32[]{:S(2)}, u32[]{:S(2)}) %collective-permute-start.10) | collective-permute-done | bytes 65568 | tf_op jit(solution)/shard_map/ppermute | solution.py:367
  21.7 2.6 %collective-permute-start.11 = (bf16[64,512]{1,0:T(8,128)(2,1)S(1)}, bf16[64,512]{1,0:T(8,128)(2,1)S(1)}, u32[]{:S(2)}, u32[]{:S(2)}) collective-permute-start(bf16[64,512]{1,0:T(8,128)(2,1)S(1)} %get-tuple-element.87), channel_id=1, source_target_pairs={{0,2},{1,3},{2,0},{3,1},{4,6},{5,7},{6,4},{7,5},{8,10},{9,11},{10,... | collective-permute-start | bytes 196616 | tf_op jit(solution)/shard_map/ppermute | solution.py:367
  24.3 4.1 %collective-permute-done.11.refs_1_ = bf16[64,512]{1,0:T(8,128)(2,1)S(1)} collective-permute-done((bf16[64,512]{1,0:T(8,128)(2,1)S(1)}, bf16[64,512]{1,0:T(8,128)(2,1)S(1)}, u32[]{:S(2)}, u32[]{:S(2)}) %collective-permute-start.11) | collective-permute-done | bytes 65568 | tf_op jit(solution)/shard_map/ppermute | solution.py:367
  28.3 1.3 %collective-permute-start.14 = (bf16[128,512]{1,0:T(8,128)(2,1)S(1)}, bf16[128,512]{1,0:T(8,128)(2,1)S(1)}, u32[]{:S(2)}, u32[]{:S(2)}) collective-permute-start(bf16[128,512]{1,0:T(8,128)(2,1)S(1)} %get-tuple-element.96), channel_id=1, source_target_pairs={{0,4},{4,8},{8,12},{12,16},{16,20},{20,24},{24,28},{1,5},{5,9},{9,... | collective-permute-start | bytes 393224 | tf_op jit(solution)/shard_map/ppermute | solution.py:472
  29.6 4.2 %collective-permute-start.12 = (bf16[64,512]{1,0:T(8,128)(2,1)S(1)}, bf16[64,512]{1,0:T(8,128)(2,1)S(1)}, u32[]{:S(2)}, u32[]{:S(2)}) collective-permute-start(bf16[64,512]{1,0:T(8,128)(2,1)S(1)} %get-tuple-element.90), channel_id=1, source_target_pairs={{0,3},{1,2},{2,1},{3,0},{4,7},{5,6},{6,5},{7,4},{8,11},{9,10},{10,... | collective-permute-start | bytes 196616 | tf_op jit(solution)/shard_map/ppermute | solution.py:367
  33.9 2.3 %collective-permute-done.12.refs_2_ = bf16[64,512]{1,0:T(8,128)(2,1)S(1)} collective-permute-done((bf16[64,512]{1,0:T(8,128)(2,1)S(1)}, bf16[64,512]{1,0:T(8,128)(2,1)S(1)}, u32[]{:S(2)}, u32[]{:S(2)}) %collective-permute-start.12) | collective-permute-done | bytes 65568 | tf_op jit(solution)/shard_map/ppermute | solution.py:367
  36.2 2.7 %collective-permute-done.13.refs_3_ = bf16[64,512]{1,0:T(8,128)(2,1)S(1)} collective-permute-done((bf16[64,512]{1,0:T(8,128)(2,1)S(1)}, bf16[64,512]{1,0:T(8,128)(2,1)S(1)}, u32[]{:S(2)}, u32[]{:S(2)}) %collective-permute-start.13) | collective-permute-done | bytes 65568 | tf_op jit(solution)/shard_map/ppermute | solution.py:367
  38.9 0.8 %cross_attention.1 = (bf16[64,512]{1,0:T(8,128)(2,1)S(1)}, bf16[64,512]{1,0:T(8,128)(2,1)S(1)}, bf16[64,512]{1,0:T(8,128)(2,1)S(1)}, bf16[64,512]{1,0:T(8,128)(2...) custom-call(bf16[256,1024]{1,0:T(8,128)(2,1)S(1)} %copy-done.2, ...), custom_call_target="tpu_custom_call" | custom-call | flops 600000000 | bytes 3000000 | tf_op jit(solution)/shard_map/cross_attention/pallas_call | solution.py:352
  39.7 3.4 %collective-permute-start.16 = (bf16[64,512]{1,0:T(8,128)(2,1)S(1)}, bf16[64,512]{1,0:T(8,128)(2,1)S(1)}, u32[]{:S(2)}, u32[]{:S(2)}) collective-permute-start(bf16[64,512]{1,0:T(8,128)(2,1)S(1)} %get-tuple-element.99), channel_id=1, source_target_pairs={{0,3},{1,2},{2,1},{3,0},{4,7},{5,6},{6,5},{7,4},{8,11},{9,10},{10,... | collective-permute-start | bytes 196616 | tf_op jit(solution)/shard_map/ppermute | solution.py:367
  43.2 2.9 %self_attention.1 = (f32[256,1024]{1,0:T(8,128)S(1)}, f32[256,1024]{1,0:T(8,128)S(1)}, f32[256,512]{1,0:T(8,128)S(1)}, bf16[128,512]{1,0:T(8,128)(2,1)S(1)}) custom-call(s32[1]{0:T(128)} %bitcast.1.me_ref.rank_ref, bf16[256,1024]{1,0:T(8,128)(2,1)S(1)} %copy-done.2, bf16[256,256]{1,0:T(8,128)(2,1)S(1)} %copy-done, bf16[256,256]{1,0:T(8,128)(2,1)S(1)} %copy-done.1, ...), custom_call_target="tpu_custom_call" | custom-call | flops 1600000000 | bytes 6000000 | tf_op jit(solution)/shard_map/self_attention/pallas_call | solution.py:352
  46.1 1.3 %collective-permute-start.25 = (bf16[128,512]{1,0:T(8,128)(2,1)S(1)}, bf16[128,512]{1,0:T(8,128)(2,1)S(1)}, u32[]{:S(2)}, u32[]{:S(2)}) collective-permute-start(bf16[128,512]{1,0:T(8,128)(2,1)S(1)} %get-tuple-element.129), channel_id=1, source_target_pairs={{4,0},{8,4},{12,8},{16,12},{20,16},{24,20},{28,24},{5,1},{9,5},{13... | collective-permute-start | bytes 393224 | tf_op jit(solution)/shard_map/ppermute | solution.py:501
  47.4 0.7 %collective-permute-done.15.refs_1_ = bf16[64,512]{1,0:T(8,128)(2,1)S(1)} collective-permute-done((bf16[64,512]{1,0:T(8,128)(2,1)S(1)}, bf16[64,512]{1,0:T(8,128)(2,1)S(1)}, u32[]{:S(2)}, u32[]{:S(2)}) %collective-permute-start.15) | collective-permute-done | bytes 65568 | tf_op jit(solution)/shard_map/ppermute | solution.py:367
  48.9 1.5 %collective-permute-start.19 = (bf16[16,2048]{1,0:T(8,128)(2,1)S(1)}, bf16[16,2048]{1,0:T(8,128)(2,1)S(1)}, u32[]{:S(2)}, u32[]{:S(2)}) collective-permute-start(bf16[16,2048]{1,0:T(8,128)(2,1)S(1)} %get-tuple-element.118), channel_id=1, source_target_pairs={{0,8},{4,12},{8,0},{12,4},{16,24},{20,28},{24,16},{28,20},{1,9},{5... | collective-permute-start | bytes 196616 | tf_op jit(solution)/shard_map/ppermute | solution.py:367
  50.8 1.3 %collective-permute-start.21 = (bf16[16,2048]{1,0:T(8,128)(2,1)S(1)}, bf16[16,2048]{1,0:T(8,128)(2,1)S(1)}, u32[]{:S(2)}, u32[]{:S(2)}) collective-permute-start(bf16[16,2048]{1,0:T(8,128)(2,1)S(1)} %get-tuple-element.120), channel_id=1, source_target_pairs={{0,16},{4,20},{8,24},{12,28},{16,0},{20,4},{24,8},{28,12},{1,17},{... | collective-permute-start | bytes 196616 | tf_op jit(solution)/shard_map/ppermute | solution.py:367
  52.5 3.4 %collective-permute-start.23 = (bf16[16,2048]{1,0:T(8,128)(2,1)S(1)}, bf16[16,2048]{1,0:T(8,128)(2,1)S(1)}, u32[]{:S(2)}, u32[]{:S(2)}) collective-permute-start(bf16[16,2048]{1,0:T(8,128)(2,1)S(1)} %get-tuple-element.122), channel_id=1, source_target_pairs={{0,24},{4,28},{8,16},{12,20},{16,8},{20,12},{24,0},{28,4},{1,25},{... | collective-permute-start | bytes 196616 | tf_op jit(solution)/shard_map/ppermute | solution.py:367
  55.8 1.6 %join_outputs.1 = (bf16[256,1024]{1,0:T(8,128)(2,1)}, bf16[256,1024]{1,0:T(8,128)(2,1)}, bf16[256,256]{1,0:T(8,128)(2,1)}, bf16[256,256]{1,0:T(8,128)(2,1)}) custom-call(bf16[8,64,256]{2,1,0:T(8,128)(2,1)S(1)} %get-tuple-element.124.w_ref, bf16[8,64,256]{2,1,0:T(8,128)(2,1)S(1)} %get-tuple-element.125.ds_ref, f32[256,1024]{1,0:T(8,128)S(1)} %get-tuple-element.126.out_ref, ...), custom_call_target="tpu_custom_call" | custom-call | flops 300000000 | bytes 5000000 | tf_op jit(solution)/shard_map/join_outputs/pallas_call | solution.py:352
  57.4 0.7 %collective-permute-done.23.refs_6_ = bf16[16,2048]{1,0:T(8,128)(2,1)S(1)} collective-permute-done((bf16[16,2048]{1,0:T(8,128)(2,1)S(1)}, bf16[16,2048]{1,0:T(8,128)(2,1)S(1)}, u32[]{:S(2)}, u32[]{:S(2)}) %collective-permute-start.23) | collective-permute-done | bytes 65568 | tf_op jit(solution)/shard_map/ppermute | solution.py:367
  58.2 2.2 %collective-permute-done.24.refs_7_ = bf16[16,2048]{1,0:T(8,128)(2,1)S(1)} collective-permute-done((bf16[16,2048]{1,0:T(8,128)(2,1)S(1)}, bf16[16,2048]{1,0:T(8,128)(2,1)S(1)}, u32[]{:S(2)}, u32[]{:S(2)}) %collective-permute-start.24) | collective-permute-done | bytes 65568 | tf_op jit(solution)/shard_map/ppermute | solution.py:367
  60.4 1.3 %sum_store_gradients.1 = (bf16[64,4,1024]{2,1,0:T(4,128)(2,1)}, bf16[64,4,1024]{2,1,0:T(4,128)(2,1)}) custom-call(bf16[256,128]{1,0:T(8,128)(2,1)S(1)} %get-tuple-element.135.owned_ref, bf16[16,2048]{1,0:T(8,128)(2,1)S(1)} %get-tuple-element.136.refs_0_, bf16[16,2048]{1,0:T(8,128)(2,1)S(1)} %collective-permute-done.18.refs_1_, ...), custom_call_target="tpu_custom_call" | custom-call | flops 200000000 | bytes 2000000 | tf_op jit(solution)/shard_map/sum_store_gradients/pallas_call | solution.py:352
  (38 shorter events, 3.3 us)
Async XLA Ops:
  1.6 1.3 %collective-permute-start = (s32[1,8,128]{2,1,0:T(8,128)S(1)}, s32[1,8,128]{2,1,0:T(8,128)S(1)}, u32[]{:S(2)}, u32[]{:S(2)}) collective-permute-start(s32[1,8,128]{2,1,0:T(8,128)S(1)} %bitcast.3), channel_id=1, source_target_pairs={{0,4},{4,0},{8,12},{12,8},{16,20},{20,16},{24,28},{28,24},{1,5},{5... | collective-permute-start | bytes 12296 | tf_op jit(solution)/shard_map/ppermute | solution.py:367
  2.9 5.8 %collective-permute-start.3 = (s32[2,8,128]{2,1,0:T(8,128)S(1)}, s32[2,8,128]{2,1,0:T(8,128)S(1)}, u32[]{:S(2)}, u32[]{:S(2)}) collective-permute-start(s32[2,8,128]{2,1,0:T(8,128)S(1)} %pad_add_fusion.refs_0_), channel_id=1, source_target_pairs={{0,24},{4,28},{8,16},{12,20},{16,8},{20,12},{24,0},{28,4},{1,25},{... | collective-permute-start | bytes 24584 | tf_op jit(solution)/shard_map/ppermute | solution.py:367
  6.7 3.7 %collective-permute-start.2 = (s32[2,8,128]{2,1,0:T(8,128)S(1)}, s32[2,8,128]{2,1,0:T(8,128)S(1)}, u32[]{:S(2)}, u32[]{:S(2)}) collective-permute-start(s32[2,8,128]{2,1,0:T(8,128)S(1)} %pad_add_fusion.refs_0_), channel_id=1, source_target_pairs={{0,16},{4,20},{8,24},{12,28},{16,0},{20,4},{24,8},{28,12},{1,17},{... | collective-permute-start | bytes 24584 | tf_op jit(solution)/shard_map/ppermute | solution.py:367
  7.2 3.7 %collective-permute-start.1 = (s32[2,8,128]{2,1,0:T(8,128)S(1)}, s32[2,8,128]{2,1,0:T(8,128)S(1)}, u32[]{:S(2)}, u32[]{:S(2)}) collective-permute-start(s32[2,8,128]{2,1,0:T(8,128)S(1)} %pad_add_fusion.refs_0_), channel_id=1, source_target_pairs={{0,8},{4,12},{8,0},{12,4},{16,24},{20,28},{24,16},{28,20},{1,9},{5... | collective-permute-start | bytes 24584 | tf_op jit(solution)/shard_map/ppermute | solution.py:367
  10.8 28.0 %copy-start.3 = (bf16[256,1024]{1,0:T(8,128)(2,1)S(1)}, bf16[256,1024]{1,0:T(8,128)(2,1)}, u32[]{:S(2)}) copy-start(bf16[256,1024]{1,0:T(8,128)(2,1)} %do_ref.3) | copy-start | bytes 1572868
  11.2 27.7 %copy-start.2 = (bf16[256,1024]{1,0:T(8,128)(2,1)S(1)}, bf16[256,1024]{1,0:T(8,128)(2,1)}, u32[]{:S(2)}) copy-start(bf16[256,1024]{1,0:T(8,128)(2,1)} %q_ref.3) | copy-start | bytes 1572868
  11.2 3.6 %collective-permute-start.4 = (bf16[16,2048]{1,0:T(8,128)(2,1)S(1)}, bf16[16,2048]{1,0:T(8,128)(2,1)S(1)}, u32[]{:S(2)}, u32[]{:S(2)}) collective-permute-start(bf16[16,2048]{1,0:T(8,128)(2,1)S(1)} %get-tuple-element.79), channel_id=1, source_target_pairs={{0,4},{4,0},{8,12},{12,8},{16,20},{20,16},{24,28},{28,24},{1,5},{5... | collective-permute-start | bytes 196616 | tf_op jit(solution)/shard_map/ppermute | solution.py:367
  11.3 5.1 %collective-permute-start.5 = (bf16[16,2048]{1,0:T(8,128)(2,1)S(1)}, bf16[16,2048]{1,0:T(8,128)(2,1)S(1)}, u32[]{:S(2)}, u32[]{:S(2)}) collective-permute-start(bf16[16,2048]{1,0:T(8,128)(2,1)S(1)} %get-tuple-element.80), channel_id=1, source_target_pairs={{0,8},{4,12},{8,0},{12,4},{16,24},{20,28},{24,16},{28,20},{1,9},{5... | collective-permute-start | bytes 196616 | tf_op jit(solution)/shard_map/ppermute | solution.py:367
  11.4 6.1 %collective-permute-start.6 = (bf16[16,2048]{1,0:T(8,128)(2,1)S(1)}, bf16[16,2048]{1,0:T(8,128)(2,1)S(1)}, u32[]{:S(2)}, u32[]{:S(2)}) collective-permute-start(bf16[16,2048]{1,0:T(8,128)(2,1)S(1)} %get-tuple-element.81), channel_id=1, source_target_pairs={{0,12},{4,8},{8,4},{12,0},{16,28},{20,24},{24,20},{28,16},{1,13},{... | collective-permute-start | bytes 196616 | tf_op jit(solution)/shard_map/ppermute | solution.py:367
  13.1 4.4 %collective-permute-start.7 = (bf16[16,2048]{1,0:T(8,128)(2,1)S(1)}, bf16[16,2048]{1,0:T(8,128)(2,1)S(1)}, u32[]{:S(2)}, u32[]{:S(2)}) collective-permute-start(bf16[16,2048]{1,0:T(8,128)(2,1)S(1)} %get-tuple-element.82), channel_id=1, source_target_pairs={{0,16},{4,20},{8,24},{12,28},{16,0},{20,4},{24,8},{28,12},{1,17},{... | collective-permute-start | bytes 196616 | tf_op jit(solution)/shard_map/ppermute | solution.py:367
  14.7 4.2 %collective-permute-start.8 = (bf16[16,2048]{1,0:T(8,128)(2,1)S(1)}, bf16[16,2048]{1,0:T(8,128)(2,1)S(1)}, u32[]{:S(2)}, u32[]{:S(2)}) collective-permute-start(bf16[16,2048]{1,0:T(8,128)(2,1)S(1)} %get-tuple-element.83), channel_id=1, source_target_pairs={{0,20},{4,16},{8,28},{12,24},{16,4},{20,0},{24,12},{28,8},{1,21},{... | collective-permute-start | bytes 196616 | tf_op jit(solution)/shard_map/ppermute | solution.py:367
  14.8 5.4 %collective-permute-start.9 = (bf16[16,2048]{1,0:T(8,128)(2,1)S(1)}, bf16[16,2048]{1,0:T(8,128)(2,1)S(1)}, u32[]{:S(2)}, u32[]{:S(2)}) collective-permute-start(bf16[16,2048]{1,0:T(8,128)(2,1)S(1)} %get-tuple-element.84), channel_id=1, source_target_pairs={{0,24},{4,28},{8,16},{12,20},{16,8},{20,12},{24,0},{28,4},{1,25},{... | collective-permute-start | bytes 196616 | tf_op jit(solution)/shard_map/ppermute | solution.py:367
  16.3 5.1 %collective-permute-start.10 = (bf16[16,2048]{1,0:T(8,128)(2,1)S(1)}, bf16[16,2048]{1,0:T(8,128)(2,1)S(1)}, u32[]{:S(2)}, u32[]{:S(2)}) collective-permute-start(bf16[16,2048]{1,0:T(8,128)(2,1)S(1)} %get-tuple-element.85), channel_id=1, source_target_pairs={{0,28},{4,24},{8,20},{12,16},{16,12},{20,8},{24,4},{28,0},{1,29},{... | collective-permute-start | bytes 196616 | tf_op jit(solution)/shard_map/ppermute | solution.py:367
  21.7 6.6 %collective-permute-start.11 = (bf16[64,512]{1,0:T(8,128)(2,1)S(1)}, bf16[64,512]{1,0:T(8,128)(2,1)S(1)}, u32[]{:S(2)}, u32[]{:S(2)}) collective-permute-start(bf16[64,512]{1,0:T(8,128)(2,1)S(1)} %get-tuple-element.87), channel_id=1, source_target_pairs={{0,2},{1,3},{2,0},{3,1},{4,6},{5,7},{6,4},{7,5},{8,10},{9,11},{10,... | collective-permute-start | bytes 196616 | tf_op jit(solution)/shard_map/ppermute | solution.py:367
  28.3 11.3 %collective-permute-start.14 = (bf16[128,512]{1,0:T(8,128)(2,1)S(1)}, bf16[128,512]{1,0:T(8,128)(2,1)S(1)}, u32[]{:S(2)}, u32[]{:S(2)}) collective-permute-start(bf16[128,512]{1,0:T(8,128)(2,1)S(1)} %get-tuple-element.96), channel_id=1, source_target_pairs={{0,4},{4,8},{8,12},{12,16},{16,20},{20,24},{24,28},{1,5},{5,9},{9,... | collective-permute-start | bytes 393224 | tf_op jit(solution)/shard_map/ppermute | solution.py:472
  29.6 6.5 %collective-permute-start.12 = (bf16[64,512]{1,0:T(8,128)(2,1)S(1)}, bf16[64,512]{1,0:T(8,128)(2,1)S(1)}, u32[]{:S(2)}, u32[]{:S(2)}) collective-permute-start(bf16[64,512]{1,0:T(8,128)(2,1)S(1)} %get-tuple-element.90), channel_id=1, source_target_pairs={{0,3},{1,2},{2,1},{3,0},{4,7},{5,6},{6,5},{7,4},{8,11},{9,10},{10,... | collective-permute-start | bytes 196616 | tf_op jit(solution)/shard_map/ppermute | solution.py:367
  33.9 5.0 %collective-permute-start.13 = (bf16[64,512]{1,0:T(8,128)(2,1)S(1)}, bf16[64,512]{1,0:T(8,128)(2,1)S(1)}, u32[]{:S(2)}, u32[]{:S(2)}) collective-permute-start(bf16[64,512]{1,0:T(8,128)(2,1)S(1)} %get-tuple-element.91), channel_id=1, source_target_pairs={{0,1},{1,0},{2,3},{3,2},{4,5},{5,4},{6,7},{7,6},{8,9},{9,8},{10,11... | collective-permute-start | bytes 196616 | tf_op jit(solution)/shard_map/ppermute | solution.py:367
  38.9 4.3 %copy-start = (bf16[256,256]{1,0:T(8,128)(2,1)S(1)}, bf16[256,256]{1,0:T(8,128)(2,1)}, u32[]{:S(2)}) copy-start(bf16[256,256]{1,0:T(8,128)(2,1)} %k_ref.1) | copy-start | bytes 393220
  38.9 4.3 %copy-start.1 = (bf16[256,256]{1,0:T(8,128)(2,1)S(1)}, bf16[256,256]{1,0:T(8,128)(2,1)}, u32[]{:S(2)}) copy-start(bf16[256,256]{1,0:T(8,128)(2,1)} %v_ref.1) | copy-start | bytes 393220
  39.6 8.5 %collective-permute-start.15 = (bf16[64,512]{1,0:T(8,128)(2,1)S(1)}, bf16[64,512]{1,0:T(8,128)(2,1)S(1)}, u32[]{:S(2)}, u32[]{:S(2)}) collective-permute-start(bf16[64,512]{1,0:T(8,128)(2,1)S(1)} %get-tuple-element.98), channel_id=1, source_target_pairs={{0,2},{1,3},{2,0},{3,1},{4,6},{5,7},{6,4},{7,5},{8,10},{9,11},{10,... | collective-permute-start | bytes 196616 | tf_op jit(solution)/shard_map/ppermute | solution.py:367
  39.7 8.4 %collective-permute-start.16 = (bf16[64,512]{1,0:T(8,128)(2,1)S(1)}, bf16[64,512]{1,0:T(8,128)(2,1)S(1)}, u32[]{:S(2)}, u32[]{:S(2)}) collective-permute-start(bf16[64,512]{1,0:T(8,128)(2,1)S(1)} %get-tuple-element.99), channel_id=1, source_target_pairs={{0,3},{1,2},{2,1},{3,0},{4,7},{5,6},{6,5},{7,4},{8,11},{9,10},{10,... | collective-permute-start | bytes 196616 | tf_op jit(solution)/shard_map/ppermute | solution.py:367
  43.1 5.4 %collective-permute-start.17 = (bf16[64,512]{1,0:T(8,128)(2,1)S(1)}, bf16[64,512]{1,0:T(8,128)(2,1)S(1)}, u32[]{:S(2)}, u32[]{:S(2)}) collective-permute-start(bf16[64,512]{1,0:T(8,128)(2,1)S(1)} %get-tuple-element.100), channel_id=1, source_target_pairs={{0,1},{1,0},{2,3},{3,2},{4,5},{5,4},{6,7},{7,6},{8,9},{9,8},{10,11... | collective-permute-start | bytes 196616 | tf_op jit(solution)/shard_map/ppermute | solution.py:367
  46.1 6.0 %collective-permute-start.25 = (bf16[128,512]{1,0:T(8,128)(2,1)S(1)}, bf16[128,512]{1,0:T(8,128)(2,1)S(1)}, u32[]{:S(2)}, u32[]{:S(2)}) collective-permute-start(bf16[128,512]{1,0:T(8,128)(2,1)S(1)} %get-tuple-element.129), channel_id=1, source_target_pairs={{4,0},{8,4},{12,8},{16,12},{20,16},{24,20},{28,24},{5,1},{9,5},{13... | collective-permute-start | bytes 393224 | tf_op jit(solution)/shard_map/ppermute | solution.py:501
  48.8 3.6 %collective-permute-start.18 = (bf16[16,2048]{1,0:T(8,128)(2,1)S(1)}, bf16[16,2048]{1,0:T(8,128)(2,1)S(1)}, u32[]{:S(2)}, u32[]{:S(2)}) collective-permute-start(bf16[16,2048]{1,0:T(8,128)(2,1)S(1)} %get-tuple-element.117), channel_id=1, source_target_pairs={{0,4},{4,0},{8,12},{12,8},{16,20},{20,16},{24,28},{28,24},{1,5},{5... | collective-permute-start | bytes 196616 | tf_op jit(solution)/shard_map/ppermute | solution.py:367
  48.9 6.9 %collective-permute-start.19 = (bf16[16,2048]{1,0:T(8,128)(2,1)S(1)}, bf16[16,2048]{1,0:T(8,128)(2,1)S(1)}, u32[]{:S(2)}, u32[]{:S(2)}) collective-permute-start(bf16[16,2048]{1,0:T(8,128)(2,1)S(1)} %get-tuple-element.118), channel_id=1, source_target_pairs={{0,8},{4,12},{8,0},{12,4},{16,24},{20,28},{24,16},{28,20},{1,9},{5... | collective-permute-start | bytes 196616 | tf_op jit(solution)/shard_map/ppermute | solution.py:367
  50.5 7.0 %collective-permute-start.20 = (bf16[16,2048]{1,0:T(8,128)(2,1)S(1)}, bf16[16,2048]{1,0:T(8,128)(2,1)S(1)}, u32[]{:S(2)}, u32[]{:S(2)}) collective-permute-start(bf16[16,2048]{1,0:T(8,128)(2,1)S(1)} %get-tuple-element.119), channel_id=1, source_target_pairs={{0,12},{4,8},{8,4},{12,0},{16,28},{20,24},{24,20},{28,16},{1,13},{... | collective-permute-start | bytes 196616 | tf_op jit(solution)/shard_map/ppermute | solution.py:367
  50.8 6.7 %collective-permute-start.21 = (bf16[16,2048]{1,0:T(8,128)(2,1)S(1)}, bf16[16,2048]{1,0:T(8,128)(2,1)S(1)}, u32[]{:S(2)}, u32[]{:S(2)}) collective-permute-start(bf16[16,2048]{1,0:T(8,128)(2,1)S(1)} %get-tuple-element.120), channel_id=1, source_target_pairs={{0,16},{4,20},{8,24},{12,28},{16,0},{20,4},{24,8},{28,12},{1,17},{... | collective-permute-start | bytes 196616 | tf_op jit(solution)/shard_map/ppermute | solution.py:367
  52.1 5.4 %collective-permute-start.22 = (bf16[16,2048]{1,0:T(8,128)(2,1)S(1)}, bf16[16,2048]{1,0:T(8,128)(2,1)S(1)}, u32[]{:S(2)}, u32[]{:S(2)}) collective-permute-start(bf16[16,2048]{1,0:T(8,128)(2,1)S(1)} %get-tuple-element.121), channel_id=1, source_target_pairs={{0,20},{4,16},{8,28},{12,24},{16,4},{20,0},{24,12},{28,8},{1,21},{... | collective-permute-start | bytes 196616 | tf_op jit(solution)/shard_map/ppermute | solution.py:367
  52.5 5.7 %collective-permute-start.23 = (bf16[16,2048]{1,0:T(8,128)(2,1)S(1)}, bf16[16,2048]{1,0:T(8,128)(2,1)S(1)}, u32[]{:S(2)}, u32[]{:S(2)}) collective-permute-start(bf16[16,2048]{1,0:T(8,128)(2,1)S(1)} %get-tuple-element.122), channel_id=1, source_target_pairs={{0,24},{4,28},{8,16},{12,20},{16,8},{20,12},{24,0},{28,4},{1,25},{... | collective-permute-start | bytes 196616 | tf_op jit(solution)/shard_map/ppermute | solution.py:367
  55.8 4.6 %collective-permute-start.24 = (bf16[16,2048]{1,0:T(8,128)(2,1)S(1)}, bf16[16,2048]{1,0:T(8,128)(2,1)S(1)}, u32[]{:S(2)}, u32[]{:S(2)}) collective-permute-start(bf16[16,2048]{1,0:T(8,128)(2,1)S(1)} %get-tuple-element.123), channel_id=1, source_target_pairs={{0,28},{4,24},{8,20},{12,16},{16,12},{20,8},{24,4},{28,0},{1,29},{... | collective-permute-start | bytes 196616 | tf_op jit(solution)/shard_map/ppermute | solution.py:367

commit v3 on v2

--- a/solution.py
+++ b/solution.py
@@ -177,14 +177,14 @@
     owned = jnp.where(row == target, 1.0, 0.0).astype(BF16)
     owned_ref[...] = owned
     picked = dot_tn(owned, store_ref[...]).astype(BF16)
-    for at, send_ref in enumerate(send_refs):
+    for at, send_ref in enumerate(by_distance(send_refs)):
         send_ref[...] = picked[at * rows_each : (at + 1) * rows_each]
 
 
 def spread_kernel(tp, z_ref, placed_ref, *refs):
     got_refs, send_refs, near_ref = refs[: -tp - 1], refs[-tp - 1 : -1], refs[-1]
     both = send_refs[0].shape[1]
-    got = jnp.concatenate([ref[...] for ref in got_refs], axis=0)
+    got = jnp.concatenate([ref[...] for ref in by_distance(got_refs)], axis=0)
     near_ref[...] = dot_tn(placed_ref[...], got).astype(BF16)
     for apart, send_ref in zip(distances(tp), send_refs):
         start = pl.multiple_of((z_ref[0] ^ apart) * both, both)
@@ -199,7 +199,7 @@
         start = pl.multiple_of((z_ref[0] ^ apart) * both, both)
         all_ref[:, pl.ds(start, both)] = grad_ref[...]
     rows = dot_nn(placed_ref[...], all_ref[...]).astype(BF16)
-    for at, send_ref in enumerate(send_refs):
+    for at, send_ref in enumerate(by_distance(send_refs)):
         send_ref[...] = rows[at * rows_each : (at + 1) * rows_each]
 
 
@@ -324,7 +324,7 @@
     slots, tokens, features = kg_ref.shape
     tp = NEIGHBOUR_LENGTH // tokens
     width = features // tp
-    got = jnp.concatenate([ref[...] for ref in got_refs], axis=0)
+    got = jnp.concatenate([ref[...] for ref in by_distance(got_refs)], axis=0)
     step = slots // chunks
     copies = []
     for i in range(chunks):
@@ -365,6 +365,23 @@
 
 def swapped(block, axis, apart):
     return lax.ppermute(block, axis, [(i, i ^ apart) for i in range(lax.axis_size(axis))])
+
+
+def plane_order(devices):
+    def key(j):
+        return (j == 1, j & 1, -bin(j >> 1).count("1"), j)
+
+    return [0] + sorted(range(1, devices), key=key)
+
+
+def by_distance(refs):
+    order = plane_order(len(refs))
+    return [refs[order.index(j)] for j in range(len(refs))]
+
+
+def crossed(blocks):
+    order = plane_order(len(blocks))
+    return [blocks[0]] + [swapped(b, "seq", j) for b, j in zip(blocks[1:], order[1:])]
 
 
 def distances(tp):
@@ -456,7 +473,9 @@
         2_000_000,
         scalars=1,
     )
-    got = [sent[0]] + [swapped(sent[j], "seq", j) for j in range(1, devices)]
+    sent, halo = lax.optimization_barrier((sent, halo))
+    got = crossed(sent)
+    halo = lax.ppermute(halo, "seq", [(i, (i + 1) % devices) for i in range(devices)])
     spread = call(
         functools.partial(spread_kernel, tp),
         "spread_rows",
@@ -468,8 +487,6 @@
         scalars=1,
     )
     near = exchanged(spread)
-    near[1], halo = lax.optimization_barrier((near[1], halo))
-    halo = lax.ppermute(halo, "seq", [(i, i + 1) for i in range(devices - 1)])
 
     blocks = spans * groups
     rows_span = per_span * NEIGHBOUR_LENGTH
@@ -498,7 +515,7 @@
         6_000_000,
         scalars=1,
     )
-    back = lax.ppermute(back, "seq", [(i + 1, i) for i in range(devices - 1)])
+    back = lax.ppermute(back, "seq", [((i + 1) % devices, i) for i in range(devices)])
     grads, self_out = lax.optimization_barrier((grads, self_out))
 
     returned = call(
@@ -512,7 +529,7 @@
         scalars=1,
     )
     returned, weights = lax.optimization_barrier((returned, weights))
-    returned = [returned[0]] + [swapped(returned[j], "seq", j) for j in range(1, devices)]
+    returned = crossed(returned)
 
     attended, query_gradient, key_gradient, value_gradient = call(
         functools.partial(join_kernel, tp),

time: 61.9 us -> 52.6 us (0.85)
  waiting for transfers between devices: 20.1 us -> 14.2 us
  starting transfers between devices: 31.1 us -> 27.7 us
    ppermute x24, waiting for transfers between devices: 20.1 us -> 14.2 us  [swapped(): lax.ppermute(block, axis, [(i, i ^ apart) for i in range(lax.axis_size(ax...]
    ppermute x24, starting transfers between devices: 28.5 us -> 26.4 us  [swapped(): lax.ppermute(block, axis, [(i, i ^ apart) for i in range(lax.axis_size(ax...]
    ppermute x2, starting transfers between devices: 2.58 us -> 1.27 us  [the longest x1 1.27 us: body(): lax.ppermute(back, 'seq', [((i + 1) % devices, i) for i in range(devices)])]
  transfers between devices with their start and end apart: 26 -> 26, of which waited for: 13 -> 14; matrix products, arithmetic and copies ran while one was open for 0% -> 0% of each run, Pallas kernels for 11% -> 14%
where the time goes in v3:
time: 52.6 us; the launch traced here: 52.4 us
  starting transfers between devices  27.7 us (53%)
  waiting for transfers between devices  14.2 us (27%)
  Pallas kernels  9.71 us (18%)
  between operations  0.75 us (1%)
    ppermute x24, starting transfers between devices, swapped(): lax.ppermute(block, axis, [(i, i ^ apart) for i in range(lax.axis_size(ax...  26.4 us
    ppermute x24, waiting for transfers between devices, swapped(): lax.ppermute(block, axis, [(i, i ^ apart) for i in range(lax.axis_size(ax...  14.2 us
    pallas_call x9, Pallas kernels, call(): pl.pallas_call(kernel, out_shape=tuple(outs), in_specs=[SMEM] * scalars +...  9.71 us
    ppermute x1, starting transfers between devices, body(): lax.ppermute(back, 'seq', [((i + 1) % devices, i) for i in range(devices)])  1.27 us
  transfers between devices with their start and end apart: 26, of which 14 were waited for; matrix products, arithmetic and copies ran while one was open for 0% of the time, Pallas kernels for 14%

profile of v3, /device:TPU:0, one launch (start us, length us, event | category | flops | bytes accessed | tf_op | source)
XLA Modules:
  0.0 52.4 jit_solution(6036401125275183267)
XLA Ops:
  0.6 0.9 %plan_requests.1 = s32[8,128]{1,0:T(8,128)S(1)} custom-call(s32[4,4]{1,0:T(4,128)} %owner_any.3, s32[4,4]{1,0:T(4,128)} %slot_any.1), custom_call_target="tpu_custom_call" | custom-call | bytes 100000 | tf_op jit(solution)/shard_map/plan_requests/pallas_call | solution.py:352
  1.6 0.5 collective-permute-start
  2.1 0.8 %collective-permute-done = s32[1,8,128]{2,1,0:T(8,128)S(1)} collective-permute-done((s32[1,8,128]{2,1,0:T(8,128)S(1)}, s32[1,8,128]{2,1,0:T(8,128)S(1)}, u32[]{:S(2)}, u32[]{:S(2)}) %collective-permute-start) | collective-permute-done | bytes 4128 | tf_op jit(solution)/shard_map/ppermute | solution.py:367
  2.9 3.8 %collective-permute-start.3 = (s32[2,8,128]{2,1,0:T(8,128)S(1)}, s32[2,8,128]{2,1,0:T(8,128)S(1)}, u32[]{:S(2)}, u32[]{:S(2)}) collective-permute-start(s32[2,8,128]{2,1,0:T(8,128)S(1)} %pad_add_fusion.refs_0_), channel_id=1, source_target_pairs={{0,24},{4,28},{8,16},{12,20},{16,8},{20,12},{24,0},{28,4},{1,25},{... | collective-permute-start | bytes 24584 | tf_op jit(solution)/shard_map/ppermute | solution.py:367
  6.7 0.5 collective-permute-start.2
  7.3 1.4 %stage_store.1 = (bf16[256,2048]{1,0:T(8,128)(2,1)S(1)}, bf16[128,512]{1,0:T(8,128)(2,1)S(1)}, bf16[128,64]{1,0:T(8,128)(2,1)S(1)}) custom-call(s32[1]{0:T(128)} %bitcast.1.me_ref.rank_ref, s32[4,4]{1,0:T(4,128)} %owner_any.3, bf16[64,4,1024]{2,1,0:T(4,128)(2,1)} %k_any.1, bf16[64,4,1024]{2,1,0:T(4,128)(2,1)} %v_any.1, bf16[256,256]{1,0:T(8,128)(2,1)} %k_ref.1, ...), custom_call_target="tpu_custom_call" | custom-call | bytes 3000000 | tf_op jit(solution)/shard_map/stage_store/pallas_call | solution.py:352
  8.7 1.7 %collective-permute-done.2.refs_2_ = s32[2,8,128]{2,1,0:T(8,128)S(1)} collective-permute-done((s32[2,8,128]{2,1,0:T(8,128)S(1)}, s32[2,8,128]{2,1,0:T(8,128)S(1)}, u32[]{:S(2)}, u32[]{:S(2)}) %collective-permute-start.2) | collective-permute-done | bytes 8224 | tf_op jit(solution)/shard_map/ppermute | solution.py:367
  10.3 0.5 collective-permute-done.1.refs_1_
  11.2 1.6 %collective-permute-start.4 = (bf16[16,2048]{1,0:T(8,128)(2,1)S(1)}, bf16[16,2048]{1,0:T(8,128)(2,1)S(1)}, u32[]{:S(2)}, u32[]{:S(2)}) collective-permute-start(bf16[16,2048]{1,0:T(8,128)(2,1)S(1)} %get-tuple-element.95), channel_id=1, source_target_pairs={{0,24},{4,28},{8,16},{12,20},{16,8},{20,12},{24,0},{28,4},{1,25},{... | collective-permute-start | bytes 196616 | tf_op jit(solution)/shard_map/ppermute | solution.py:367
  12.8 1.5 %collective-permute-start.5 = (bf16[16,2048]{1,0:T(8,128)(2,1)S(1)}, bf16[16,2048]{1,0:T(8,128)(2,1)S(1)}, u32[]{:S(2)}, u32[]{:S(2)}) collective-permute-start(bf16[16,2048]{1,0:T(8,128)(2,1)S(1)} %get-tuple-element.96), channel_id=1, source_target_pairs={{0,8},{4,12},{8,0},{12,4},{16,24},{20,28},{24,16},{28,20},{1,9},{5... | collective-permute-start | bytes 196616 | tf_op jit(solution)/shard_map/ppermute | solution.py:367
  14.3 0.5 collective-permute-start.6
  14.8 2.7 %collective-permute-start.8 = (bf16[16,2048]{1,0:T(8,128)(2,1)S(1)}, bf16[16,2048]{1,0:T(8,128)(2,1)S(1)}, u32[]{:S(2)}, u32[]{:S(2)}) collective-permute-start(bf16[16,2048]{1,0:T(8,128)(2,1)S(1)} %get-tuple-element.99), channel_id=1, source_target_pairs={{0,12},{4,8},{8,4},{12,0},{16,28},{20,24},{24,20},{28,16},{1,13},{... | collective-permute-start | bytes 196616 | tf_op jit(solution)/shard_map/ppermute | solution.py:367
  17.5 0.6 %collective-permute-start.10 = (bf16[16,2048]{1,0:T(8,128)(2,1)S(1)}, bf16[16,2048]{1,0:T(8,128)(2,1)S(1)}, u32[]{:S(2)}, u32[]{:S(2)}) collective-permute-start(bf16[16,2048]{1,0:T(8,128)(2,1)S(1)} %get-tuple-element.101), channel_id=1, source_target_pairs={{0,4},{4,0},{8,12},{12,8},{16,20},{20,16},{24,28},{28,24},{1,5},{5... | collective-permute-start | bytes 196616 | tf_op jit(solution)/shard_map/ppermute | solution.py:367
  18.1 1.8 %collective-permute-done.6.refs_3_ = bf16[16,2048]{1,0:T(8,128)(2,1)S(1)} collective-permute-done((bf16[16,2048]{1,0:T(8,128)(2,1)S(1)}, bf16[16,2048]{1,0:T(8,128)(2,1)S(1)}, u32[]{:S(2)}, u32[]{:S(2)}) %collective-permute-start.6) | collective-permute-done | bytes 65568 | tf_op jit(solution)/shard_map/ppermute | solution.py:367
  19.9 0.8 %collective-permute-done.8.refs_5_ = bf16[16,2048]{1,0:T(8,128)(2,1)S(1)} collective-permute-done((bf16[16,2048]{1,0:T(8,128)(2,1)S(1)}, bf16[16,2048]{1,0:T(8,128)(2,1)S(1)}, u32[]{:S(2)}, u32[]{:S(2)}) %collective-permute-start.8) | collective-permute-done | bytes 65568 | tf_op jit(solution)/shard_map/ppermute | solution.py:367
  20.7 0.6 %collective-permute-done.9.refs_6_ = bf16[16,2048]{1,0:T(8,128)(2,1)S(1)} collective-permute-done((bf16[16,2048]{1,0:T(8,128)(2,1)S(1)}, bf16[16,2048]{1,0:T(8,128)(2,1)S(1)}, u32[]{:S(2)}, u32[]{:S(2)}) %collective-permute-start.9) | collective-permute-done | bytes 65568 | tf_op jit(solution)/shard_map/ppermute | solution.py:367
  21.6 2.7 %collective-permute-start.11 = (bf16[64,512]{1,0:T(8,128)(2,1)S(1)}, bf16[64,512]{1,0:T(8,128)(2,1)S(1)}, u32[]{:S(2)}, u32[]{:S(2)}) collective-permute-start(bf16[64,512]{1,0:T(8,128)(2,1)S(1)} %get-tuple-element.103), channel_id=1, source_target_pairs={{0,2},{1,3},{2,0},{3,1},{4,6},{5,7},{6,4},{7,5},{8,10},{9,11},{10,... | collective-permute-start | bytes 196616 | tf_op jit(solution)/shard_map/ppermute | solution.py:367
  24.2 1.3 %collective-permute-start.12 = (bf16[64,512]{1,0:T(8,128)(2,1)S(1)}, bf16[64,512]{1,0:T(8,128)(2,1)S(1)}, u32[]{:S(2)}, u32[]{:S(2)}) collective-permute-start(bf16[64,512]{1,0:T(8,128)(2,1)S(1)} %get-tuple-element.104), channel_id=1, source_target_pairs={{0,3},{1,2},{2,1},{3,0},{4,7},{5,6},{6,5},{7,4},{8,11},{9,10},{10,... | collective-permute-start | bytes 196616 | tf_op jit(solution)/shard_map/ppermute | solution.py:367
  25.8 1.4 %collective-permute-done.11.refs_1_ = bf16[64,512]{1,0:T(8,128)(2,1)S(1)} collective-permute-done((bf16[64,512]{1,0:T(8,128)(2,1)S(1)}, bf16[64,512]{1,0:T(8,128)(2,1)S(1)}, u32[]{:S(2)}, u32[]{:S(2)}) %collective-permute-start.11) | collective-permute-done | bytes 65568 | tf_op jit(solution)/shard_map/ppermute | solution.py:367
  27.2 3.3 %collective-permute-done.12.refs_2_ = bf16[64,512]{1,0:T(8,128)(2,1)S(1)} collective-permute-done((bf16[64,512]{1,0:T(8,128)(2,1)S(1)}, bf16[64,512]{1,0:T(8,128)(2,1)S(1)}, u32[]{:S(2)}, u32[]{:S(2)}) %collective-permute-start.12) | collective-permute-done | bytes 65568 | tf_op jit(solution)/shard_map/ppermute | solution.py:367
  30.6 0.8 %cross_attention.1 = (bf16[64,512]{1,0:T(8,128)(2,1)S(1)}, bf16[64,512]{1,0:T(8,128)(2,1)S(1)}, bf16[64,512]{1,0:T(8,128)(2,1)S(1)}, bf16[64,512]{1,0:T(8,128)(2...) custom-call(bf16[256,1024]{1,0:T(8,128)(2,1)S(1)} %copy-done.2, ...), custom_call_target="tpu_custom_call" | custom-call | flops 600000000 | bytes 3000000 | tf_op jit(solution)/shard_map/cross_attention/pallas_call | solution.py:352
  31.4 2.5 %collective-permute-start.15 = (bf16[64,512]{1,0:T(8,128)(2,1)S(1)}, bf16[64,512]{1,0:T(8,128)(2,1)S(1)}, u32[]{:S(2)}, u32[]{:S(2)}) collective-permute-start(bf16[64,512]{1,0:T(8,128)(2,1)S(1)} %get-tuple-element.112), channel_id=1, source_target_pairs={{0,2},{1,3},{2,0},{3,1},{4,6},{5,7},{6,4},{7,5},{8,10},{9,11},{10,... | collective-permute-start | bytes 196616 | tf_op jit(solution)/shard_map/ppermute | solution.py:367
  33.9 0.6 %collective-permute-start.16 = (bf16[64,512]{1,0:T(8,128)(2,1)S(1)}, bf16[64,512]{1,0:T(8,128)(2,1)S(1)}, u32[]{:S(2)}, u32[]{:S(2)}) collective-permute-start(bf16[64,512]{1,0:T(8,128)(2,1)S(1)} %get-tuple-element.113), channel_id=1, source_target_pairs={{0,3},{1,2},{2,1},{3,0},{4,7},{5,6},{6,5},{7,4},{8,11},{9,10},{10,... | collective-permute-start | bytes 196616 | tf_op jit(solution)/shard_map/ppermute | solution.py:367
  34.9 2.9 %self_attention.1 = (f32[256,1024]{1,0:T(8,128)S(1)}, f32[256,1024]{1,0:T(8,128)S(1)}, f32[256,512]{1,0:T(8,128)S(1)}, bf16[128,512]{1,0:T(8,128)(2,1)S(1)}) custom-call(s32[1]{0:T(128)} %bitcast.1.me_ref.rank_ref, bf16[256,1024]{1,0:T(8,128)(2,1)S(1)} %copy-done.2, bf16[256,256]{1,0:T(8,128)(2,1)S(1)} %copy-done, bf16[256,256]{1,0:T(8,128)(2,1)S(1)} %copy-done.1, ...), custom_call_target="tpu_custom_call" | custom-call | flops 1600000000 | bytes 6000000 | tf_op jit(solution)/shard_map/self_attention/pallas_call | solution.py:352
  37.8 1.3 %collective-permute-start.25 = (bf16[128,512]{1,0:T(8,128)(2,1)S(1)}, bf16[128,512]{1,0:T(8,128)(2,1)S(1)}, u32[]{:S(2)}, u32[]{:S(2)}) collective-permute-start(bf16[128,512]{1,0:T(8,128)(2,1)S(1)} %get-tuple-element.143), channel_id=1, source_target_pairs={{4,0},{8,4},{12,8},{16,12},{20,16},{24,20},{28,24},{0,28},{5,1},{9... | collective-permute-start | bytes 393224 | tf_op jit(solution)/shard_map/ppermute | solution.py:518
  39.1 0.9 %collective-permute-done.16.refs_2_ = bf16[64,512]{1,0:T(8,128)(2,1)S(1)} collective-permute-done((bf16[64,512]{1,0:T(8,128)(2,1)S(1)}, bf16[64,512]{1,0:T(8,128)(2,1)S(1)}, u32[]{:S(2)}, u32[]{:S(2)}) %collective-permute-start.16) | collective-permute-done | bytes 65568 | tf_op jit(solution)/shard_map/ppermute | solution.py:367
  40.3 2.6 %collective-permute-start.18 = (bf16[16,2048]{1,0:T(8,128)(2,1)S(1)}, bf16[16,2048]{1,0:T(8,128)(2,1)S(1)}, u32[]{:S(2)}, u32[]{:S(2)}) collective-permute-start(bf16[16,2048]{1,0:T(8,128)(2,1)S(1)} %get-tuple-element.131), channel_id=1, source_target_pairs={{0,24},{4,28},{8,16},{12,20},{16,8},{20,12},{24,0},{28,4},{1,25},{... | collective-permute-start | bytes 196616 | tf_op jit(solution)/shard_map/ppermute | solution.py:367
  42.9 0.6 %collective-permute-start.19 = (bf16[16,2048]{1,0:T(8,128)(2,1)S(1)}, bf16[16,2048]{1,0:T(8,128)(2,1)S(1)}, u32[]{:S(2)}, u32[]{:S(2)}) collective-permute-start(bf16[16,2048]{1,0:T(8,128)(2,1)S(1)} %get-tuple-element.132), channel_id=1, source_target_pairs={{0,8},{4,12},{8,0},{12,4},{16,24},{20,28},{24,16},{28,20},{1,9},{5... | collective-permute-start | bytes 196616 | tf_op jit(solution)/shard_map/ppermute | solution.py:367
  43.9 2.8 %collective-permute-start.22 = (bf16[16,2048]{1,0:T(8,128)(2,1)S(1)}, bf16[16,2048]{1,0:T(8,128)(2,1)S(1)}, u32[]{:S(2)}, u32[]{:S(2)}) collective-permute-start(bf16[16,2048]{1,0:T(8,128)(2,1)S(1)} %get-tuple-element.135), channel_id=1, source_target_pairs={{0,12},{4,8},{8,4},{12,0},{16,28},{20,24},{24,20},{28,16},{1,13},{... | collective-permute-start | bytes 196616 | tf_op jit(solution)/shard_map/ppermute | solution.py:367
  47.3 1.6 %join_outputs.1 = (bf16[256,1024]{1,0:T(8,128)(2,1)}, bf16[256,1024]{1,0:T(8,128)(2,1)}, bf16[256,256]{1,0:T(8,128)(2,1)}, bf16[256,256]{1,0:T(8,128)(2,1)}) custom-call(bf16[8,64,256]{2,1,0:T(8,128)(2,1)S(1)} %get-tuple-element.138.w_ref, bf16[8,64,256]{2,1,0:T(8,128)(2,1)S(1)} %get-tuple-element.139.ds_ref, f32[256,1024]{1,0:T(8,128)S(1)} %get-tuple-element.140.out_ref, ...), custom_call_target="tpu_custom_call" | custom-call | flops 300000000 | bytes 5000000 | tf_op jit(solution)/shard_map/join_outputs/pallas_call | solution.py:352
  49.4 1.7 %collective-permute-done.23.refs_6_ = bf16[16,2048]{1,0:T(8,128)(2,1)S(1)} collective-permute-done((bf16[16,2048]{1,0:T(8,128)(2,1)S(1)}, bf16[16,2048]{1,0:T(8,128)(2,1)S(1)}, u32[]{:S(2)}, u32[]{:S(2)}) %collective-permute-start.23) | collective-permute-done | bytes 65568 | tf_op jit(solution)/shard_map/ppermute | solution.py:367
  51.1 1.3 %sum_store_gradients.1 = (bf16[64,4,1024]{2,1,0:T(4,128)(2,1)}, bf16[64,4,1024]{2,1,0:T(4,128)(2,1)}) custom-call(bf16[256,128]{1,0:T(8,128)(2,1)S(1)} %get-tuple-element.149.owned_ref, bf16[16,2048]{1,0:T(8,128)(2,1)S(1)} %get-tuple-element.150.refs_0_, bf16[16,2048]{1,0:T(8,128)(2,1)S(1)} %collective-permute-done.18.refs_1_, ...), custom_call_target="tpu_custom_call" | custom-call | flops 200000000 | bytes 2000000 | tf_op jit(solution)/shard_map/sum_store_gradients/pallas_call | solution.py:352
  (38 shorter events, 3.3 us)
Async XLA Ops:
  1.6 1.3 %collective-permute-start = (s32[1,8,128]{2,1,0:T(8,128)S(1)}, s32[1,8,128]{2,1,0:T(8,128)S(1)}, u32[]{:S(2)}, u32[]{:S(2)}) collective-permute-start(s32[1,8,128]{2,1,0:T(8,128)S(1)} %bitcast.3), channel_id=1, source_target_pairs={{0,4},{4,0},{8,12},{12,8},{16,20},{20,16},{24,28},{28,24},{1,5},{5... | collective-permute-start | bytes 12296 | tf_op jit(solution)/shard_map/ppermute | solution.py:367
  2.9 5.8 %collective-permute-start.3 = (s32[2,8,128]{2,1,0:T(8,128)S(1)}, s32[2,8,128]{2,1,0:T(8,128)S(1)}, u32[]{:S(2)}, u32[]{:S(2)}) collective-permute-start(s32[2,8,128]{2,1,0:T(8,128)S(1)} %pad_add_fusion.refs_0_), channel_id=1, source_target_pairs={{0,24},{4,28},{8,16},{12,20},{16,8},{20,12},{24,0},{28,4},{1,25},{... | collective-permute-start | bytes 24584 | tf_op jit(solution)/shard_map/ppermute | solution.py:367
  6.7 3.7 %collective-permute-start.2 = (s32[2,8,128]{2,1,0:T(8,128)S(1)}, s32[2,8,128]{2,1,0:T(8,128)S(1)}, u32[]{:S(2)}, u32[]{:S(2)}) collective-permute-start(s32[2,8,128]{2,1,0:T(8,128)S(1)} %pad_add_fusion.refs_0_), channel_id=1, source_target_pairs={{0,16},{4,20},{8,24},{12,28},{16,0},{20,4},{24,8},{28,12},{1,17},{... | collective-permute-start | bytes 24584 | tf_op jit(solution)/shard_map/ppermute | solution.py:367
  7.2 3.7 %collective-permute-start.1 = (s32[2,8,128]{2,1,0:T(8,128)S(1)}, s32[2,8,128]{2,1,0:T(8,128)S(1)}, u32[]{:S(2)}, u32[]{:S(2)}) collective-permute-start(s32[2,8,128]{2,1,0:T(8,128)S(1)} %pad_add_fusion.refs_0_), channel_id=1, source_target_pairs={{0,8},{4,12},{8,0},{12,4},{16,24},{20,28},{24,16},{28,20},{1,9},{5... | collective-permute-start | bytes 24584 | tf_op jit(solution)/shard_map/ppermute | solution.py:367
  10.8 19.7 %copy-start.3 = (bf16[256,1024]{1,0:T(8,128)(2,1)S(1)}, bf16[256,1024]{1,0:T(8,128)(2,1)}, u32[]{:S(2)}) copy-start(bf16[256,1024]{1,0:T(8,128)(2,1)} %do_ref.3) | copy-start | bytes 1572868
  11.2 19.4 %copy-start.2 = (bf16[256,1024]{1,0:T(8,128)(2,1)S(1)}, bf16[256,1024]{1,0:T(8,128)(2,1)}, u32[]{:S(2)}) copy-start(bf16[256,1024]{1,0:T(8,128)(2,1)} %q_ref.3) | copy-start | bytes 1572868
  11.2 6.3 %collective-permute-start.4 = (bf16[16,2048]{1,0:T(8,128)(2,1)S(1)}, bf16[16,2048]{1,0:T(8,128)(2,1)S(1)}, u32[]{:S(2)}, u32[]{:S(2)}) collective-permute-start(bf16[16,2048]{1,0:T(8,128)(2,1)S(1)} %get-tuple-element.95), channel_id=1, source_target_pairs={{0,24},{4,28},{8,16},{12,20},{16,8},{20,12},{24,0},{28,4},{1,25},{... | collective-permute-start | bytes 196616 | tf_op jit(solution)/shard_map/ppermute | solution.py:367
  12.8 4.7 %collective-permute-start.5 = (bf16[16,2048]{1,0:T(8,128)(2,1)S(1)}, bf16[16,2048]{1,0:T(8,128)(2,1)S(1)}, u32[]{:S(2)}, u32[]{:S(2)}) collective-permute-start(bf16[16,2048]{1,0:T(8,128)(2,1)S(1)} %get-tuple-element.96), channel_id=1, source_target_pairs={{0,8},{4,12},{8,0},{12,4},{16,24},{20,28},{24,16},{28,20},{1,9},{5... | collective-permute-start | bytes 196616 | tf_op jit(solution)/shard_map/ppermute | solution.py:367
  14.3 5.6 %collective-permute-start.6 = (bf16[16,2048]{1,0:T(8,128)(2,1)S(1)}, bf16[16,2048]{1,0:T(8,128)(2,1)S(1)}, u32[]{:S(2)}, u32[]{:S(2)}) collective-permute-start(bf16[16,2048]{1,0:T(8,128)(2,1)S(1)} %get-tuple-element.97), channel_id=1, source_target_pairs={{0,16},{4,20},{8,24},{12,28},{16,0},{20,4},{24,8},{28,12},{1,17},{... | collective-permute-start | bytes 196616 | tf_op jit(solution)/shard_map/ppermute | solution.py:367
  14.8 5.1 %collective-permute-start.7 = (bf16[16,2048]{1,0:T(8,128)(2,1)S(1)}, bf16[16,2048]{1,0:T(8,128)(2,1)S(1)}, u32[]{:S(2)}, u32[]{:S(2)}) collective-permute-start(bf16[16,2048]{1,0:T(8,128)(2,1)S(1)} %get-tuple-element.98), channel_id=1, source_target_pairs={{0,28},{4,24},{8,20},{12,16},{16,12},{20,8},{24,4},{28,0},{1,29},{... | collective-permute-start | bytes 196616 | tf_op jit(solution)/shard_map/ppermute | solution.py:367
  14.8 5.9 %collective-permute-start.8 = (bf16[16,2048]{1,0:T(8,128)(2,1)S(1)}, bf16[16,2048]{1,0:T(8,128)(2,1)S(1)}, u32[]{:S(2)}, u32[]{:S(2)}) collective-permute-start(bf16[16,2048]{1,0:T(8,128)(2,1)S(1)} %get-tuple-element.99), channel_id=1, source_target_pairs={{0,12},{4,8},{8,4},{12,0},{16,28},{20,24},{24,20},{28,16},{1,13},{... | collective-permute-start | bytes 196616 | tf_op jit(solution)/shard_map/ppermute | solution.py:367
  17.5 3.8 %collective-permute-start.9 = (bf16[16,2048]{1,0:T(8,128)(2,1)S(1)}, bf16[16,2048]{1,0:T(8,128)(2,1)S(1)}, u32[]{:S(2)}, u32[]{:S(2)}) collective-permute-start(bf16[16,2048]{1,0:T(8,128)(2,1)S(1)} %get-tuple-element.100), channel_id=1, source_target_pairs={{0,20},{4,16},{8,28},{12,24},{16,4},{20,0},{24,12},{28,8},{1,21},{... | collective-permute-start | bytes 196616 | tf_op jit(solution)/shard_map/ppermute | solution.py:367
  17.5 3.8 %collective-permute-start.10 = (bf16[16,2048]{1,0:T(8,128)(2,1)S(1)}, bf16[16,2048]{1,0:T(8,128)(2,1)S(1)}, u32[]{:S(2)}, u32[]{:S(2)}) collective-permute-start(bf16[16,2048]{1,0:T(8,128)(2,1)S(1)} %get-tuple-element.101), channel_id=1, source_target_pairs={{0,4},{4,0},{8,12},{12,8},{16,20},{20,16},{24,28},{28,24},{1,5},{5... | collective-permute-start | bytes 196616 | tf_op jit(solution)/shard_map/ppermute | solution.py:367
  19.9 11.4 %collective-permute-start.14 = (bf16[128,512]{1,0:T(8,128)(2,1)S(1)}, bf16[128,512]{1,0:T(8,128)(2,1)S(1)}, u32[]{:S(2)}, u32[]{:S(2)}) collective-permute-start(bf16[128,512]{1,0:T(8,128)(2,1)S(1)} %get-tuple-element.110), channel_id=1, source_target_pairs={{0,4},{4,8},{8,12},{12,16},{16,20},{20,24},{24,28},{28,0},{1,5},{5... | collective-permute-start | bytes 393224 | tf_op jit(solution)/shard_map/ppermute | solution.py:478
  21.6 5.6 %collective-permute-start.11 = (bf16[64,512]{1,0:T(8,128)(2,1)S(1)}, bf16[64,512]{1,0:T(8,128)(2,1)S(1)}, u32[]{:S(2)}, u32[]{:S(2)}) collective-permute-start(bf16[64,512]{1,0:T(8,128)(2,1)S(1)} %get-tuple-element.103), channel_id=1, source_target_pairs={{0,2},{1,3},{2,0},{3,1},{4,6},{5,7},{6,4},{7,5},{8,10},{9,11},{10,... | collective-permute-start | bytes 196616 | tf_op jit(solution)/shard_map/ppermute | solution.py:367
  24.2 6.2 %collective-permute-start.12 = (bf16[64,512]{1,0:T(8,128)(2,1)S(1)}, bf16[64,512]{1,0:T(8,128)(2,1)S(1)}, u32[]{:S(2)}, u32[]{:S(2)}) collective-permute-start(bf16[64,512]{1,0:T(8,128)(2,1)S(1)} %get-tuple-element.104), channel_id=1, source_target_pairs={{0,3},{1,2},{2,1},{3,0},{4,7},{5,6},{6,5},{7,4},{8,11},{9,10},{10,... | collective-permute-start | bytes 196616 | tf_op jit(solution)/shard_map/ppermute | solution.py:367
  25.6 5.0 %collective-permute-start.13 = (bf16[64,512]{1,0:T(8,128)(2,1)S(1)}, bf16[64,512]{1,0:T(8,128)(2,1)S(1)}, u32[]{:S(2)}, u32[]{:S(2)}) collective-permute-start(bf16[64,512]{1,0:T(8,128)(2,1)S(1)} %get-tuple-element.105), channel_id=1, source_target_pairs={{0,1},{1,0},{2,3},{3,2},{4,5},{5,4},{6,7},{7,6},{8,9},{9,8},{10,11... | collective-permute-start | bytes 196616 | tf_op jit(solution)/shard_map/ppermute | solution.py:367
  30.6 4.3 %copy-start = (bf16[256,256]{1,0:T(8,128)(2,1)S(1)}, bf16[256,256]{1,0:T(8,128)(2,1)}, u32[]{:S(2)}) copy-start(bf16[256,256]{1,0:T(8,128)(2,1)} %k_ref.1) | copy-start | bytes 393220
  30.6 4.3 %copy-start.1 = (bf16[256,256]{1,0:T(8,128)(2,1)S(1)}, bf16[256,256]{1,0:T(8,128)(2,1)}, u32[]{:S(2)}) copy-start(bf16[256,256]{1,0:T(8,128)(2,1)} %v_ref.1) | copy-start | bytes 393220
  31.4 7.7 %collective-permute-start.15 = (bf16[64,512]{1,0:T(8,128)(2,1)S(1)}, bf16[64,512]{1,0:T(8,128)(2,1)S(1)}, u32[]{:S(2)}, u32[]{:S(2)}) collective-permute-start(bf16[64,512]{1,0:T(8,128)(2,1)S(1)} %get-tuple-element.112), channel_id=1, source_target_pairs={{0,2},{1,3},{2,0},{3,1},{4,6},{5,7},{6,4},{7,5},{8,10},{9,11},{10,... | collective-permute-start | bytes 196616 | tf_op jit(solution)/shard_map/ppermute | solution.py:367
  33.9 6.1 %collective-permute-start.16 = (bf16[64,512]{1,0:T(8,128)(2,1)S(1)}, bf16[64,512]{1,0:T(8,128)(2,1)S(1)}, u32[]{:S(2)}, u32[]{:S(2)}) collective-permute-start(bf16[64,512]{1,0:T(8,128)(2,1)S(1)} %get-tuple-element.113), channel_id=1, source_target_pairs={{0,3},{1,2},{2,1},{3,0},{4,7},{5,6},{6,5},{7,4},{8,11},{9,10},{10,... | collective-permute-start | bytes 196616 | tf_op jit(solution)/shard_map/ppermute | solution.py:367
  34.5 5.5 %collective-permute-start.17 = (bf16[64,512]{1,0:T(8,128)(2,1)S(1)}, bf16[64,512]{1,0:T(8,128)(2,1)S(1)}, u32[]{:S(2)}, u32[]{:S(2)}) collective-permute-start(bf16[64,512]{1,0:T(8,128)(2,1)S(1)} %get-tuple-element.114), channel_id=1, source_target_pairs={{0,1},{1,0},{2,3},{3,2},{4,5},{5,4},{6,7},{7,6},{8,9},{9,8},{10,11... | collective-permute-start | bytes 196616 | tf_op jit(solution)/shard_map/ppermute | solution.py:367
  37.8 6.1 %collective-permute-start.25 = (bf16[128,512]{1,0:T(8,128)(2,1)S(1)}, bf16[128,512]{1,0:T(8,128)(2,1)S(1)}, u32[]{:S(2)}, u32[]{:S(2)}) collective-permute-start(bf16[128,512]{1,0:T(8,128)(2,1)S(1)} %get-tuple-element.143), channel_id=1, source_target_pairs={{4,0},{8,4},{12,8},{16,12},{20,16},{24,20},{28,24},{0,28},{5,1},{9... | collective-permute-start | bytes 393224 | tf_op jit(solution)/shard_map/ppermute | solution.py:518
  40.3 6.4 %collective-permute-start.18 = (bf16[16,2048]{1,0:T(8,128)(2,1)S(1)}, bf16[16,2048]{1,0:T(8,128)(2,1)S(1)}, u32[]{:S(2)}, u32[]{:S(2)}) collective-permute-start(bf16[16,2048]{1,0:T(8,128)(2,1)S(1)} %get-tuple-element.131), channel_id=1, source_target_pairs={{0,24},{4,28},{8,16},{12,20},{16,8},{20,12},{24,0},{28,4},{1,25},{... | collective-permute-start | bytes 196616 | tf_op jit(solution)/shard_map/ppermute | solution.py:367
  42.9 4.3 %collective-permute-start.19 = (bf16[16,2048]{1,0:T(8,128)(2,1)S(1)}, bf16[16,2048]{1,0:T(8,128)(2,1)S(1)}, u32[]{:S(2)}, u32[]{:S(2)}) collective-permute-start(bf16[16,2048]{1,0:T(8,128)(2,1)S(1)} %get-tuple-element.132), channel_id=1, source_target_pairs={{0,8},{4,12},{8,0},{12,4},{16,24},{20,28},{24,16},{28,20},{1,9},{5... | collective-permute-start | bytes 196616 | tf_op jit(solution)/shard_map/ppermute | solution.py:367
  43.5 5.4 %collective-permute-start.20 = (bf16[16,2048]{1,0:T(8,128)(2,1)S(1)}, bf16[16,2048]{1,0:T(8,128)(2,1)S(1)}, u32[]{:S(2)}, u32[]{:S(2)}) collective-permute-start(bf16[16,2048]{1,0:T(8,128)(2,1)S(1)} %get-tuple-element.133), channel_id=1, source_target_pairs={{0,16},{4,20},{8,24},{12,28},{16,0},{20,4},{24,8},{28,12},{1,17},{... | collective-permute-start | bytes 196616 | tf_op jit(solution)/shard_map/ppermute | solution.py:367
  43.9 5.2 %collective-permute-start.21 = (bf16[16,2048]{1,0:T(8,128)(2,1)S(1)}, bf16[16,2048]{1,0:T(8,128)(2,1)S(1)}, u32[]{:S(2)}, u32[]{:S(2)}) collective-permute-start(bf16[16,2048]{1,0:T(8,128)(2,1)S(1)} %get-tuple-element.134), channel_id=1, source_target_pairs={{0,28},{4,24},{8,20},{12,16},{16,12},{20,8},{24,4},{28,0},{1,29},{... | collective-permute-start | bytes 196616 | tf_op jit(solution)/shard_map/ppermute | solution.py:367
  43.9 5.4 %collective-permute-start.22 = (bf16[16,2048]{1,0:T(8,128)(2,1)S(1)}, bf16[16,2048]{1,0:T(8,128)(2,1)S(1)}, u32[]{:S(2)}, u32[]{:S(2)}) collective-permute-start(bf16[16,2048]{1,0:T(8,128)(2,1)S(1)} %get-tuple-element.135), channel_id=1, source_target_pairs={{0,12},{4,8},{8,4},{12,0},{16,28},{20,24},{24,20},{28,16},{1,13},{... | collective-permute-start | bytes 196616 | tf_op jit(solution)/shard_map/ppermute | solution.py:367
  46.7 4.4 %collective-permute-start.23 = (bf16[16,2048]{1,0:T(8,128)(2,1)S(1)}, bf16[16,2048]{1,0:T(8,128)(2,1)S(1)}, u32[]{:S(2)}, u32[]{:S(2)}) collective-permute-start(bf16[16,2048]{1,0:T(8,128)(2,1)S(1)} %get-tuple-element.136), channel_id=1, source_target_pairs={{0,20},{4,16},{8,28},{12,24},{16,4},{20,0},{24,12},{28,8},{1,21},{... | collective-permute-start | bytes 196616 | tf_op jit(solution)/shard_map/ppermute | solution.py:367
  47.1 4.0 %collective-permute-start.24 = (bf16[16,2048]{1,0:T(8,128)(2,1)S(1)}, bf16[16,2048]{1,0:T(8,128)(2,1)S(1)}, u32[]{:S(2)}, u32[]{:S(2)}) collective-permute-start(bf16[16,2048]{1,0:T(8,128)(2,1)S(1)} %get-tuple-element.137), channel_id=1, source_target_pairs={{0,4},{4,0},{8,12},{12,8},{16,20},{20,16},{24,28},{28,24},{1,5},{5... | collective-permute-start | bytes 196616 | tf_op jit(solution)/shard_map/ppermute | solution.py:367

commit v4 on v3

--- a/solution.py
+++ b/solution.py
@@ -100,11 +100,14 @@
     rows_each,
     chunks,
     me_ref,
+    z_ref,
+    sibling_k_ref,
+    sibling_v_ref,
     owner_any,
+    sk_any,
+    sv_any,
     k_any,
     v_any,
-    sk_any,
-    sv_any,
     store_ref,
     halo_ref,
     placed_ref,
@@ -113,23 +116,22 @@
     v_ref,
     sems,
 ):
-    slots, tokens, features = k_ref.shape
+    store_refs = (k_ref, v_ref, sibling_k_ref, sibling_v_ref)
+    slots, tokens, features = store_refs[0].shape
     kv_width = sk_any.shape[1]
     window = halo_ref.shape[0]
     tail = slice(sk_any.shape[0] - window, sk_any.shape[0])
     step = slots // chunks
-    fetch_owner = pltpu.make_async_copy(owner_any, owner_ref, sems.at[2 * chunks + 2])
+    fetch_owner = pltpu.make_async_copy(owner_any, owner_ref, sems.at[0])
     fetch_owner.start()
+    left, right = slice(0, kv_width), slice(kv_width, 2 * kv_width)
     copies = []
     for i in range(chunks):
         part = slice(i * step, (i + 1) * step)
-        copies.append(pltpu.make_async_copy(k_any.at[part], k_ref.at[part], sems.at[2 * i]))
-        copies.append(pltpu.make_async_copy(v_any.at[part], v_ref.at[part], sems.at[2 * i + 1]))
-    left, right = slice(0, kv_width), slice(kv_width, 2 * kv_width)
-    copies.append(pltpu.make_async_copy(sk_any.at[tail], halo_ref.at[:, left], sems.at[2 * chunks]))
-    copies.append(
-        pltpu.make_async_copy(sv_any.at[tail], halo_ref.at[:, right], sems.at[2 * chunks + 1])
-    )
+        copies.append(pltpu.make_async_copy(k_any.at[part], k_ref.at[part], sems.at[3 + 2 * i]))
+        copies.append(pltpu.make_async_copy(v_any.at[part], v_ref.at[part], sems.at[4 + 2 * i]))
+    copies.append(pltpu.make_async_copy(sk_any.at[tail], halo_ref.at[:, left], sems.at[1]))
+    copies.append(pltpu.make_async_copy(sv_any.at[tail], halo_ref.at[:, right], sems.at[2]))
     for copy in copies:
         copy.start()
     fetch_owner.wait()
@@ -142,53 +144,63 @@
     row = lax.broadcasted_iota(jnp.int32, (lanes, used), 0)
     placed_ref[...] = jnp.where(row == place, 1.0, 0.0).astype(BF16)
     for i in range(chunks):
+        part = slice(i * step, (i + 1) * step)
         copies[2 * i].wait()
         copies[2 * i + 1].wait()
-        part = slice(i * step, (i + 1) * step)
-        rows = slice(i * step * tokens, (i + 1) * step * tokens)
-        for z in range(features // kv_width):
-            cols = slice(z * kv_width, (z + 1) * kv_width)
-            at = 2 * z * kv_width
-            for ref in (k_ref, v_ref):
-                store_ref[rows, at : at + kv_width] = ref[part, :, cols].reshape(
-                    step * tokens, kv_width
-                )
-                at += kv_width
+        for j in range(4):
+            core, kind = j // 2, j % 2
+            first = (core * slots + i * step) * tokens
+            rows = slice(first, first + step * tokens)
+            for d, apart in enumerate(farthest_first(features // kv_width)):
+                start = pl.multiple_of((z_ref[0] ^ apart) * kv_width, kv_width)
+                at = (2 * d + kind) * kv_width
+                store_ref[rows, at : at + kv_width] = store_refs[j][
+                    part, :, pl.ds(start, kv_width)
+                ].reshape(step * tokens, kv_width)
     for copy in copies[2 * chunks :]:
         copy.wait()
 
 
-def pack_kernel(pieces, me_ref, store_ref, *refs):
-    wanted_refs, send_refs, owned_ref = refs[:pieces], refs[pieces:-1], refs[-1]
-    rows_each = send_refs[0].shape[0]
-    rows, lanes = owned_ref.shape
+def pack_kernel(rows_each, me_ref, store_ref, *refs):
+    pieces = len(refs) // 3
+    wanted_refs, far_refs, near_refs, target_ref = (
+        refs[:pieces],
+        by_chip(refs[pieces : 2 * pieces]),
+        by_chip(refs[2 * pieces : 3 * pieces]),
+        refs[-1],
+    )
+    rows, columns = store_ref.shape[0], store_ref.shape[1] // 2
+    lanes = target_ref.shape[1]
+    width = wanted_refs[0].shape[1]
     me = me_ref[0]
-    width = wanted_refs[0].shape[2]
     lane = lax.broadcasted_iota(jnp.int32, (1, width), 1)
     parts = [jnp.full((1, width), -1, jnp.int32) for _ in range(lanes // width)]
-    entries = [(ref, i) for ref in wanted_refs for i in range(ref.shape[0])]
-    for apart, (wanted_ref, i) in enumerate(entries):
-        part, at = divmod(apart * rows_each, width)
-        from_there = wanted_ref[i, pl.ds(me, 1), :]
-        here = (lane >= at) & (lane < at + rows_each)
-        parts[part] = jnp.where(here, from_there, parts[part])
+    for m, wanted_ref in enumerate(by_chip(wanted_refs)):
+        for core in range(2):
+            part, at = divmod((2 * m + core) * rows_each, width)
+            from_there = wanted_ref[pl.ds(me ^ core, 1), :]
+            here = (lane >= at) & (lane < at + rows_each)
+            parts[part] = jnp.where(here, from_there, parts[part])
     target = jnp.concatenate(parts, axis=1)
+    target_ref[...] = target
+    second = (lax.broadcasted_iota(jnp.int32, (1, lanes), 1) // rows_each) % 2
+    target = jnp.where(target >= 0, target + second * (rows // 2), -1)
     row = lax.broadcasted_iota(jnp.int32, (rows, lanes), 0)
-    owned = jnp.where(row == target, 1.0, 0.0).astype(BF16)
-    owned_ref[...] = owned
-    picked = dot_tn(owned, store_ref[...]).astype(BF16)
-    for at, send_ref in enumerate(by_distance(send_refs)):
-        send_ref[...] = picked[at * rows_each : (at + 1) * rows_each]
-
-
-def spread_kernel(tp, z_ref, placed_ref, *refs):
-    got_refs, send_refs, near_ref = refs[: -tp - 1], refs[-tp - 1 : -1], refs[-1]
-    both = send_refs[0].shape[1]
-    got = jnp.concatenate([ref[...] for ref in by_distance(got_refs)], axis=0)
-    near_ref[...] = dot_tn(placed_ref[...], got).astype(BF16)
-    for apart, send_ref in zip(distances(tp), send_refs):
-        start = pl.multiple_of((z_ref[0] ^ apart) * both, both)
-        send_ref[...] = near_ref[:, pl.ds(start, both)]
+    picks = jnp.where(row == target, 1.0, 0.0).astype(BF16)
+    for half, send_refs in enumerate((far_refs, near_refs)):
+        cols = slice(half * columns, (half + 1) * columns)
+        picked = dot_tn(picks, store_ref[:, cols]).astype(BF16)
+        for m, send_ref in enumerate(send_refs):
+            send_ref[...] = picked[2 * m * rows_each : 2 * (m + 1) * rows_each]
+
+
+def spread_kernel(parts, placed_ref, *refs):
+    got_refs, send_refs = refs[: -parts], refs[-parts :]
+    width = send_refs[0].shape[1]
+    got = jnp.concatenate([ref[...] for ref in by_chip(got_refs)], axis=0)
+    rows = dot_tn(placed_ref[...], got).astype(BF16)
+    for i, send_ref in enumerate(send_refs):
+        send_ref[...] = rows[:, i * width : (i + 1) * width]
 
 
 def scatter_kernel(tp, z_ref, placed_ref, *refs):
@@ -319,17 +331,22 @@
     ).astype(BF16)
 
 
-def sum_kernel(chunks, owned_ref, *refs):
+def sum_kernel(chunks, target_ref, other_ref, *refs):
     got_refs, (kg_any, vg_any, kg_ref, vg_ref, sems) = refs[:-5], refs[-5:]
     slots, tokens, features = kg_ref.shape
     tp = NEIGHBOUR_LENGTH // tokens
     width = features // tp
     got = jnp.concatenate([ref[...] for ref in by_distance(got_refs)], axis=0)
+    lanes = target_ref.shape[1]
+    odd = (lax.broadcasted_iota(jnp.int32, (1, lanes), 1) // got_refs[0].shape[0]) % 2
+    target = jnp.where(odd == 0, target_ref[...], other_ref[...])
+    row = lax.broadcasted_iota(jnp.int32, (slots * tokens, lanes), 0)
+    owned = jnp.where(row == target, 1.0, 0.0).astype(BF16)
     step = slots // chunks
     copies = []
     for i in range(chunks):
         part = slice(i * step, (i + 1) * step)
-        total = dot_nn(owned_ref[i * step * tokens : (i + 1) * step * tokens], got).astype(BF16)
+        total = dot_nn(owned[i * step * tokens : (i + 1) * step * tokens], got).astype(BF16)
         for z in range(tp):
             cols = slice(z * width, (z + 1) * width)
             at = 2 * z * width
@@ -382,6 +399,24 @@
 def crossed(blocks):
     order = plane_order(len(blocks))
     return [blocks[0]] + [swapped(b, "seq", j) for b, j in zip(blocks[1:], order[1:])]
+
+
+def chip_order(chips):
+    return [0] + sorted(range(1, chips), key=lambda m: (-bin(m).count("1"), m))
+
+
+def by_chip(refs):
+    order = chip_order(len(refs))
+    return [refs[order.index(m)] for m in range(len(refs))]
+
+
+def between_chips(blocks):
+    order = chip_order(len(blocks))
+    return [blocks[0]] + [swapped(b, "seq", 2 * m) for b, m in zip(blocks[1:], order[1:])]
+
+
+def farthest_first(tp):
+    return distances(tp)[1:] + [0]
 
 
 def distances(tp):
@@ -423,6 +458,8 @@
     rank = lax.axis_index("seq").astype(int32).reshape(1)
     z_rank = lax.axis_index("tp").astype(int32).reshape(1)
 
+    sibling_keys = swapped(enc_keys, "seq", 1)
+    sibling_values = swapped(encoded_values, "seq", 1)
     (want,) = call(
         functools.partial(plan_kernel, tokens, cap),
         "plan_requests",
@@ -437,56 +474,53 @@
         ],
         fetched=2,
     )
-    known, step = want[None], 1
-    while devices // step > 4:
-        known = jnp.concatenate([known, swapped(known, "seq", step)], axis=0)
-        step *= 2
-    pieces = [known] + [swapped(known, "seq", far) for far in range(step, devices, step)]
+    chips = devices // 2
+    order = chip_order(chips)
+    pieces = [want] + [swapped(want, "seq", 2 * m) for m in order[1:]]
 
     chunks = 4
+    features = enc_keys.shape[2]
     store, halo, placed = call(
         functools.partial(stage_kernel, rows_each, chunks),
         "stage_store",
-        (rank, nbr_owner, enc_keys, encoded_values, sequence_keys, sequence_values),
+        (rank, z_rank, sibling_keys, sibling_values, nbr_owner, sequence_keys, sequence_values)
+        + (enc_keys, encoded_values),
         (
-            struct((store_rows, 2 * enc_keys.shape[2]), BF16),
+            struct((2 * store_rows, 2 * features), BF16),
             struct((window, both), BF16),
             struct((lanes, used), BF16),
         ),
         0,
-        3_000_000,
-        scratch=[
-            pltpu.SMEM(nbr_owner.shape, int32),
-            pltpu.VMEM(enc_keys.shape, BF16),
-            pltpu.VMEM(encoded_values.shape, BF16),
-            pltpu.SemaphoreType.DMA((2 * chunks + 3,)),
-        ],
-        scalars=1,
+        5_000_000,
+        scratch=[pltpu.SMEM(nbr_owner.shape, int32)]
+        + [pltpu.VMEM(enc_keys.shape, BF16)] * 2
+        + [pltpu.SemaphoreType.DMA((3 + 2 * chunks,))],
+        scalars=2,
         fetched=5,
     )
-    *sent, owned = call(
-        functools.partial(pack_kernel, len(pieces)),
+    halo = lax.ppermute(halo, "seq", [(i, (i + 1) % devices) for i in range(devices)])
+    block = struct((2 * rows_each, features), BF16)
+    *sent, target = call(
+        functools.partial(pack_kernel, rows_each),
         "pack_requests",
         (rank, store, *pieces),
-        [struct((rows_each, tp * both), BF16)] * devices + [struct((store_rows, lanes), BF16)],
+        [block] * (2 * chips) + [struct((1, lanes), int32)],
         200_000_000,
         2_000_000,
         scalars=1,
     )
-    sent, halo = lax.optimization_barrier((sent, halo))
-    got = crossed(sent)
-    halo = lax.ppermute(halo, "seq", [(i, (i + 1) % devices) for i in range(devices)])
-    spread = call(
-        functools.partial(spread_kernel, tp),
-        "spread_rows",
-        (z_rank, placed, *got),
-        [struct((used, both), BF16)] * tp,
-        50_000_000,
-        1_000_000,
-        scratch=[pltpu.VMEM((used, tp * both), BF16)],
-        scalars=1,
-    )
-    near = exchanged(spread)
+    parts = tp // 2
+    moved = []
+    for name, blocks in (("spread_far", sent[:chips]), ("spread_near", sent[chips:])):
+        moved += call(
+            functools.partial(spread_kernel, parts),
+            name,
+            (placed, *between_chips(blocks)),
+            [struct((used, both), BF16)] * parts,
+            1_000_000,
+            10_000,
+        )
+    near = exchanged(moved[-1:] + moved[:-1])
 
     blocks = spans * groups
     rows_span = per_span * NEIGHBOUR_LENGTH
@@ -499,7 +533,7 @@
         600_000_000,
         3_000_000,
     )
-    grads, halo = lax.optimization_barrier((grads, halo))
+    grads, halo, target = lax.optimization_barrier((grads, halo, target))
     grads = exchanged(grads)
     self_out, self_dq, self_dkv, back = call(
         self_kernel,
@@ -516,6 +550,7 @@
         scalars=1,
     )
     back = lax.ppermute(back, "seq", [((i + 1) % devices, i) for i in range(devices)])
+    other_target = swapped(target, "seq", 1)
     grads, self_out = lax.optimization_barrier((grads, self_out))
 
     returned = call(
@@ -548,7 +583,7 @@
     store_kgrad, store_vgrad = call(
         functools.partial(sum_kernel, chunks),
         "sum_store_gradients",
-        (owned, *returned),
+        (target, other_target, *returned),
         (struct(enc_keys.shape, BF16), struct(encoded_values.shape, BF16)),
         200_000_000,
         2_000_000,

time: 52.6 us -> 50.3 us (0.956)
  waiting for transfers between devices: 14.2 us -> 12.8 us
  starting transfers between devices: 27.7 us -> 26.4 us
    ppermute x24 -> x25, waiting for transfers between devices: 14.2 us -> 12.8 us  [swapped(): lax.ppermute(block, axis, [(i, i ^ apart) for i in range(lax.axis_size(ax...]
    ppermute x24 -> x25, starting transfers between devices: 26.4 us -> 25.4 us  [swapped(): lax.ppermute(block, axis, [(i, i ^ apart) for i in range(lax.axis_size(ax...]
    pallas_call x9 -> x10, Pallas kernels: 9.71 us -> 10.1 us  [call(): pl.pallas_call(kernel, out_shape=tuple(outs), in_specs=[SMEM] * scalars +...]
  transfers between devices with their start and end apart: 26 -> 27, of which waited for: 14 -> 12; matrix products, arithmetic and copies ran while one was open for 0% -> 0% of each run, Pallas kernels for 14% -> 17%
where the time goes in v4:
time: 50.3 us; the launch traced here: 50.1 us
  starting transfers between devices  26.4 us (52%)
  waiting for transfers between devices  12.8 us (25%)
  Pallas kernels  10.1 us (20%)
  between operations  0.76 us (2%)
    ppermute x25, starting transfers between devices, swapped(): lax.ppermute(block, axis, [(i, i ^ apart) for i in range(lax.axis_size(ax...  25.4 us
    ppermute x25, waiting for transfers between devices, swapped(): lax.ppermute(block, axis, [(i, i ^ apart) for i in range(lax.axis_size(ax...  12.8 us
    pallas_call x10, Pallas kernels, call(): pl.pallas_call(kernel, out_shape=tuple(outs), in_specs=[SMEM] * scalars +...  10.1 us
  transfers between devices with their start and end apart: 27, of which 12 were waited for; matrix products, arithmetic and copies ran while one was open for 0% of the time, Pallas kernels for 17%

profile of v4, /device:TPU:0, one launch (start us, length us, event | category | flops | bytes accessed | tf_op | source)
XLA Modules:
  0.0 50.1 jit_solution(2628448947147189031)
XLA Ops:
  0.6 0.5 %collective-permute-start = (bf16[64,4,1024]{2,1,0:T(4,128)(2,1)}, bf16[64,4,1024]{2,1,0:T(4,128)(2,1)S(1)}, u32[]{:S(2)}, u32[]{:S(2)}) collective-permute-start(bf16[64,4,1024]{2,1,0:T(4,128)(2,1)} %k_any.1), channel_id=1, source_target_pairs={{0,4},{4,0},{8,12},{12,8},{16,20},{20,16},{24,28},{28,24},{1,5},{5... | collective-permute-start | bytes 1572872 | tf_op jit(solution)/shard_map/ppermute | solution.py:384
  1.2 0.9 %plan_requests.1.refs_0_ = s32[8,128]{1,0:T(8,128)S(1)} custom-call(s32[4,4]{1,0:T(4,128)} %owner_any.3, s32[4,4]{1,0:T(4,128)} %slot_any.1), custom_call_target="tpu_custom_call" | custom-call | bytes 100000 | tf_op jit(solution)/shard_map/plan_requests/pallas_call | solution.py:369
  2.2 3.9 %collective-permute-start.2 = (s32[8,128]{1,0:T(8,128)S(1)}, s32[8,128]{1,0:T(8,128)S(1)}, u32[]{:S(2)}, u32[]{:S(2)}) collective-permute-start(s32[8,128]{1,0:T(8,128)S(1)} %plan_requests.1.refs_0_), channel_id=1, source_target_pairs={{0,24},{4,28},{8,16},{12,20},{16,8},{20,12},{24,0},{28,4},{1,25},{... | collective-permute-start | bytes 12296 | tf_op jit(solution)/shard_map/ppermute | solution.py:384
  6.1 0.5 %collective-permute-start.3 = (s32[8,128]{1,0:T(8,128)S(1)}, s32[8,128]{1,0:T(8,128)S(1)}, u32[]{:S(2)}, u32[]{:S(2)}) collective-permute-start(s32[8,128]{1,0:T(8,128)S(1)} %plan_requests.1.refs_0_), channel_id=1, source_target_pairs={{0,8},{4,12},{8,0},{12,4},{16,24},{20,28},{24,16},{28,20},{1,9},{5... | collective-permute-start | bytes 12296 | tf_op jit(solution)/shard_map/ppermute | solution.py:384
  6.8 1.5 %stage_store.1 = (bf16[512,2048]{1,0:T(8,128)(2,1)S(1)}, bf16[128,512]{1,0:T(8,128)(2,1)S(1)}, bf16[128,64]{1,0:T(8,128)(2,1)S(1)}) custom-call(s32[1]{0:T(128)} %bitcast.1.me_ref.rank_ref, s32[1]{0:T(128)} %bitcast.z_ref, bf16[64,4,1024]{2,1,0:T(4,128)(2,1)S(1)} %collective-permute-done.sibling_k_ref, ...), custom_call_target="tpu_custom_call" | custom-call | bytes 5000000 | tf_op jit(solution)/shard_map/stage_store/pallas_call | solution.py:369
  8.3 1.4 %collective-permute-done.3.refs_2_ = s32[8,128]{1,0:T(8,128)S(1)} collective-permute-done((s32[8,128]{1,0:T(8,128)S(1)}, s32[8,128]{1,0:T(8,128)S(1)}, u32[]{:S(2)}, u32[]{:S(2)}) %collective-permute-start.3) | collective-permute-done | bytes 4128 | tf_op jit(solution)/shard_map/ppermute | solution.py:384
  9.7 0.5 %collective-permute-done.4.refs_3_ = s32[8,128]{1,0:T(8,128)S(1)} collective-permute-done((s32[8,128]{1,0:T(8,128)S(1)}, s32[8,128]{1,0:T(8,128)S(1)}, u32[]{:S(2)}, u32[]{:S(2)}) %collective-permute-start.4) | collective-permute-done | bytes 4128 | tf_op jit(solution)/shard_map/ppermute | solution.py:384
  10.7 1.5 %collective-permute-start.8 = (bf16[32,1024]{1,0:T(8,128)(2,1)S(1)}, bf16[32,1024]{1,0:T(8,128)(2,1)S(1)}, u32[]{:S(2)}, u32[]{:S(2)}) collective-permute-start(bf16[32,1024]{1,0:T(8,128)(2,1)S(1)} %get-tuple-element.83), channel_id=1, source_target_pairs={{0,24},{4,28},{8,16},{12,20},{16,8},{20,12},{24,0},{28,4},{1,25},{... | collective-permute-start | bytes 196616 | tf_op jit(solution)/shard_map/ppermute | solution.py:384
  12.4 1.9 %collective-permute-start.10 = (bf16[32,1024]{1,0:T(8,128)(2,1)S(1)}, bf16[32,1024]{1,0:T(8,128)(2,1)S(1)}, u32[]{:S(2)}, u32[]{:S(2)}) collective-permute-start(bf16[32,1024]{1,0:T(8,128)(2,1)S(1)} %get-tuple-element.85), channel_id=1, source_target_pairs={{0,16},{4,20},{8,24},{12,28},{16,0},{20,4},{24,8},{28,12},{1,17},{... | collective-permute-start | bytes 196616 | tf_op jit(solution)/shard_map/ppermute | solution.py:384
  14.3 1.4 %collective-permute-start.5 = (bf16[32,1024]{1,0:T(8,128)(2,1)S(1)}, bf16[32,1024]{1,0:T(8,128)(2,1)S(1)}, u32[]{:S(2)}, u32[]{:S(2)}) collective-permute-start(bf16[32,1024]{1,0:T(8,128)(2,1)S(1)} %get-tuple-element.78), channel_id=1, source_target_pairs={{0,24},{4,28},{8,16},{12,20},{16,8},{20,12},{24,0},{28,4},{1,25},{... | collective-permute-start | bytes 196616 | tf_op jit(solution)/shard_map/ppermute | solution.py:384
  15.9 0.8 %collective-permute-done.8.refs_1_ = bf16[32,1024]{1,0:T(8,128)(2,1)S(1)} collective-permute-done((bf16[32,1024]{1,0:T(8,128)(2,1)S(1)}, bf16[32,1024]{1,0:T(8,128)(2,1)S(1)}, u32[]{:S(2)}, u32[]{:S(2)}) %collective-permute-start.8) | collective-permute-done | bytes 65568 | tf_op jit(solution)/shard_map/ppermute | solution.py:384
  16.7 1.1 %collective-permute-start.7 = (bf16[32,1024]{1,0:T(8,128)(2,1)S(1)}, bf16[32,1024]{1,0:T(8,128)(2,1)S(1)}, u32[]{:S(2)}, u32[]{:S(2)}) collective-permute-start(bf16[32,1024]{1,0:T(8,128)(2,1)S(1)} %get-tuple-element.80), channel_id=1, source_target_pairs={{0,16},{4,20},{8,24},{12,28},{16,0},{20,4},{24,8},{28,12},{1,17},{... | collective-permute-start | bytes 196616 | tf_op jit(solution)/shard_map/ppermute | solution.py:384
  18.3 2.7 %collective-permute-start.11 = (bf16[64,512]{1,0:T(8,128)(2,1)S(1)}, bf16[64,512]{1,0:T(8,128)(2,1)S(1)}, u32[]{:S(2)}, u32[]{:S(2)}) collective-permute-start(bf16[64,512]{1,0:T(8,128)(2,1)S(1)} %get-tuple-element.86), channel_id=1, source_target_pairs={{0,2},{1,3},{2,0},{3,1},{4,6},{5,7},{6,4},{7,5},{8,10},{9,11},{10,... | collective-permute-start | bytes 196616 | tf_op jit(solution)/shard_map/ppermute | solution.py:384
  20.9 2.1 %collective-permute-start.12 = (bf16[64,512]{1,0:T(8,128)(2,1)S(1)}, bf16[64,512]{1,0:T(8,128)(2,1)S(1)}, u32[]{:S(2)}, u32[]{:S(2)}) collective-permute-start(bf16[64,512]{1,0:T(8,128)(2,1)S(1)} %get-tuple-element.87), channel_id=1, source_target_pairs={{0,3},{1,2},{2,1},{3,0},{4,7},{5,6},{6,5},{7,4},{8,11},{9,10},{10,... | collective-permute-start | bytes 196616 | tf_op jit(solution)/shard_map/ppermute | solution.py:384
  23.4 0.5 %collective-permute-done.11.refs_1_ = bf16[64,512]{1,0:T(8,128)(2,1)S(1)} collective-permute-done((bf16[64,512]{1,0:T(8,128)(2,1)S(1)}, bf16[64,512]{1,0:T(8,128)(2,1)S(1)}, u32[]{:S(2)}, u32[]{:S(2)}) %collective-permute-start.11) | collective-permute-done | bytes 65568 | tf_op jit(solution)/shard_map/ppermute | solution.py:384
  23.9 3.9 %collective-permute-done.12.refs_2_ = bf16[64,512]{1,0:T(8,128)(2,1)S(1)} collective-permute-done((bf16[64,512]{1,0:T(8,128)(2,1)S(1)}, bf16[64,512]{1,0:T(8,128)(2,1)S(1)}, u32[]{:S(2)}, u32[]{:S(2)}) %collective-permute-start.12) | collective-permute-done | bytes 65568 | tf_op jit(solution)/shard_map/ppermute | solution.py:384
  27.8 1.0 %collective-permute-done.13.refs_3_ = bf16[64,512]{1,0:T(8,128)(2,1)S(1)} collective-permute-done((bf16[64,512]{1,0:T(8,128)(2,1)S(1)}, bf16[64,512]{1,0:T(8,128)(2,1)S(1)}, u32[]{:S(2)}, u32[]{:S(2)}) %collective-permute-start.13) | collective-permute-done | bytes 65568 | tf_op jit(solution)/shard_map/ppermute | solution.py:384
  28.8 0.8 %cross_attention.1 = (bf16[64,512]{1,0:T(8,128)(2,1)S(1)}, bf16[64,512]{1,0:T(8,128)(2,1)S(1)}, bf16[64,512]{1,0:T(8,128)(2,1)S(1)}, bf16[64,512]{1,0:T(8,128)(2...) custom-call(bf16[256,1024]{1,0:T(8,128)(2,1)S(1)} %copy-done.2, ...), custom_call_target="tpu_custom_call" | custom-call | flops 600000000 | bytes 3000000 | tf_op jit(solution)/shard_map/cross_attention/pallas_call | solution.py:369
  29.6 2.3 %collective-permute-start.15 = (bf16[64,512]{1,0:T(8,128)(2,1)S(1)}, bf16[64,512]{1,0:T(8,128)(2,1)S(1)}, u32[]{:S(2)}, u32[]{:S(2)}) collective-permute-start(bf16[64,512]{1,0:T(8,128)(2,1)S(1)} %get-tuple-element.96), channel_id=1, source_target_pairs={{0,2},{1,3},{2,0},{3,1},{4,6},{5,7},{6,4},{7,5},{8,10},{9,11},{10,... | collective-permute-start | bytes 196616 | tf_op jit(solution)/shard_map/ppermute | solution.py:384
  31.9 1.0 %collective-permute-start.16 = (bf16[64,512]{1,0:T(8,128)(2,1)S(1)}, bf16[64,512]{1,0:T(8,128)(2,1)S(1)}, u32[]{:S(2)}, u32[]{:S(2)}) collective-permute-start(bf16[64,512]{1,0:T(8,128)(2,1)S(1)} %get-tuple-element.97), channel_id=1, source_target_pairs={{0,3},{1,2},{2,1},{3,0},{4,7},{5,6},{6,5},{7,4},{8,11},{9,10},{10,... | collective-permute-start | bytes 196616 | tf_op jit(solution)/shard_map/ppermute | solution.py:384
  33.3 2.9 %self_attention.1 = (f32[256,1024]{1,0:T(8,128)S(1)}, f32[256,1024]{1,0:T(8,128)S(1)}, f32[256,512]{1,0:T(8,128)S(1)}, bf16[128,512]{1,0:T(8,128)(2,1)S(1)}) custom-call(s32[1]{0:T(128)} %bitcast.1.me_ref.rank_ref, bf16[256,1024]{1,0:T(8,128)(2,1)S(1)} %copy-done.2, bf16[256,256]{1,0:T(8,128)(2,1)S(1)} %copy-done, bf16[256,256]{1,0:T(8,128)(2,1)S(1)} %copy-done.1, ...), custom_call_target="tpu_custom_call" | custom-call | flops 1600000000 | bytes 6000000 | tf_op jit(solution)/shard_map/self_attention/pallas_call | solution.py:369
  36.2 0.9 %collective-permute-start.25 = (bf16[128,512]{1,0:T(8,128)(2,1)S(1)}, bf16[128,512]{1,0:T(8,128)(2,1)S(1)}, u32[]{:S(2)}, u32[]{:S(2)}) collective-permute-start(bf16[128,512]{1,0:T(8,128)(2,1)S(1)} %get-tuple-element.127), channel_id=1, source_target_pairs={{4,0},{8,4},{12,8},{16,12},{20,16},{24,20},{28,24},{0,28},{5,1},{9... | collective-permute-start | bytes 393224 | tf_op jit(solution)/shard_map/ppermute | solution.py:552
  37.2 1.1 %collective-permute-done.16.refs_2_ = bf16[64,512]{1,0:T(8,128)(2,1)S(1)} collective-permute-done((bf16[64,512]{1,0:T(8,128)(2,1)S(1)}, bf16[64,512]{1,0:T(8,128)(2,1)S(1)}, u32[]{:S(2)}, u32[]{:S(2)}) %collective-permute-start.16) | collective-permute-done | bytes 65568 | tf_op jit(solution)/shard_map/ppermute | solution.py:384
  38.9 1.8 %collective-permute-start.18 = (bf16[16,2048]{1,0:T(8,128)(2,1)S(1)}, bf16[16,2048]{1,0:T(8,128)(2,1)S(1)}, u32[]{:S(2)}, u32[]{:S(2)}) collective-permute-start(bf16[16,2048]{1,0:T(8,128)(2,1)S(1)} %get-tuple-element.115), channel_id=1, source_target_pairs={{0,24},{4,28},{8,16},{12,20},{16,8},{20,12},{24,0},{28,4},{1,25},{... | collective-permute-start | bytes 196616 | tf_op jit(solution)/shard_map/ppermute | solution.py:384
  41.1 1.4 %collective-permute-start.20 = (bf16[16,2048]{1,0:T(8,128)(2,1)S(1)}, bf16[16,2048]{1,0:T(8,128)(2,1)S(1)}, u32[]{:S(2)}, u32[]{:S(2)}) collective-permute-start(bf16[16,2048]{1,0:T(8,128)(2,1)S(1)} %get-tuple-element.117), channel_id=1, source_target_pairs={{0,16},{4,20},{8,24},{12,28},{16,0},{20,4},{24,8},{28,12},{1,17},{... | collective-permute-start | bytes 196616 | tf_op jit(solution)/shard_map/ppermute | solution.py:384
  42.5 1.7 %collective-permute-done.18.refs_1_ = bf16[16,2048]{1,0:T(8,128)(2,1)S(1)} collective-permute-done((bf16[16,2048]{1,0:T(8,128)(2,1)S(1)}, bf16[16,2048]{1,0:T(8,128)(2,1)S(1)}, u32[]{:S(2)}, u32[]{:S(2)}) %collective-permute-start.18) | collective-permute-done | bytes 65568 | tf_op jit(solution)/shard_map/ppermute | solution.py:384
  44.3 0.7 %collective-permute-done.19.refs_2_ = bf16[16,2048]{1,0:T(8,128)(2,1)S(1)} collective-permute-done((bf16[16,2048]{1,0:T(8,128)(2,1)S(1)}, bf16[16,2048]{1,0:T(8,128)(2,1)S(1)}, u32[]{:S(2)}, u32[]{:S(2)}) %collective-permute-start.19) | collective-permute-done | bytes 65568 | tf_op jit(solution)/shard_map/ppermute | solution.py:384
  45.0 1.2 %collective-permute-start.23 = (bf16[16,2048]{1,0:T(8,128)(2,1)S(1)}, bf16[16,2048]{1,0:T(8,128)(2,1)S(1)}, u32[]{:S(2)}, u32[]{:S(2)}) collective-permute-start(bf16[16,2048]{1,0:T(8,128)(2,1)S(1)} %get-tuple-element.120), channel_id=1, source_target_pairs={{0,20},{4,16},{8,28},{12,24},{16,4},{20,0},{24,12},{28,8},{1,21},{... | collective-permute-start | bytes 196616 | tf_op jit(solution)/shard_map/ppermute | solution.py:384
  46.2 0.5 %collective-permute-start.26 = (s32[1,128]{1,0:T(1,128)S(1)}, s32[1,128]{1,0:T(1,128)S(1)}, u32[]{:S(2)}, u32[]{:S(2)}) collective-permute-start(s32[1,128]{1,0:T(1,128)S(1)} %get-tuple-element.133.target_ref), channel_id=1, source_target_pairs={{0,4},{4,0},{8,12},{12,8},{16,20},{20,16},{24,28},{28,24},{1,5},{5... | collective-permute-start | bytes 1544 | tf_op jit(solution)/shard_map/ppermute | solution.py:384
  46.7 1.6 %join_outputs.1 = (bf16[256,1024]{1,0:T(8,128)(2,1)}, bf16[256,1024]{1,0:T(8,128)(2,1)}, bf16[256,256]{1,0:T(8,128)(2,1)}, bf16[256,256]{1,0:T(8,128)(2,1)}) custom-call(bf16[8,64,256]{2,1,0:T(8,128)(2,1)S(1)} %get-tuple-element.122.w_ref, bf16[8,64,256]{2,1,0:T(8,128)(2,1)S(1)} %get-tuple-element.123.ds_ref, f32[256,1024]{1,0:T(8,128)S(1)} %get-tuple-element.124.out_ref, ...), custom_call_target="tpu_custom_call" | custom-call | flops 300000000 | bytes 5000000 | tf_op jit(solution)/shard_map/join_outputs/pallas_call | solution.py:369
  48.3 0.5 %collective-permute-done.23.refs_6_ = bf16[16,2048]{1,0:T(8,128)(2,1)S(1)} collective-permute-done((bf16[16,2048]{1,0:T(8,128)(2,1)S(1)}, bf16[16,2048]{1,0:T(8,128)(2,1)S(1)}, u32[]{:S(2)}, u32[]{:S(2)}) %collective-permute-start.23) | collective-permute-done | bytes 65568 | tf_op jit(solution)/shard_map/ppermute | solution.py:384
  48.9 1.3 %sum_store_gradients.1 = (bf16[64,4,1024]{2,1,0:T(4,128)(2,1)}, bf16[64,4,1024]{2,1,0:T(4,128)(2,1)}) custom-call(s32[1,128]{1,0:T(1,128)S(1)} %get-tuple-element.133.target_ref, s32[1,128]{1,0:T(1,128)S(1)} %collective-permute-done.26.other_ref, bf16[16,2048]{1,0:T(8,128)(2,1)S(1)} %get-tuple-element.134.refs_0_, ...), custom_call_target="tpu_custom_call" | custom-call | flops 200000000 | bytes 2000000 | tf_op jit(solution)/shard_map/sum_store_gradients/pallas_call | solution.py:369
  (40 shorter events, 3.4 us)
Async XLA Ops:
  0.6 6.1 %collective-permute-start = (bf16[64,4,1024]{2,1,0:T(4,128)(2,1)}, bf16[64,4,1024]{2,1,0:T(4,128)(2,1)S(1)}, u32[]{:S(2)}, u32[]{:S(2)}) collective-permute-start(bf16[64,4,1024]{2,1,0:T(4,128)(2,1)} %k_any.1), channel_id=1, source_target_pairs={{0,4},{4,0},{8,12},{12,8},{16,20},{20,16},{24,28},{28,24},{1,5},{5... | collective-permute-start | bytes 1572872 | tf_op jit(solution)/shard_map/ppermute | solution.py:384
  1.1 5.6 %collective-permute-start.1 = (bf16[64,4,1024]{2,1,0:T(4,128)(2,1)}, bf16[64,4,1024]{2,1,0:T(4,128)(2,1)S(1)}, u32[]{:S(2)}, u32[]{:S(2)}) collective-permute-start(bf16[64,4,1024]{2,1,0:T(4,128)(2,1)} %v_any.1), channel_id=1, source_target_pairs={{0,4},{4,0},{8,12},{12,8},{16,20},{20,16},{24,28},{28,24},{1,5},{5... | collective-permute-start | bytes 1572872 | tf_op jit(solution)/shard_map/ppermute | solution.py:384
  2.2 6.1 %collective-permute-start.2 = (s32[8,128]{1,0:T(8,128)S(1)}, s32[8,128]{1,0:T(8,128)S(1)}, u32[]{:S(2)}, u32[]{:S(2)}) collective-permute-start(s32[8,128]{1,0:T(8,128)S(1)} %plan_requests.1.refs_0_), channel_id=1, source_target_pairs={{0,24},{4,28},{8,16},{12,20},{16,8},{20,12},{24,0},{28,4},{1,25},{... | collective-permute-start | bytes 12296 | tf_op jit(solution)/shard_map/ppermute | solution.py:384
  6.1 3.6 %collective-permute-start.3 = (s32[8,128]{1,0:T(8,128)S(1)}, s32[8,128]{1,0:T(8,128)S(1)}, u32[]{:S(2)}, u32[]{:S(2)}) collective-permute-start(s32[8,128]{1,0:T(8,128)S(1)} %plan_requests.1.refs_0_), channel_id=1, source_target_pairs={{0,8},{4,12},{8,0},{12,4},{16,24},{20,28},{24,16},{28,20},{1,9},{5... | collective-permute-start | bytes 12296 | tf_op jit(solution)/shard_map/ppermute | solution.py:384
  6.6 3.6 %collective-permute-start.4 = (s32[8,128]{1,0:T(8,128)S(1)}, s32[8,128]{1,0:T(8,128)S(1)}, u32[]{:S(2)}, u32[]{:S(2)}) collective-permute-start(s32[8,128]{1,0:T(8,128)S(1)} %plan_requests.1.refs_0_), channel_id=1, source_target_pairs={{0,16},{4,20},{8,24},{12,28},{16,0},{20,4},{24,8},{28,12},{1,17},{... | collective-permute-start | bytes 12296 | tf_op jit(solution)/shard_map/ppermute | solution.py:384
  6.7 22.0 %copy-start.2 = (bf16[256,1024]{1,0:T(8,128)(2,1)S(1)}, bf16[256,1024]{1,0:T(8,128)(2,1)}, u32[]{:S(2)}) copy-start(bf16[256,1024]{1,0:T(8,128)(2,1)} %q_ref.3) | copy-start | bytes 1572868
  6.7 22.0 %copy-start.3 = (bf16[256,1024]{1,0:T(8,128)(2,1)S(1)}, bf16[256,1024]{1,0:T(8,128)(2,1)}, u32[]{:S(2)}) copy-start(bf16[256,1024]{1,0:T(8,128)(2,1)} %do_ref.3) | copy-start | bytes 1572868
  10.2 23.1 %copy-start = (bf16[256,256]{1,0:T(8,128)(2,1)S(1)}, bf16[256,256]{1,0:T(8,128)(2,1)}, u32[]{:S(2)}) copy-start(bf16[256,256]{1,0:T(8,128)(2,1)} %k_ref.1) | copy-start | bytes 393220
  10.2 23.1 %copy-start.1 = (bf16[256,256]{1,0:T(8,128)(2,1)S(1)}, bf16[256,256]{1,0:T(8,128)(2,1)}, u32[]{:S(2)}) copy-start(bf16[256,256]{1,0:T(8,128)(2,1)} %v_ref.1) | copy-start | bytes 393220
  10.7 5.9 %collective-permute-start.8 = (bf16[32,1024]{1,0:T(8,128)(2,1)S(1)}, bf16[32,1024]{1,0:T(8,128)(2,1)S(1)}, u32[]{:S(2)}, u32[]{:S(2)}) collective-permute-start(bf16[32,1024]{1,0:T(8,128)(2,1)S(1)} %get-tuple-element.83), channel_id=1, source_target_pairs={{0,24},{4,28},{8,16},{12,20},{16,8},{20,12},{24,0},{28,4},{1,25},{... | collective-permute-start | bytes 196616 | tf_op jit(solution)/shard_map/ppermute | solution.py:384
  12.2 5.6 %collective-permute-start.9 = (bf16[32,1024]{1,0:T(8,128)(2,1)S(1)}, bf16[32,1024]{1,0:T(8,128)(2,1)S(1)}, u32[]{:S(2)}, u32[]{:S(2)}) collective-permute-start(bf16[32,1024]{1,0:T(8,128)(2,1)S(1)} %get-tuple-element.84), channel_id=1, source_target_pairs={{0,8},{4,12},{8,0},{12,4},{16,24},{20,28},{24,16},{28,20},{1,9},{5... | collective-permute-start | bytes 196616 | tf_op jit(solution)/shard_map/ppermute | solution.py:384
  12.4 5.7 %collective-permute-start.10 = (bf16[32,1024]{1,0:T(8,128)(2,1)S(1)}, bf16[32,1024]{1,0:T(8,128)(2,1)S(1)}, u32[]{:S(2)}, u32[]{:S(2)}) collective-permute-start(bf16[32,1024]{1,0:T(8,128)(2,1)S(1)} %get-tuple-element.85), channel_id=1, source_target_pairs={{0,16},{4,20},{8,24},{12,28},{16,0},{20,4},{24,8},{28,12},{1,17},{... | collective-permute-start | bytes 196616 | tf_op jit(solution)/shard_map/ppermute | solution.py:384
  14.3 6.7 %collective-permute-start.5 = (bf16[32,1024]{1,0:T(8,128)(2,1)S(1)}, bf16[32,1024]{1,0:T(8,128)(2,1)S(1)}, u32[]{:S(2)}, u32[]{:S(2)}) collective-permute-start(bf16[32,1024]{1,0:T(8,128)(2,1)S(1)} %get-tuple-element.78), channel_id=1, source_target_pairs={{0,24},{4,28},{8,16},{12,20},{16,8},{20,12},{24,0},{28,4},{1,25},{... | collective-permute-start | bytes 196616 | tf_op jit(solution)/shard_map/ppermute | solution.py:384
  15.7 7.3 %collective-permute-start.6 = (bf16[32,1024]{1,0:T(8,128)(2,1)S(1)}, bf16[32,1024]{1,0:T(8,128)(2,1)S(1)}, u32[]{:S(2)}, u32[]{:S(2)}) collective-permute-start(bf16[32,1024]{1,0:T(8,128)(2,1)S(1)} %get-tuple-element.79), channel_id=1, source_target_pairs={{0,8},{4,12},{8,0},{12,4},{16,24},{20,28},{24,16},{28,20},{1,9},{5... | collective-permute-start | bytes 196616 | tf_op jit(solution)/shard_map/ppermute | solution.py:384
  16.7 6.4 %collective-permute-start.7 = (bf16[32,1024]{1,0:T(8,128)(2,1)S(1)}, bf16[32,1024]{1,0:T(8,128)(2,1)S(1)}, u32[]{:S(2)}, u32[]{:S(2)}) collective-permute-start(bf16[32,1024]{1,0:T(8,128)(2,1)S(1)} %get-tuple-element.80), channel_id=1, source_target_pairs={{0,16},{4,20},{8,24},{12,28},{16,0},{20,4},{24,8},{28,12},{1,17},{... | collective-permute-start | bytes 196616 | tf_op jit(solution)/shard_map/ppermute | solution.py:384
  17.8 11.8 %collective-permute-start.14 = (bf16[128,512]{1,0:T(8,128)(2,1)S(1)}, bf16[128,512]{1,0:T(8,128)(2,1)S(1)}, u32[]{:S(2)}, u32[]{:S(2)}) collective-permute-start(bf16[128,512]{1,0:T(8,128)(2,1)S(1)} %get-tuple-element.93), channel_id=1, source_target_pairs={{0,4},{4,8},{8,12},{12,16},{16,20},{20,24},{24,28},{28,0},{1,5},{5... | collective-permute-start | bytes 393224 | tf_op jit(solution)/shard_map/ppermute | solution.py:501
  18.3 5.6 %collective-permute-start.11 = (bf16[64,512]{1,0:T(8,128)(2,1)S(1)}, bf16[64,512]{1,0:T(8,128)(2,1)S(1)}, u32[]{:S(2)}, u32[]{:S(2)}) collective-permute-start(bf16[64,512]{1,0:T(8,128)(2,1)S(1)} %get-tuple-element.86), channel_id=1, source_target_pairs={{0,2},{1,3},{2,0},{3,1},{4,6},{5,7},{6,4},{7,5},{8,10},{9,11},{10,... | collective-permute-start | bytes 196616 | tf_op jit(solution)/shard_map/ppermute | solution.py:384
  20.9 6.8 %collective-permute-start.12 = (bf16[64,512]{1,0:T(8,128)(2,1)S(1)}, bf16[64,512]{1,0:T(8,128)(2,1)S(1)}, u32[]{:S(2)}, u32[]{:S(2)}) collective-permute-start(bf16[64,512]{1,0:T(8,128)(2,1)S(1)} %get-tuple-element.87), channel_id=1, source_target_pairs={{0,3},{1,2},{2,1},{3,0},{4,7},{5,6},{6,5},{7,4},{8,11},{9,10},{10,... | collective-permute-start | bytes 196616 | tf_op jit(solution)/shard_map/ppermute | solution.py:384
  23.3 5.5 %collective-permute-start.13 = (bf16[64,512]{1,0:T(8,128)(2,1)S(1)}, bf16[64,512]{1,0:T(8,128)(2,1)S(1)}, u32[]{:S(2)}, u32[]{:S(2)}) collective-permute-start(bf16[64,512]{1,0:T(8,128)(2,1)S(1)} %get-tuple-element.88), channel_id=1, source_target_pairs={{0,1},{1,0},{2,3},{3,2},{4,5},{5,4},{6,7},{7,6},{8,9},{9,8},{10,11... | collective-permute-start | bytes 196616 | tf_op jit(solution)/shard_map/ppermute | solution.py:384
  29.6 7.6 %collective-permute-start.15 = (bf16[64,512]{1,0:T(8,128)(2,1)S(1)}, bf16[64,512]{1,0:T(8,128)(2,1)S(1)}, u32[]{:S(2)}, u32[]{:S(2)}) collective-permute-start(bf16[64,512]{1,0:T(8,128)(2,1)S(1)} %get-tuple-element.96), channel_id=1, source_target_pairs={{0,2},{1,3},{2,0},{3,1},{4,6},{5,7},{6,4},{7,5},{8,10},{9,11},{10,... | collective-permute-start | bytes 196616 | tf_op jit(solution)/shard_map/ppermute | solution.py:384
  31.9 6.4 %collective-permute-start.16 = (bf16[64,512]{1,0:T(8,128)(2,1)S(1)}, bf16[64,512]{1,0:T(8,128)(2,1)S(1)}, u32[]{:S(2)}, u32[]{:S(2)}) collective-permute-start(bf16[64,512]{1,0:T(8,128)(2,1)S(1)} %get-tuple-element.97), channel_id=1, source_target_pairs={{0,3},{1,2},{2,1},{3,0},{4,7},{5,6},{6,5},{7,4},{8,11},{9,10},{10,... | collective-permute-start | bytes 196616 | tf_op jit(solution)/shard_map/ppermute | solution.py:384
  32.8 5.8 %collective-permute-start.17 = (bf16[64,512]{1,0:T(8,128)(2,1)S(1)}, bf16[64,512]{1,0:T(8,128)(2,1)S(1)}, u32[]{:S(2)}, u32[]{:S(2)}) collective-permute-start(bf16[64,512]{1,0:T(8,128)(2,1)S(1)} %get-tuple-element.98), channel_id=1, source_target_pairs={{0,1},{1,0},{2,3},{3,2},{4,5},{5,4},{6,7},{7,6},{8,9},{9,8},{10,11... | collective-permute-start | bytes 196616 | tf_op jit(solution)/shard_map/ppermute | solution.py:384
  36.2 10.0 %collective-permute-start.25 = (bf16[128,512]{1,0:T(8,128)(2,1)S(1)}, bf16[128,512]{1,0:T(8,128)(2,1)S(1)}, u32[]{:S(2)}, u32[]{:S(2)}) collective-permute-start(bf16[128,512]{1,0:T(8,128)(2,1)S(1)} %get-tuple-element.127), channel_id=1, source_target_pairs={{4,0},{8,4},{12,8},{16,12},{20,16},{24,20},{28,24},{0,28},{5,1},{9... | collective-permute-start | bytes 393224 | tf_op jit(solution)/shard_map/ppermute | solution.py:552
  38.9 5.2 %collective-permute-start.18 = (bf16[16,2048]{1,0:T(8,128)(2,1)S(1)}, bf16[16,2048]{1,0:T(8,128)(2,1)S(1)}, u32[]{:S(2)}, u32[]{:S(2)}) collective-permute-start(bf16[16,2048]{1,0:T(8,128)(2,1)S(1)} %get-tuple-element.115), channel_id=1, source_target_pairs={{0,24},{4,28},{8,16},{12,20},{16,8},{20,12},{24,0},{28,4},{1,25},{... | collective-permute-start | bytes 196616 | tf_op jit(solution)/shard_map/ppermute | solution.py:384
  40.8 4.3 %collective-permute-start.19 = (bf16[16,2048]{1,0:T(8,128)(2,1)S(1)}, bf16[16,2048]{1,0:T(8,128)(2,1)S(1)}, u32[]{:S(2)}, u32[]{:S(2)}) collective-permute-start(bf16[16,2048]{1,0:T(8,128)(2,1)S(1)} %get-tuple-element.116), channel_id=1, source_target_pairs={{0,8},{4,12},{8,0},{12,4},{16,24},{20,28},{24,16},{28,20},{1,9},{5... | collective-permute-start | bytes 196616 | tf_op jit(solution)/shard_map/ppermute | solution.py:384
  41.1 5.1 %collective-permute-start.20 = (bf16[16,2048]{1,0:T(8,128)(2,1)S(1)}, bf16[16,2048]{1,0:T(8,128)(2,1)S(1)}, u32[]{:S(2)}, u32[]{:S(2)}) collective-permute-start(bf16[16,2048]{1,0:T(8,128)(2,1)S(1)} %get-tuple-element.117), channel_id=1, source_target_pairs={{0,16},{4,20},{8,24},{12,28},{16,0},{20,4},{24,8},{28,12},{1,17},{... | collective-permute-start | bytes 196616 | tf_op jit(solution)/shard_map/ppermute | solution.py:384
  42.5 5.8 %collective-permute-start.21 = (bf16[16,2048]{1,0:T(8,128)(2,1)S(1)}, bf16[16,2048]{1,0:T(8,128)(2,1)S(1)}, u32[]{:S(2)}, u32[]{:S(2)}) collective-permute-start(bf16[16,2048]{1,0:T(8,128)(2,1)S(1)} %get-tuple-element.118), channel_id=1, source_target_pairs={{0,28},{4,24},{8,20},{12,16},{16,12},{20,8},{24,4},{28,0},{1,29},{... | collective-permute-start | bytes 196616 | tf_op jit(solution)/shard_map/ppermute | solution.py:384
  44.2 4.1 %collective-permute-start.22 = (bf16[16,2048]{1,0:T(8,128)(2,1)S(1)}, bf16[16,2048]{1,0:T(8,128)(2,1)S(1)}, u32[]{:S(2)}, u32[]{:S(2)}) collective-permute-start(bf16[16,2048]{1,0:T(8,128)(2,1)S(1)} %get-tuple-element.119), channel_id=1, source_target_pairs={{0,12},{4,8},{8,4},{12,0},{16,28},{20,24},{24,20},{28,16},{1,13},{... | collective-permute-start | bytes 196616 | tf_op jit(solution)/shard_map/ppermute | solution.py:384
  45.0 3.8 %collective-permute-start.23 = (bf16[16,2048]{1,0:T(8,128)(2,1)S(1)}, bf16[16,2048]{1,0:T(8,128)(2,1)S(1)}, u32[]{:S(2)}, u32[]{:S(2)}) collective-permute-start(bf16[16,2048]{1,0:T(8,128)(2,1)S(1)} %get-tuple-element.120), channel_id=1, source_target_pairs={{0,20},{4,16},{8,28},{12,24},{16,4},{20,0},{24,12},{28,8},{1,21},{... | collective-permute-start | bytes 196616 | tf_op jit(solution)/shard_map/ppermute | solution.py:384
  46.2 2.6 %collective-permute-start.24 = (bf16[16,2048]{1,0:T(8,128)(2,1)S(1)}, bf16[16,2048]{1,0:T(8,128)(2,1)S(1)}, u32[]{:S(2)}, u32[]{:S(2)}) collective-permute-start(bf16[16,2048]{1,0:T(8,128)(2,1)S(1)} %get-tuple-element.121), channel_id=1, source_target_pairs={{0,4},{4,0},{8,12},{12,8},{16,20},{20,16},{24,28},{28,24},{1,5},{5... | collective-permute-start | bytes 196616 | tf_op jit(solution)/shard_map/ppermute | solution.py:384
  46.2 2.6 %collective-permute-start.26 = (s32[1,128]{1,0:T(1,128)S(1)}, s32[1,128]{1,0:T(1,128)S(1)}, u32[]{:S(2)}, u32[]{:S(2)}) collective-permute-start(s32[1,128]{1,0:T(1,128)S(1)} %get-tuple-element.133.target_ref), channel_id=1, source_target_pairs={{0,4},{4,0},{8,12},{12,8},{16,20},{20,16},{24,28},{28,24},{1,5},{5... | collective-permute-start | bytes 1544 | tf_op jit(solution)/shard_map/ppermute | solution.py:384

commit v5 on v4

--- a/solution.py
+++ b/solution.py
@@ -203,16 +203,25 @@
         send_ref[...] = rows[:, i * width : (i + 1) * width]
 
 
-def scatter_kernel(tp, z_ref, placed_ref, *refs):
-    grad_refs, send_refs, all_ref = refs[:tp], refs[tp:-1], refs[-1]
-    both = grad_refs[0].shape[1]
-    rows_each = send_refs[0].shape[0]
-    for apart, grad_ref in zip(distances(tp), grad_refs):
-        start = pl.multiple_of((z_ref[0] ^ apart) * both, both)
-        all_ref[:, pl.ds(start, both)] = grad_ref[...]
-    rows = dot_nn(placed_ref[...], all_ref[...]).astype(BF16)
-    for at, send_ref in enumerate(by_distance(send_refs)):
-        send_ref[...] = rows[at * rows_each : (at + 1) * rows_each]
+def scatter_kernel(chips, placed_ref, *refs):
+    grad_refs, send_refs = refs[:-chips], refs[-chips:]
+    grads = jnp.concatenate([ref[...] for ref in grad_refs], axis=1)
+    rows = dot_nn(placed_ref[...], grads).astype(BF16)
+    step = send_refs[0].shape[0]
+    for m, send_ref in enumerate(by_chip(send_refs)):
+        send_ref[...] = rows[m * step : (m + 1) * step]
+
+
+def part_cores_kernel(*refs):
+    got_refs, (same_ref, other_ref) = refs[:-2], refs[-2:]
+    chips = len(got_refs) // 2
+    rows, columns = got_refs[0].shape[0] // 2, got_refs[0].shape[1]
+    for half in range(2):
+        cols = slice(half * columns, (half + 1) * columns)
+        for m, got_ref in enumerate(by_chip(got_refs[half * chips : (half + 1) * chips])):
+            here = slice(m * rows, (m + 1) * rows)
+            same_ref[here, cols] = got_ref[:rows]
+            other_ref[here, cols] = got_ref[rows:]
 
 
 def self_kernel(
@@ -331,14 +340,30 @@
     ).astype(BF16)
 
 
-def sum_kernel(chunks, target_ref, other_ref, *refs):
-    got_refs, (kg_any, vg_any, kg_ref, vg_ref, sems) = refs[:-5], refs[-5:]
+def sum_kernel(
+    chunks,
+    rows_each,
+    z_ref,
+    target_ref,
+    other_ref,
+    same_rows,
+    other_rows,
+    kg_any,
+    vg_any,
+    kg_ref,
+    vg_ref,
+    sems,
+):
     slots, tokens, features = kg_ref.shape
     tp = NEIGHBOUR_LENGTH // tokens
     width = features // tp
-    got = jnp.concatenate([ref[...] for ref in by_distance(got_refs)], axis=0)
+    got = []
+    for m in range(same_rows.shape[0] // rows_each):
+        here = slice(m * rows_each, (m + 1) * rows_each)
+        got += [same_rows[here], other_rows[here]]
+    got = jnp.concatenate(got, axis=0)
     lanes = target_ref.shape[1]
-    odd = (lax.broadcasted_iota(jnp.int32, (1, lanes), 1) // got_refs[0].shape[0]) % 2
+    odd = (lax.broadcasted_iota(jnp.int32, (1, lanes), 1) // rows_each) % 2
     target = jnp.where(odd == 0, target_ref[...], other_ref[...])
     row = lax.broadcasted_iota(jnp.int32, (slots * tokens, lanes), 0)
     owned = jnp.where(row == target, 1.0, 0.0).astype(BF16)
@@ -347,9 +372,9 @@
     for i in range(chunks):
         part = slice(i * step, (i + 1) * step)
         total = dot_nn(owned[i * step * tokens : (i + 1) * step * tokens], got).astype(BF16)
-        for z in range(tp):
-            cols = slice(z * width, (z + 1) * width)
-            at = 2 * z * width
+        for d, apart in enumerate(farthest_first(tp)):
+            cols = pl.ds(pl.multiple_of((z_ref[0] ^ apart) * width, width), width)
+            at = 2 * d * width
             kg_ref[part, :, cols] = total[:, at : at + width].reshape(step, tokens, width)
             vg_ref[part, :, cols] = total[:, at + width : at + 2 * width].reshape(
                 step, tokens, width
@@ -382,23 +407,6 @@
 
 def swapped(block, axis, apart):
     return lax.ppermute(block, axis, [(i, i ^ apart) for i in range(lax.axis_size(axis))])
-
-
-def plane_order(devices):
-    def key(j):
-        return (j == 1, j & 1, -bin(j >> 1).count("1"), j)
-
-    return [0] + sorted(range(1, devices), key=key)
-
-
-def by_distance(refs):
-    order = plane_order(len(refs))
-    return [refs[order.index(j)] for j in range(len(refs))]
-
-
-def crossed(blocks):
-    order = plane_order(len(blocks))
-    return [blocks[0]] + [swapped(b, "seq", j) for b, j in zip(blocks[1:], order[1:])]
 
 
 def chip_order(chips):
@@ -498,7 +506,6 @@
         scalars=2,
         fetched=5,
     )
-    halo = lax.ppermute(halo, "seq", [(i, (i + 1) % devices) for i in range(devices)])
     block = struct((2 * rows_each, features), BF16)
     *sent, target = call(
         functools.partial(pack_kernel, rows_each),
@@ -511,16 +518,35 @@
     )
     parts = tp // 2
     moved = []
-    for name, blocks in (("spread_far", sent[:chips]), ("spread_near", sent[chips:])):
+    far, near = between_chips(sent[:chips]), sent[chips:]
+    for name, got in (("spread_far", far), ("spread_near", between_chips(near))):
         moved += call(
             functools.partial(spread_kernel, parts),
             name,
-            (placed, *between_chips(blocks)),
+            (placed, *got),
             [struct((used, both), BF16)] * parts,
             1_000_000,
             10_000,
         )
     near = exchanged(moved[-1:] + moved[:-1])
+    halo = lax.ppermute(halo, "seq", [(i, (i + 1) % devices) for i in range(devices)])
+    other_target = swapped(target, "seq", 1)
+    self_out, self_dq, self_dkv, back = call(
+        self_kernel,
+        "self_attention",
+        (rank, queries, sequence_keys, sequence_values, output_gradient, halo),
+        (
+            struct((tokens_here, query_width), F32),
+            struct((tokens_here, query_width), F32),
+            struct((tokens_here, both), F32),
+            struct((window, both), BF16),
+        ),
+        1_000_000,
+        10_000,
+        scalars=1,
+    )
+    back = lax.ppermute(back, "seq", [((i + 1) % devices, i) for i in range(devices)])
+    near[1], self_out = lax.optimization_barrier((near[1], self_out))
 
     blocks = spans * groups
     rows_span = per_span * NEIGHBOUR_LENGTH
@@ -533,39 +559,24 @@
         600_000_000,
         3_000_000,
     )
-    grads, halo, target = lax.optimization_barrier((grads, halo, target))
     grads = exchanged(grads)
-    self_out, self_dq, self_dkv, back = call(
-        self_kernel,
-        "self_attention",
-        (rank, queries, sequence_keys, sequence_values, output_gradient, halo),
-        (
-            struct((tokens_here, query_width), F32),
-            struct((tokens_here, query_width), F32),
-            struct((tokens_here, both), F32),
-            struct((window, both), BF16),
-        ),
-        1_600_000_000,
-        6_000_000,
-        scalars=1,
-    )
-    back = lax.ppermute(back, "seq", [((i + 1) % devices, i) for i in range(devices)])
-    other_target = swapped(target, "seq", 1)
-    grads, self_out = lax.optimization_barrier((grads, self_out))
-
-    returned = call(
-        functools.partial(scatter_kernel, tp),
-        "scatter_gradients",
-        (z_rank, placed, *grads),
-        [struct((rows_each, tp * both), BF16)] * devices,
-        50_000_000,
-        1_000_000,
-        scratch=[pltpu.VMEM((used, tp * both), BF16)],
-        scalars=1,
-    )
-    returned, weights = lax.optimization_barrier((returned, weights))
-    returned = crossed(returned)
-
+    grads = grads[1:] + grads[:1]
+    returned = []
+    for name, half in (("scatter_near", grads[parts:]), ("scatter_far", grads[:parts])):
+        if returned:
+            half, returned[2] = lax.optimization_barrier((half, returned[2]))
+        sent = call(
+            functools.partial(scatter_kernel, chips),
+            name,
+            (placed, *half),
+            [block] * chips,
+            1_000_000,
+            10_000,
+        )
+        if returned:
+            sent, weights = lax.optimization_barrier((sent, weights))
+        returned += between_chips(sent)
+    returned = returned[chips:] + returned[:chips]
     attended, query_gradient, key_gradient, value_gradient = call(
         functools.partial(join_kernel, tp),
         "join_outputs",
@@ -579,11 +590,21 @@
         300_000_000,
         5_000_000,
     )
-    returned, attended = lax.optimization_barrier((returned, attended))
+    returned[0], attended = lax.optimization_barrier((returned[0], attended))
+    same, other = call(
+        part_cores_kernel,
+        "part_cores",
+        tuple(returned),
+        [struct((lanes // 2, 2 * features), BF16)] * 2,
+        0,
+        10_000,
+    )
+    other = swapped(other, "seq", 1)
+
     store_kgrad, store_vgrad = call(
-        functools.partial(sum_kernel, chunks),
+        functools.partial(sum_kernel, chunks, rows_each),
         "sum_store_gradients",
-        (target, other_target, *returned),
+        (z_rank, target, other_target, same, other),
         (struct(enc_keys.shape, BF16), struct(encoded_values.shape, BF16)),
         200_000_000,
         2_000_000,
@@ -592,6 +613,7 @@
             pltpu.VMEM(encoded_values.shape, BF16),
             pltpu.SemaphoreType.DMA((2 * chunks,)),
         ],
+        scalars=1,
         stores=True,
     )
     return (

time: 50.3 us -> 50.8 us (level)
  starting transfers between devices: 26.4 us -> 29.2 us
  waiting for transfers between devices: 12.8 us -> 10.3 us
    ppermute x25, starting transfers between devices: 25.4 us -> 28.4 us  [swapped(): lax.ppermute(block, axis, [(i, i ^ apart) for i in range(lax.axis_size(ax...]
    ppermute x25, waiting for transfers between devices: 12.8 us -> 10.3 us  [swapped(): lax.ppermute(block, axis, [(i, i ^ apart) for i in range(lax.axis_size(ax...]
    pallas_call x10 -> x12, Pallas kernels: 10.1 us -> 10.3 us  [call(): pl.pallas_call(kernel, out_shape=tuple(outs), in_specs=[SMEM] * scalars +...]
  transfers between devices with their start and end apart: 27 -> 27, of which waited for: 12 -> 10; matrix products, arithmetic and copies ran while one was open for 0% -> 0% of each run, Pallas kernels for 17% -> 15%
where the time goes in v5:
time: 50.8 us; the launch traced here: 50.6 us
  starting transfers between devices  29.2 us (57%)
  Pallas kernels  10.3 us (20%)
  waiting for transfers between devices  10.3 us (20%)
  between operations  0.8 us (2%)
    ppermute x25, starting transfers between devices, swapped(): lax.ppermute(block, axis, [(i, i ^ apart) for i in range(lax.axis_size(ax...  28.4 us
    ppermute x25, waiting for transfers between devices, swapped(): lax.ppermute(block, axis, [(i, i ^ apart) for i in range(lax.axis_size(ax...  10.3 us
    pallas_call x12, Pallas kernels, call(): pl.pallas_call(kernel, out_shape=tuple(outs), in_specs=[SMEM] * scalars +...  10.3 us
  transfers between devices with their start and end apart: 27, of which 10 were waited for; matrix products, arithmetic and copies ran while one was open for 0% of the time, Pallas kernels for 15%

profile of v5, /device:TPU:0, one launch (start us, length us, event | category | flops | bytes accessed | tf_op | source)
XLA Modules:
  0.0 50.6 jit_solution(9827591981016203131)
XLA Ops:
  1.2 0.9 %plan_requests.1.refs_0_ = s32[8,128]{1,0:T(8,128)S(1)} custom-call(s32[4,4]{1,0:T(4,128)} %owner_any.3, s32[4,4]{1,0:T(4,128)} %slot_any.1), custom_call_target="tpu_custom_call" | custom-call | bytes 100000 | tf_op jit(solution)/shard_map/plan_requests/pallas_call | solution.py:394
  2.2 3.9 %collective-permute-start.2 = (s32[8,128]{1,0:T(8,128)S(1)}, s32[8,128]{1,0:T(8,128)S(1)}, u32[]{:S(2)}, u32[]{:S(2)}) collective-permute-start(s32[8,128]{1,0:T(8,128)S(1)} %plan_requests.1.refs_0_), channel_id=1, source_target_pairs={{0,24},{4,28},{8,16},{12,20},{16,8},{20,12},{24,0},{28,4},{1,25},{... | collective-permute-start | bytes 12296 | tf_op jit(solution)/shard_map/ppermute | solution.py:409
  6.1 0.5 %collective-permute-start.3 = (s32[8,128]{1,0:T(8,128)S(1)}, s32[8,128]{1,0:T(8,128)S(1)}, u32[]{:S(2)}, u32[]{:S(2)}) collective-permute-start(s32[8,128]{1,0:T(8,128)S(1)} %plan_requests.1.refs_0_), channel_id=1, source_target_pairs={{0,8},{4,12},{8,0},{12,4},{16,24},{20,28},{24,16},{28,20},{1,9},{5... | collective-permute-start | bytes 12296 | tf_op jit(solution)/shard_map/ppermute | solution.py:409
  6.8 1.5 %stage_store.1 = (bf16[512,2048]{1,0:T(8,128)(2,1)S(1)}, bf16[128,512]{1,0:T(8,128)(2,1)S(1)}, bf16[128,64]{1,0:T(8,128)(2,1)S(1)}) custom-call(s32[1]{0:T(128)} %bitcast.me_ref.rank_ref, s32[1]{0:T(128)} %bitcast.1.z_ref, bf16[64,4,1024]{2,1,0:T(4,128)(2,1)S(1)} %collective-permute-done.sibling_k_ref, ...), custom_call_target="tpu_custom_call" | custom-call | bytes 5000000 | tf_op jit(solution)/shard_map/stage_store/pallas_call | solution.py:394
  8.3 1.4 %collective-permute-done.3.refs_2_ = s32[8,128]{1,0:T(8,128)S(1)} collective-permute-done((s32[8,128]{1,0:T(8,128)S(1)}, s32[8,128]{1,0:T(8,128)S(1)}, u32[]{:S(2)}, u32[]{:S(2)}) %collective-permute-start.3) | collective-permute-done | bytes 4128 | tf_op jit(solution)/shard_map/ppermute | solution.py:409
  9.7 0.5 %collective-permute-done.4.refs_3_ = s32[8,128]{1,0:T(8,128)S(1)} collective-permute-done((s32[8,128]{1,0:T(8,128)S(1)}, s32[8,128]{1,0:T(8,128)S(1)}, u32[]{:S(2)}, u32[]{:S(2)}) %collective-permute-start.4) | collective-permute-done | bytes 4128 | tf_op jit(solution)/shard_map/ppermute | solution.py:409
  10.9 2.8 %collective-permute-start.8 = (bf16[32,1024]{1,0:T(8,128)(2,1)S(1)}, bf16[32,1024]{1,0:T(8,128)(2,1)S(1)}, u32[]{:S(2)}, u32[]{:S(2)}) collective-permute-start(bf16[32,1024]{1,0:T(8,128)(2,1)S(1)} %get-tuple-element.68), channel_id=1, source_target_pairs={{0,24},{4,28},{8,16},{12,20},{16,8},{20,12},{24,0},{28,4},{1,25},{... | collective-permute-start | bytes 196616 | tf_op jit(solution)/shard_map/ppermute | solution.py:409
  13.7 0.5 %collective-permute-start.9 = (bf16[32,1024]{1,0:T(8,128)(2,1)S(1)}, bf16[32,1024]{1,0:T(8,128)(2,1)S(1)}, u32[]{:S(2)}, u32[]{:S(2)}) collective-permute-start(bf16[32,1024]{1,0:T(8,128)(2,1)S(1)} %get-tuple-element.69), channel_id=1, source_target_pairs={{0,8},{4,12},{8,0},{12,4},{16,24},{20,28},{24,16},{28,20},{1,9},{5... | collective-permute-start | bytes 196616 | tf_op jit(solution)/shard_map/ppermute | solution.py:409
  14.3 1.4 %collective-permute-start.5 = (bf16[32,1024]{1,0:T(8,128)(2,1)S(1)}, bf16[32,1024]{1,0:T(8,128)(2,1)S(1)}, u32[]{:S(2)}, u32[]{:S(2)}) collective-permute-start(bf16[32,1024]{1,0:T(8,128)(2,1)S(1)} %get-tuple-element.63), channel_id=1, source_target_pairs={{0,24},{4,28},{8,16},{12,20},{16,8},{20,12},{24,0},{28,4},{1,25},{... | collective-permute-start | bytes 196616 | tf_op jit(solution)/shard_map/ppermute | solution.py:409
  15.7 0.8 %collective-permute-start.6 = (bf16[32,1024]{1,0:T(8,128)(2,1)S(1)}, bf16[32,1024]{1,0:T(8,128)(2,1)S(1)}, u32[]{:S(2)}, u32[]{:S(2)}) collective-permute-start(bf16[32,1024]{1,0:T(8,128)(2,1)S(1)} %get-tuple-element.64), channel_id=1, source_target_pairs={{0,8},{4,12},{8,0},{12,4},{16,24},{20,28},{24,16},{28,20},{1,9},{5... | collective-permute-start | bytes 196616 | tf_op jit(solution)/shard_map/ppermute | solution.py:409
  16.6 1.4 %collective-permute-start.7 = (bf16[32,1024]{1,0:T(8,128)(2,1)S(1)}, bf16[32,1024]{1,0:T(8,128)(2,1)S(1)}, u32[]{:S(2)}, u32[]{:S(2)}) collective-permute-start(bf16[32,1024]{1,0:T(8,128)(2,1)S(1)} %get-tuple-element.65), channel_id=1, source_target_pairs={{0,16},{4,20},{8,24},{12,28},{16,0},{20,4},{24,8},{28,12},{1,17},{... | collective-permute-start | bytes 196616 | tf_op jit(solution)/shard_map/ppermute | solution.py:409
  18.0 0.7 %collective-permute-done.9.refs_2_ = bf16[32,1024]{1,0:T(8,128)(2,1)S(1)} collective-permute-done((bf16[32,1024]{1,0:T(8,128)(2,1)S(1)}, bf16[32,1024]{1,0:T(8,128)(2,1)S(1)}, u32[]{:S(2)}, u32[]{:S(2)}) %collective-permute-start.9) | collective-permute-done | bytes 65568 | tf_op jit(solution)/shard_map/ppermute | solution.py:409
  18.9 2.7 %collective-permute-start.11 = (bf16[64,512]{1,0:T(8,128)(2,1)S(1)}, bf16[64,512]{1,0:T(8,128)(2,1)S(1)}, u32[]{:S(2)}, u32[]{:S(2)}) collective-permute-start(bf16[64,512]{1,0:T(8,128)(2,1)S(1)} %get-tuple-element.71), channel_id=1, source_target_pairs={{0,2},{1,3},{2,0},{3,1},{4,6},{5,7},{6,4},{7,5},{8,10},{9,11},{10,... | collective-permute-start | bytes 196616 | tf_op jit(solution)/shard_map/ppermute | solution.py:409
  21.6 2.2 %collective-permute-start.13 = (bf16[64,512]{1,0:T(8,128)(2,1)S(1)}, bf16[64,512]{1,0:T(8,128)(2,1)S(1)}, u32[]{:S(2)}, u32[]{:S(2)}) collective-permute-start(bf16[64,512]{1,0:T(8,128)(2,1)S(1)} %get-tuple-element.75), channel_id=1, source_target_pairs={{0,3},{1,2},{2,1},{3,0},{4,7},{5,6},{6,5},{7,4},{8,11},{9,10},{10,... | collective-permute-start | bytes 196616 | tf_op jit(solution)/shard_map/ppermute | solution.py:409
  24.3 2.9 %self_attention.1 = (f32[256,1024]{1,0:T(8,128)S(1)}, f32[256,1024]{1,0:T(8,128)S(1)}, f32[256,512]{1,0:T(8,128)S(1)}, bf16[128,512]{1,0:T(8,128)(2,1)S(1)}) custom-call(s32[1]{0:T(128)} %bitcast.me_ref.rank_ref, bf16[256,1024]{1,0:T(8,128)(2,1)S(1)} %copy-done, bf16[256,256]{1,0:T(8,128)(2,1)S(1)} %copy-done.2, bf16[256,256]{1,0:T(8,128)(2,1)S(1)} %copy-done.3, ...), custom_call_target="tpu_custom_call" | custom-call | flops 1000000 | bytes 10000 | tf_op jit(solution)/shard_map/self_attention/pallas_call | solution.py:394
  27.2 0.8 %collective-permute-done.13.refs_2_ = bf16[64,512]{1,0:T(8,128)(2,1)S(1)} collective-permute-done((bf16[64,512]{1,0:T(8,128)(2,1)S(1)}, bf16[64,512]{1,0:T(8,128)(2,1)S(1)}, u32[]{:S(2)}, u32[]{:S(2)}) %collective-permute-start.13) | collective-permute-done | bytes 65568 | tf_op jit(solution)/shard_map/ppermute | solution.py:409
  28.0 1.2 %collective-permute-done.14.refs_3_ = bf16[64,512]{1,0:T(8,128)(2,1)S(1)} collective-permute-done((bf16[64,512]{1,0:T(8,128)(2,1)S(1)}, bf16[64,512]{1,0:T(8,128)(2,1)S(1)}, u32[]{:S(2)}, u32[]{:S(2)}) %collective-permute-start.14) | collective-permute-done | bytes 65568 | tf_op jit(solution)/shard_map/ppermute | solution.py:409
  29.2 0.8 %cross_attention.1 = (bf16[64,512]{1,0:T(8,128)(2,1)S(1)}, bf16[64,512]{1,0:T(8,128)(2,1)S(1)}, bf16[64,512]{1,0:T(8,128)(2,1)S(1)}, bf16[64,512]{1,0:T(8,128)(2...) custom-call(bf16[256,1024]{1,0:T(8,128)(2,1)S(1)} %copy-done, bf16[256,1024]{1,0:T(8,128)(2,1)S(1)} %copy-done.1, ...), custom_call_target="tpu_custom_call" | custom-call | flops 600000000 | bytes 3000000 | tf_op jit(solution)/shard_map/cross_attention/pallas_call | solution.py:394
  29.9 0.8 %collective-permute-start.17 = (bf16[64,512]{1,0:T(8,128)(2,1)S(1)}, bf16[64,512]{1,0:T(8,128)(2,1)S(1)}, u32[]{:S(2)}, u32[]{:S(2)}) collective-permute-start(bf16[64,512]{1,0:T(8,128)(2,1)S(1)} %get-tuple-element.79), channel_id=1, source_target_pairs={{0,1},{1,0},{2,3},{3,2},{4,5},{5,4},{6,7},{7,6},{8,9},{9,8},{10,11... | collective-permute-start | bytes 196616 | tf_op jit(solution)/shard_map/ppermute | solution.py:409
  30.7 0.8 %collective-permute-start.19 = (bf16[128,512]{1,0:T(8,128)(2,1)S(1)}, bf16[128,512]{1,0:T(8,128)(2,1)S(1)}, u32[]{:S(2)}, u32[]{:S(2)}) collective-permute-start(bf16[128,512]{1,0:T(8,128)(2,1)S(1)} %get-tuple-element.95), channel_id=1, source_target_pairs={{4,0},{8,4},{12,8},{16,12},{20,16},{24,20},{28,24},{0,28},{5,1},{9... | collective-permute-start | bytes 393224 | tf_op jit(solution)/shard_map/ppermute | solution.py:548
  31.6 1.6 %collective-permute-start.15 = (bf16[64,512]{1,0:T(8,128)(2,1)S(1)}, bf16[64,512]{1,0:T(8,128)(2,1)S(1)}, u32[]{:S(2)}, u32[]{:S(2)}) collective-permute-start(bf16[64,512]{1,0:T(8,128)(2,1)S(1)} %get-tuple-element.77), channel_id=1, source_target_pairs={{0,2},{1,3},{2,0},{3,1},{4,6},{5,7},{6,4},{7,5},{8,10},{9,11},{10,... | collective-permute-start | bytes 196616 | tf_op jit(solution)/shard_map/ppermute | solution.py:409
  33.2 1.7 %collective-permute-start.16 = (bf16[64,512]{1,0:T(8,128)(2,1)S(1)}, bf16[64,512]{1,0:T(8,128)(2,1)S(1)}, u32[]{:S(2)}, u32[]{:S(2)}) collective-permute-start(bf16[64,512]{1,0:T(8,128)(2,1)S(1)} %get-tuple-element.78), channel_id=1, source_target_pairs={{0,3},{1,2},{2,1},{3,0},{4,7},{5,6},{6,5},{7,4},{8,11},{9,10},{10,... | collective-permute-start | bytes 196616 | tf_op jit(solution)/shard_map/ppermute | solution.py:409
  35.1 1.0 %collective-permute-start.18 = (bf16[32,1024]{1,0:T(8,128)(2,1)S(1)}, bf16[32,1024]{1,0:T(8,128)(2,1)S(1)}, u32[]{:S(2)}, u32[]{:S(2)}) collective-permute-start(bf16[32,1024]{1,0:T(8,128)(2,1)S(1)} %get-tuple-element.81), channel_id=1, source_target_pairs={{0,8},{4,12},{8,0},{12,4},{16,24},{20,28},{24,16},{28,20},{1,9},{5... | collective-permute-start | bytes 196616 | tf_op jit(solution)/shard_map/ppermute | solution.py:409
  36.1 1.1 %collective-permute-start.24 = (bf16[32,1024]{1,0:T(8,128)(2,1)S(1)}, bf16[32,1024]{1,0:T(8,128)(2,1)S(1)}, u32[]{:S(2)}, u32[]{:S(2)}) collective-permute-start(bf16[32,1024]{1,0:T(8,128)(2,1)S(1)} %get-tuple-element.107), channel_id=1, source_target_pairs={{0,24},{4,28},{8,16},{12,20},{16,8},{20,12},{24,0},{28,4},{1,25},{... | collective-permute-start | bytes 196616 | tf_op jit(solution)/shard_map/ppermute | solution.py:409
  37.2 2.5 %collective-permute-done.15.refs_0_ = bf16[64,512]{1,0:T(8,128)(2,1)S(1)} collective-permute-done((bf16[64,512]{1,0:T(8,128)(2,1)S(1)}, bf16[64,512]{1,0:T(8,128)(2,1)S(1)}, u32[]{:S(2)}, u32[]{:S(2)}) %collective-permute-start.15) | collective-permute-done | bytes 65568 | tf_op jit(solution)/shard_map/ppermute | solution.py:409
  40.3 1.2 %collective-permute-start.21 = (bf16[32,1024]{1,0:T(8,128)(2,1)S(1)}, bf16[32,1024]{1,0:T(8,128)(2,1)S(1)}, u32[]{:S(2)}, u32[]{:S(2)}) collective-permute-start(bf16[32,1024]{1,0:T(8,128)(2,1)S(1)} %get-tuple-element.103), channel_id=1, source_target_pairs={{0,24},{4,28},{8,16},{12,20},{16,8},{20,12},{24,0},{28,4},{1,25},{... | collective-permute-start | bytes 196616 | tf_op jit(solution)/shard_map/ppermute | solution.py:409
  41.5 1.9 %collective-permute-start.22 = (bf16[32,1024]{1,0:T(8,128)(2,1)S(1)}, bf16[32,1024]{1,0:T(8,128)(2,1)S(1)}, u32[]{:S(2)}, u32[]{:S(2)}) collective-permute-start(bf16[32,1024]{1,0:T(8,128)(2,1)S(1)} %get-tuple-element.104), channel_id=1, source_target_pairs={{0,8},{4,12},{8,0},{12,4},{16,24},{20,28},{24,16},{28,20},{1,9},{5... | collective-permute-start | bytes 196616 | tf_op jit(solution)/shard_map/ppermute | solution.py:409
  43.9 1.6 %join_outputs.1 = (bf16[256,1024]{1,0:T(8,128)(2,1)}, bf16[256,1024]{1,0:T(8,128)(2,1)}, bf16[256,256]{1,0:T(8,128)(2,1)}, bf16[256,256]{1,0:T(8,128)(2,1)}) custom-call(bf16[8,64,256]{2,1,0:T(8,128)(2,1)S(1)} %get-tuple-element.90.w_ref, bf16[8,64,256]{2,1,0:T(8,128)(2,1)S(1)} %get-tuple-element.91.ds_ref, f32[256,1024]{1,0:T(8,128)S(1)} %get-tuple-element.92.out_ref, ...), custom_call_target="tpu_custom_call" | custom-call | flops 300000000 | bytes 5000000 | tf_op jit(solution)/shard_map/join_outputs/pallas_call | solution.py:394
  45.6 0.8 %collective-permute-done.22.refs_2_ = bf16[32,1024]{1,0:T(8,128)(2,1)S(1)} collective-permute-done((bf16[32,1024]{1,0:T(8,128)(2,1)S(1)}, bf16[32,1024]{1,0:T(8,128)(2,1)S(1)}, u32[]{:S(2)}, u32[]{:S(2)}) %collective-permute-start.22) | collective-permute-done | bytes 65568 | tf_op jit(solution)/shard_map/ppermute | solution.py:409
  46.4 1.3 %collective-permute-done.23.refs_3_ = bf16[32,1024]{1,0:T(8,128)(2,1)S(1)} collective-permute-done((bf16[32,1024]{1,0:T(8,128)(2,1)S(1)}, bf16[32,1024]{1,0:T(8,128)(2,1)S(1)}, u32[]{:S(2)}, u32[]{:S(2)}) %collective-permute-start.23) | collective-permute-done | bytes 65568 | tf_op jit(solution)/shard_map/ppermute | solution.py:409
  48.3 1.0 %collective-permute-done.20.other_ref = s32[1,128]{1,0:T(1,128)S(1)} collective-permute-done((s32[1,128]{1,0:T(1,128)S(1)}, s32[1,128]{1,0:T(1,128)S(1)}, u32[]{:S(2)}, u32[]{:S(2)}) %collective-permute-start.20) | collective-permute-done | bytes 544 | tf_op jit(solution)/shard_map/ppermute | solution.py:409
  49.4 1.3 %sum_store_gradients.1 = (bf16[64,4,1024]{2,1,0:T(4,128)(2,1)}, bf16[64,4,1024]{2,1,0:T(4,128)(2,1)}) custom-call(s32[1]{0:T(128)} %bitcast.1.z_ref, s32[1,128]{1,0:T(1,128)S(1)} %get-tuple-element.101.target_ref, s32[1,128]{1,0:T(1,128)S(1)} %collective-permute-done.20.other_ref, bf16[64,2048]{1,0:T(8,128)(2,1)S(1)} %get-tuple-element.110.same_rows, ...), custom_call_target="tpu_custom_call" | custom-call | flops 200000000 | bytes 2000000 | tf_op jit(solution)/shard_map/sum_store_gradients/pallas_call | solution.py:394
  (42 shorter events, 4.1 us)
Async XLA Ops:
  0.6 6.1 %collective-permute-start = (bf16[64,4,1024]{2,1,0:T(4,128)(2,1)}, bf16[64,4,1024]{2,1,0:T(4,128)(2,1)S(1)}, u32[]{:S(2)}, u32[]{:S(2)}) collective-permute-start(bf16[64,4,1024]{2,1,0:T(4,128)(2,1)} %k_any.1), channel_id=1, source_target_pairs={{0,4},{4,0},{8,12},{12,8},{16,20},{20,16},{24,28},{28,24},{1,5},{5... | collective-permute-start | bytes 1572872 | tf_op jit(solution)/shard_map/ppermute | solution.py:409
  1.1 5.6 %collective-permute-start.1 = (bf16[64,4,1024]{2,1,0:T(4,128)(2,1)}, bf16[64,4,1024]{2,1,0:T(4,128)(2,1)S(1)}, u32[]{:S(2)}, u32[]{:S(2)}) collective-permute-start(bf16[64,4,1024]{2,1,0:T(4,128)(2,1)} %v_any.1), channel_id=1, source_target_pairs={{0,4},{4,0},{8,12},{12,8},{16,20},{20,16},{24,28},{28,24},{1,5},{5... | collective-permute-start | bytes 1572872 | tf_op jit(solution)/shard_map/ppermute | solution.py:409
  2.2 6.2 %collective-permute-start.2 = (s32[8,128]{1,0:T(8,128)S(1)}, s32[8,128]{1,0:T(8,128)S(1)}, u32[]{:S(2)}, u32[]{:S(2)}) collective-permute-start(s32[8,128]{1,0:T(8,128)S(1)} %plan_requests.1.refs_0_), channel_id=1, source_target_pairs={{0,24},{4,28},{8,16},{12,20},{16,8},{20,12},{24,0},{28,4},{1,25},{... | collective-permute-start | bytes 12296 | tf_op jit(solution)/shard_map/ppermute | solution.py:409
  6.1 3.6 %collective-permute-start.3 = (s32[8,128]{1,0:T(8,128)S(1)}, s32[8,128]{1,0:T(8,128)S(1)}, u32[]{:S(2)}, u32[]{:S(2)}) collective-permute-start(s32[8,128]{1,0:T(8,128)S(1)} %plan_requests.1.refs_0_), channel_id=1, source_target_pairs={{0,8},{4,12},{8,0},{12,4},{16,24},{20,28},{24,16},{28,20},{1,9},{5... | collective-permute-start | bytes 12296 | tf_op jit(solution)/shard_map/ppermute | solution.py:409
  6.6 3.6 %collective-permute-start.4 = (s32[8,128]{1,0:T(8,128)S(1)}, s32[8,128]{1,0:T(8,128)S(1)}, u32[]{:S(2)}, u32[]{:S(2)}) collective-permute-start(s32[8,128]{1,0:T(8,128)S(1)} %plan_requests.1.refs_0_), channel_id=1, source_target_pairs={{0,16},{4,20},{8,24},{12,28},{16,0},{20,4},{24,8},{28,12},{1,17},{... | collective-permute-start | bytes 12296 | tf_op jit(solution)/shard_map/ppermute | solution.py:409
  6.7 17.5 %copy-start = (bf16[256,1024]{1,0:T(8,128)(2,1)S(1)}, bf16[256,1024]{1,0:T(8,128)(2,1)}, u32[]{:S(2)}) copy-start(bf16[256,1024]{1,0:T(8,128)(2,1)} %q_ref.3) | copy-start | bytes 1572868
  6.7 17.5 %copy-start.1 = (bf16[256,1024]{1,0:T(8,128)(2,1)S(1)}, bf16[256,1024]{1,0:T(8,128)(2,1)}, u32[]{:S(2)}) copy-start(bf16[256,1024]{1,0:T(8,128)(2,1)} %do_ref.3) | copy-start | bytes 1572868
  6.8 17.5 %copy-start.2 = (bf16[256,256]{1,0:T(8,128)(2,1)S(1)}, bf16[256,256]{1,0:T(8,128)(2,1)}, u32[]{:S(2)}) copy-start(bf16[256,256]{1,0:T(8,128)(2,1)} %k_ref.1) | copy-start | bytes 393220
  6.8 17.5 %copy-start.3 = (bf16[256,256]{1,0:T(8,128)(2,1)S(1)}, bf16[256,256]{1,0:T(8,128)(2,1)}, u32[]{:S(2)}) copy-start(bf16[256,256]{1,0:T(8,128)(2,1)} %v_ref.1) | copy-start | bytes 393220
  10.7 5.0 %collective-permute-start.10 = (bf16[32,1024]{1,0:T(8,128)(2,1)S(1)}, bf16[32,1024]{1,0:T(8,128)(2,1)S(1)}, u32[]{:S(2)}, u32[]{:S(2)}) collective-permute-start(bf16[32,1024]{1,0:T(8,128)(2,1)S(1)} %get-tuple-element.70), channel_id=1, source_target_pairs={{0,16},{4,20},{8,24},{12,28},{16,0},{20,4},{24,8},{28,12},{1,17},{... | collective-permute-start | bytes 196616 | tf_op jit(solution)/shard_map/ppermute | solution.py:409
  10.9 5.7 %collective-permute-start.8 = (bf16[32,1024]{1,0:T(8,128)(2,1)S(1)}, bf16[32,1024]{1,0:T(8,128)(2,1)S(1)}, u32[]{:S(2)}, u32[]{:S(2)}) collective-permute-start(bf16[32,1024]{1,0:T(8,128)(2,1)S(1)} %get-tuple-element.68), channel_id=1, source_target_pairs={{0,24},{4,28},{8,16},{12,20},{16,8},{20,12},{24,0},{28,4},{1,25},{... | collective-permute-start | bytes 196616 | tf_op jit(solution)/shard_map/ppermute | solution.py:409
  13.7 4.9 %collective-permute-start.9 = (bf16[32,1024]{1,0:T(8,128)(2,1)S(1)}, bf16[32,1024]{1,0:T(8,128)(2,1)S(1)}, u32[]{:S(2)}, u32[]{:S(2)}) collective-permute-start(bf16[32,1024]{1,0:T(8,128)(2,1)S(1)} %get-tuple-element.69), channel_id=1, source_target_pairs={{0,8},{4,12},{8,0},{12,4},{16,24},{20,28},{24,16},{28,20},{1,9},{5... | collective-permute-start | bytes 196616 | tf_op jit(solution)/shard_map/ppermute | solution.py:409
  14.3 10.0 %collective-permute-start.12 = (bf16[128,512]{1,0:T(8,128)(2,1)S(1)}, bf16[128,512]{1,0:T(8,128)(2,1)S(1)}, u32[]{:S(2)}, u32[]{:S(2)}) collective-permute-start(bf16[128,512]{1,0:T(8,128)(2,1)S(1)} %get-tuple-element.72), channel_id=1, source_target_pairs={{0,4},{4,8},{8,12},{12,16},{16,20},{20,24},{24,28},{28,0},{1,5},{5... | collective-permute-start | bytes 393224 | tf_op jit(solution)/shard_map/ppermute | solution.py:532
  14.3 7.3 %collective-permute-start.5 = (bf16[32,1024]{1,0:T(8,128)(2,1)S(1)}, bf16[32,1024]{1,0:T(8,128)(2,1)S(1)}, u32[]{:S(2)}, u32[]{:S(2)}) collective-permute-start(bf16[32,1024]{1,0:T(8,128)(2,1)S(1)} %get-tuple-element.63), channel_id=1, source_target_pairs={{0,24},{4,28},{8,16},{12,20},{16,8},{20,12},{24,0},{28,4},{1,25},{... | collective-permute-start | bytes 196616 | tf_op jit(solution)/shard_map/ppermute | solution.py:409
  15.7 8.0 %collective-permute-start.6 = (bf16[32,1024]{1,0:T(8,128)(2,1)S(1)}, bf16[32,1024]{1,0:T(8,128)(2,1)S(1)}, u32[]{:S(2)}, u32[]{:S(2)}) collective-permute-start(bf16[32,1024]{1,0:T(8,128)(2,1)S(1)} %get-tuple-element.64), channel_id=1, source_target_pairs={{0,8},{4,12},{8,0},{12,4},{16,24},{20,28},{24,16},{28,20},{1,9},{5... | collective-permute-start | bytes 196616 | tf_op jit(solution)/shard_map/ppermute | solution.py:409
  16.6 7.2 %collective-permute-start.7 = (bf16[32,1024]{1,0:T(8,128)(2,1)S(1)}, bf16[32,1024]{1,0:T(8,128)(2,1)S(1)}, u32[]{:S(2)}, u32[]{:S(2)}) collective-permute-start(bf16[32,1024]{1,0:T(8,128)(2,1)S(1)} %get-tuple-element.65), channel_id=1, source_target_pairs={{0,16},{4,20},{8,24},{12,28},{16,0},{20,4},{24,8},{28,12},{1,17},{... | collective-permute-start | bytes 196616 | tf_op jit(solution)/shard_map/ppermute | solution.py:409
  18.9 8.3 %collective-permute-start.11 = (bf16[64,512]{1,0:T(8,128)(2,1)S(1)}, bf16[64,512]{1,0:T(8,128)(2,1)S(1)}, u32[]{:S(2)}, u32[]{:S(2)}) collective-permute-start(bf16[64,512]{1,0:T(8,128)(2,1)S(1)} %get-tuple-element.71), channel_id=1, source_target_pairs={{0,2},{1,3},{2,0},{3,1},{4,6},{5,7},{6,4},{7,5},{8,10},{9,11},{10,... | collective-permute-start | bytes 196616 | tf_op jit(solution)/shard_map/ppermute | solution.py:409
  21.6 6.4 %collective-permute-start.13 = (bf16[64,512]{1,0:T(8,128)(2,1)S(1)}, bf16[64,512]{1,0:T(8,128)(2,1)S(1)}, u32[]{:S(2)}, u32[]{:S(2)}) collective-permute-start(bf16[64,512]{1,0:T(8,128)(2,1)S(1)} %get-tuple-element.75), channel_id=1, source_target_pairs={{0,3},{1,2},{2,1},{3,0},{4,7},{5,6},{6,5},{7,4},{8,11},{9,10},{10,... | collective-permute-start | bytes 196616 | tf_op jit(solution)/shard_map/ppermute | solution.py:409
  24.0 5.2 %collective-permute-start.14 = (bf16[64,512]{1,0:T(8,128)(2,1)S(1)}, bf16[64,512]{1,0:T(8,128)(2,1)S(1)}, u32[]{:S(2)}, u32[]{:S(2)}) collective-permute-start(bf16[64,512]{1,0:T(8,128)(2,1)S(1)} %get-tuple-element.76), channel_id=1, source_target_pairs={{0,1},{1,0},{2,3},{3,2},{4,5},{5,4},{6,7},{7,6},{8,9},{9,8},{10,11... | collective-permute-start | bytes 196616 | tf_op jit(solution)/shard_map/ppermute | solution.py:409
  29.9 5.0 %collective-permute-start.17 = (bf16[64,512]{1,0:T(8,128)(2,1)S(1)}, bf16[64,512]{1,0:T(8,128)(2,1)S(1)}, u32[]{:S(2)}, u32[]{:S(2)}) collective-permute-start(bf16[64,512]{1,0:T(8,128)(2,1)S(1)} %get-tuple-element.79), channel_id=1, source_target_pairs={{0,1},{1,0},{2,3},{3,2},{4,5},{5,4},{6,7},{7,6},{8,9},{9,8},{10,11... | collective-permute-start | bytes 196616 | tf_op jit(solution)/shard_map/ppermute | solution.py:409
  30.7 12.7 %collective-permute-start.19 = (bf16[128,512]{1,0:T(8,128)(2,1)S(1)}, bf16[128,512]{1,0:T(8,128)(2,1)S(1)}, u32[]{:S(2)}, u32[]{:S(2)}) collective-permute-start(bf16[128,512]{1,0:T(8,128)(2,1)S(1)} %get-tuple-element.95), channel_id=1, source_target_pairs={{4,0},{8,4},{12,8},{16,12},{20,16},{24,20},{28,24},{0,28},{5,1},{9... | collective-permute-start | bytes 393224 | tf_op jit(solution)/shard_map/ppermute | solution.py:548
  31.6 8.1 %collective-permute-start.15 = (bf16[64,512]{1,0:T(8,128)(2,1)S(1)}, bf16[64,512]{1,0:T(8,128)(2,1)S(1)}, u32[]{:S(2)}, u32[]{:S(2)}) collective-permute-start(bf16[64,512]{1,0:T(8,128)(2,1)S(1)} %get-tuple-element.77), channel_id=1, source_target_pairs={{0,2},{1,3},{2,0},{3,1},{4,6},{5,7},{6,4},{7,5},{8,10},{9,11},{10,... | collective-permute-start | bytes 196616 | tf_op jit(solution)/shard_map/ppermute | solution.py:409
  33.2 6.9 %collective-permute-start.16 = (bf16[64,512]{1,0:T(8,128)(2,1)S(1)}, bf16[64,512]{1,0:T(8,128)(2,1)S(1)}, u32[]{:S(2)}, u32[]{:S(2)}) collective-permute-start(bf16[64,512]{1,0:T(8,128)(2,1)S(1)} %get-tuple-element.78), channel_id=1, source_target_pairs={{0,3},{1,2},{2,1},{3,0},{4,7},{5,6},{6,5},{7,4},{8,11},{9,10},{10,... | collective-permute-start | bytes 196616 | tf_op jit(solution)/shard_map/ppermute | solution.py:409
  35.1 5.0 %collective-permute-start.18 = (bf16[32,1024]{1,0:T(8,128)(2,1)S(1)}, bf16[32,1024]{1,0:T(8,128)(2,1)S(1)}, u32[]{:S(2)}, u32[]{:S(2)}) collective-permute-start(bf16[32,1024]{1,0:T(8,128)(2,1)S(1)} %get-tuple-element.81), channel_id=1, source_target_pairs={{0,8},{4,12},{8,0},{12,4},{16,24},{20,28},{24,16},{28,20},{1,9},{5... | collective-permute-start | bytes 196616 | tf_op jit(solution)/shard_map/ppermute | solution.py:409
  36.1 9.4 %collective-permute-start.24 = (bf16[32,1024]{1,0:T(8,128)(2,1)S(1)}, bf16[32,1024]{1,0:T(8,128)(2,1)S(1)}, u32[]{:S(2)}, u32[]{:S(2)}) collective-permute-start(bf16[32,1024]{1,0:T(8,128)(2,1)S(1)} %get-tuple-element.107), channel_id=1, source_target_pairs={{0,24},{4,28},{8,16},{12,20},{16,8},{20,12},{24,0},{28,4},{1,25},{... | collective-permute-start | bytes 196616 | tf_op jit(solution)/shard_map/ppermute | solution.py:409
  39.7 5.8 %collective-permute-start.25 = (bf16[32,1024]{1,0:T(8,128)(2,1)S(1)}, bf16[32,1024]{1,0:T(8,128)(2,1)S(1)}, u32[]{:S(2)}, u32[]{:S(2)}) collective-permute-start(bf16[32,1024]{1,0:T(8,128)(2,1)S(1)} %get-tuple-element.109), channel_id=1, source_target_pairs={{0,16},{4,20},{8,24},{12,28},{16,0},{20,4},{24,8},{28,12},{1,17},{... | collective-permute-start | bytes 196616 | tf_op jit(solution)/shard_map/ppermute | solution.py:409
  40.3 5.2 %collective-permute-start.21 = (bf16[32,1024]{1,0:T(8,128)(2,1)S(1)}, bf16[32,1024]{1,0:T(8,128)(2,1)S(1)}, u32[]{:S(2)}, u32[]{:S(2)}) collective-permute-start(bf16[32,1024]{1,0:T(8,128)(2,1)S(1)} %get-tuple-element.103), channel_id=1, source_target_pairs={{0,24},{4,28},{8,16},{12,20},{16,8},{20,12},{24,0},{28,4},{1,25},{... | collective-permute-start | bytes 196616 | tf_op jit(solution)/shard_map/ppermute | solution.py:409
  41.5 4.9 %collective-permute-start.22 = (bf16[32,1024]{1,0:T(8,128)(2,1)S(1)}, bf16[32,1024]{1,0:T(8,128)(2,1)S(1)}, u32[]{:S(2)}, u32[]{:S(2)}) collective-permute-start(bf16[32,1024]{1,0:T(8,128)(2,1)S(1)} %get-tuple-element.104), channel_id=1, source_target_pairs={{0,8},{4,12},{8,0},{12,4},{16,24},{20,28},{24,16},{28,20},{1,9},{5... | collective-permute-start | bytes 196616 | tf_op jit(solution)/shard_map/ppermute | solution.py:409
  43.4 4.3 %collective-permute-start.23 = (bf16[32,1024]{1,0:T(8,128)(2,1)S(1)}, bf16[32,1024]{1,0:T(8,128)(2,1)S(1)}, u32[]{:S(2)}, u32[]{:S(2)}) collective-permute-start(bf16[32,1024]{1,0:T(8,128)(2,1)S(1)} %get-tuple-element.105), channel_id=1, source_target_pairs={{0,16},{4,20},{8,24},{12,28},{16,0},{20,4},{24,8},{28,12},{1,17},{... | collective-permute-start | bytes 196616 | tf_op jit(solution)/shard_map/ppermute | solution.py:409
  47.8 1.6 %collective-permute-start.26 = (bf16[64,2048]{1,0:T(8,128)(2,1)S(1)}, bf16[64,2048]{1,0:T(8,128)(2,1)S(1)}, u32[]{:S(2)}, u32[]{:S(2)}) collective-permute-start(bf16[64,2048]{1,0:T(8,128)(2,1)S(1)} %get-tuple-element.111), channel_id=1, source_target_pairs={{0,4},{4,0},{8,12},{12,8},{16,20},{20,16},{24,28},{28,24},{1,5},{5... | collective-permute-start | bytes 786440 | tf_op jit(solution)/shard_map/ppermute | solution.py:409
  47.8 1.5 %collective-permute-start.20 = (s32[1,128]{1,0:T(1,128)S(1)}, s32[1,128]{1,0:T(1,128)S(1)}, u32[]{:S(2)}, u32[]{:S(2)}) collective-permute-start(s32[1,128]{1,0:T(1,128)S(1)} %get-tuple-element.101.target_ref), channel_id=1, source_target_pairs={{0,4},{4,0},{8,12},{12,8},{16,20},{20,16},{24,28},{28,24},{1,5},{5... | collective-permute-start | bytes 1544 | tf_op jit(solution)/shard_map/ppermute | solution.py:409

commit v6 on v5

--- a/solution.py
+++ b/solution.py
@@ -169,7 +169,7 @@
         by_chip(refs[2 * pieces : 3 * pieces]),
         refs[-1],
     )
-    rows, columns = store_ref.shape[0], store_ref.shape[1] // 2
+    rows = store_ref.shape[0]
     lanes = target_ref.shape[1]
     width = wanted_refs[0].shape[1]
     me = me_ref[0]
@@ -187,8 +187,8 @@
     target = jnp.where(target >= 0, target + second * (rows // 2), -1)
     row = lax.broadcasted_iota(jnp.int32, (rows, lanes), 0)
     picks = jnp.where(row == target, 1.0, 0.0).astype(BF16)
-    for half, send_refs in enumerate((far_refs, near_refs)):
-        cols = slice(half * columns, (half + 1) * columns)
+    split = far_refs[0].shape[1]
+    for cols, send_refs in ((slice(0, split), far_refs), (slice(split, None), near_refs)):
         picked = dot_tn(picks, store_ref[:, cols]).astype(BF16)
         for m, send_ref in enumerate(send_refs):
             send_ref[...] = picked[2 * m * rows_each : 2 * (m + 1) * rows_each]
@@ -511,23 +511,32 @@
         functools.partial(pack_kernel, rows_each),
         "pack_requests",
         (rank, store, *pieces),
-        [block] * (2 * chips) + [struct((1, lanes), int32)],
+        [struct((2 * rows_each, (tp - 1) * both), BF16)] * chips
+        + [struct((2 * rows_each, both), BF16)] * chips
+        + [struct((1, lanes), int32)],
         200_000_000,
         2_000_000,
         scalars=1,
     )
     parts = tp // 2
-    moved = []
-    far, near = between_chips(sent[:chips]), sent[chips:]
-    for name, got in (("spread_far", far), ("spread_near", between_chips(near))):
-        moved += call(
-            functools.partial(spread_kernel, parts),
-            name,
-            (placed, *got),
-            [struct((used, both), BF16)] * parts,
-            1_000_000,
-            10_000,
-        )
+    far, near = sent[:chips], sent[chips:]
+    moved = call(
+        functools.partial(spread_kernel, tp - 1),
+        "spread_far",
+        (placed, *between_chips(far)),
+        [struct((used, both), BF16)] * (tp - 1),
+        1_000_000,
+        10_000,
+    )
+    moved = list(moved)
+    moved += call(
+        functools.partial(spread_kernel, 1),
+        "spread_near",
+        (placed, *between_chips(near)),
+        [struct((used, both), BF16)],
+        1_000_000,
+        10_000,
+    )
     near = exchanged(moved[-1:] + moved[:-1])
     halo = lax.ppermute(halo, "seq", [(i, (i + 1) % devices) for i in range(devices)])
     other_target = swapped(target, "seq", 1)
@@ -564,7 +573,9 @@
     returned = []
     for name, half in (("scatter_near", grads[parts:]), ("scatter_far", grads[:parts])):
         if returned:
-            half, returned[2] = lax.optimization_barrier((half, returned[2]))
+            half, returned[2], other_target = lax.optimization_barrier(
+                (half, returned[2], other_target)
+            )
         sent = call(
             functools.partial(scatter_kernel, chips),
             name,

time: 50.8 us -> 53.6 us (1.055)
  starting transfers between devices: 29.2 us -> 30.9 us
  waiting for transfers between devices: 10.3 us -> 11.3 us
    ppermute x25, starting transfers between devices: 28.4 us -> 30.9 us  [swapped(): lax.ppermute(block, axis, [(i, i ^ apart) for i in range(lax.axis_size(ax...]
    ppermute x25, waiting for transfers between devices: 10.3 us -> 11.3 us  [swapped(): lax.ppermute(block, axis, [(i, i ^ apart) for i in range(lax.axis_size(ax...]
    ppermute x1, starting transfers between devices: 0.84 us -> 0.01 us  [body(): lax.ppermute(back, 'seq', [((i + 1) % devices, i) for i in range(devices)])]
  transfers between devices with their start and end apart: 27 -> 27, of which waited for: 10 -> 10; matrix products, arithmetic and copies ran while one was open for 0% -> 0% of each run, Pallas kernels for 15% -> 14%
where the time goes in v6:
time: 53.6 us; the launch traced here: 53.4 us
  starting transfers between devices  30.9 us (58%)
  waiting for transfers between devices  11.3 us (21%)
  Pallas kernels  10.3 us (19%)
  between operations  0.85 us (2%)
    ppermute x25, starting transfers between devices, swapped(): lax.ppermute(block, axis, [(i, i ^ apart) for i in range(lax.axis_size(ax...  30.9 us
    ppermute x25, waiting for transfers between devices, swapped(): lax.ppermute(block, axis, [(i, i ^ apart) for i in range(lax.axis_size(ax...  11.3 us
    pallas_call x12, Pallas kernels, call(): pl.pallas_call(kernel, out_shape=tuple(outs), in_specs=[SMEM] * scalars +...  10.3 us
  transfers between devices with their start and end apart: 27, of which 10 were waited for; matrix products, arithmetic and copies ran while one was open for 0% of the time, Pallas kernels for 14%

profile of v6, /device:TPU:0, one launch (start us, length us, event | category | flops | bytes accessed | tf_op | source)
XLA Modules:
  0.0 53.4 jit_solution(6092180549645363075)
XLA Ops:
  0.6 0.5 collective-permute-start
  1.2 0.9 %plan_requests.1.refs_0_ = s32[8,128]{1,0:T(8,128)S(1)} custom-call(s32[4,4]{1,0:T(4,128)} %owner_any.3, s32[4,4]{1,0:T(4,128)} %slot_any.1), custom_call_target="tpu_custom_call" | custom-call | bytes 100000 | tf_op jit(solution)/shard_map/plan_requests/pallas_call | solution.py:394
  2.2 3.0 %collective-permute-start.4 = (s32[8,128]{1,0:T(8,128)S(1)}, s32[8,128]{1,0:T(8,128)S(1)}, u32[]{:S(2)}, u32[]{:S(2)}) collective-permute-start(s32[8,128]{1,0:T(8,128)S(1)} %plan_requests.1.refs_0_), channel_id=1, source_target_pairs={{0,16},{4,20},{8,24},{12,28},{16,0},{20,4},{24,8},{28,12},{1,17},{... | collective-permute-start | bytes 12296 | tf_op jit(solution)/shard_map/ppermute | solution.py:409
  5.2 1.5 %collective-permute-start.3 = (s32[8,128]{1,0:T(8,128)S(1)}, s32[8,128]{1,0:T(8,128)S(1)}, u32[]{:S(2)}, u32[]{:S(2)}) collective-permute-start(s32[8,128]{1,0:T(8,128)S(1)} %plan_requests.1.refs_0_), channel_id=1, source_target_pairs={{0,8},{4,12},{8,0},{12,4},{16,24},{20,28},{24,16},{28,20},{1,9},{5... | collective-permute-start | bytes 12296 | tf_op jit(solution)/shard_map/ppermute | solution.py:409
  6.8 1.5 %stage_store.1 = (bf16[512,2048]{1,0:T(8,128)(2,1)S(1)}, bf16[128,512]{1,0:T(8,128)(2,1)S(1)}, bf16[128,64]{1,0:T(8,128)(2,1)S(1)}) custom-call(s32[1]{0:T(128)} %bitcast.me_ref.rank_ref, s32[1]{0:T(128)} %bitcast.1.z_ref, bf16[64,4,1024]{2,1,0:T(4,128)(2,1)S(1)} %collective-permute-done.sibling_k_ref, ...), custom_call_target="tpu_custom_call" | custom-call | bytes 5000000 | tf_op jit(solution)/shard_map/stage_store/pallas_call | solution.py:394
  8.3 0.5 collective-permute-done.3.refs_2_
  8.8 2.4 %collective-permute-done.2.refs_1_ = s32[8,128]{1,0:T(8,128)S(1)} collective-permute-done((s32[8,128]{1,0:T(8,128)S(1)}, s32[8,128]{1,0:T(8,128)S(1)}, u32[]{:S(2)}, u32[]{:S(2)}) %collective-permute-start.2) | collective-permute-done | bytes 4128 | tf_op jit(solution)/shard_map/ppermute | solution.py:409
  11.2 0.5 pack_requests.1
  11.8 1.9 %collective-permute-start.9 = (bf16[32,1536]{1,0:T(8,128)(2,1)S(1)}, bf16[32,1536]{1,0:T(8,128)(2,1)S(1)}, u32[]{:S(2)}, u32[]{:S(2)}) collective-permute-start(bf16[32,1536]{1,0:T(8,128)(2,1)S(1)} %get-tuple-element.68), channel_id=1, source_target_pairs={{0,8},{4,12},{8,0},{12,4},{16,24},{20,28},{24,16},{28,20},{1,9},{5... | collective-permute-start | bytes 294920 | tf_op jit(solution)/shard_map/ppermute | solution.py:409
  13.7 1.5 %collective-permute-start.10 = (bf16[32,1536]{1,0:T(8,128)(2,1)S(1)}, bf16[32,1536]{1,0:T(8,128)(2,1)S(1)}, u32[]{:S(2)}, u32[]{:S(2)}) collective-permute-start(bf16[32,1536]{1,0:T(8,128)(2,1)S(1)} %get-tuple-element.69), channel_id=1, source_target_pairs={{0,16},{4,20},{8,24},{12,28},{16,0},{20,4},{24,8},{28,12},{1,17},{... | collective-permute-start | bytes 294920 | tf_op jit(solution)/shard_map/ppermute | solution.py:409
  15.3 1.9 %collective-permute-done.8.refs_1_ = bf16[32,1536]{1,0:T(8,128)(2,1)S(1)} collective-permute-done((bf16[32,1536]{1,0:T(8,128)(2,1)S(1)}, bf16[32,1536]{1,0:T(8,128)(2,1)S(1)}, u32[]{:S(2)}, u32[]{:S(2)}) %collective-permute-start.8) | collective-permute-done | bytes 98336 | tf_op jit(solution)/shard_map/ppermute | solution.py:409
  17.2 0.6 %collective-permute-start.6 = (bf16[32,512]{1,0:T(8,128)(2,1)S(1)}, bf16[32,512]{1,0:T(8,128)(2,1)S(1)}, u32[]{:S(2)}, u32[]{:S(2)}) collective-permute-start(bf16[32,512]{1,0:T(8,128)(2,1)S(1)} %get-tuple-element.64), channel_id=1, source_target_pairs={{0,8},{4,12},{8,0},{12,4},{16,24},{20,28},{24,16},{28,20},{1,9},{5... | collective-permute-start | bytes 98312 | tf_op jit(solution)/shard_map/ppermute | solution.py:409
  17.8 0.5 collective-permute-done.10.refs_3_
  18.5 2.7 %collective-permute-start.11 = (bf16[64,512]{1,0:T(8,128)(2,1)S(1)}, bf16[64,512]{1,0:T(8,128)(2,1)S(1)}, u32[]{:S(2)}, u32[]{:S(2)}) collective-permute-start(bf16[64,512]{1,0:T(8,128)(2,1)S(1)} %get-tuple-element.70), channel_id=1, source_target_pairs={{0,2},{1,3},{2,0},{3,1},{4,6},{5,7},{6,4},{7,5},{8,10},{9,11},{10,... | collective-permute-start | bytes 196616 | tf_op jit(solution)/shard_map/ppermute | solution.py:409
  21.2 1.3 %collective-permute-start.13 = (bf16[64,512]{1,0:T(8,128)(2,1)S(1)}, bf16[64,512]{1,0:T(8,128)(2,1)S(1)}, u32[]{:S(2)}, u32[]{:S(2)}) collective-permute-start(bf16[64,512]{1,0:T(8,128)(2,1)S(1)} %get-tuple-element.74), channel_id=1, source_target_pairs={{0,3},{1,2},{2,1},{3,0},{4,7},{5,6},{6,5},{7,4},{8,11},{9,10},{10,... | collective-permute-start | bytes 196616 | tf_op jit(solution)/shard_map/ppermute | solution.py:409
  22.8 3.6 %collective-permute-start.7 = (bf16[32,512]{1,0:T(8,128)(2,1)S(1)}, bf16[32,512]{1,0:T(8,128)(2,1)S(1)}, u32[]{:S(2)}, u32[]{:S(2)}) collective-permute-start(bf16[32,512]{1,0:T(8,128)(2,1)S(1)} %get-tuple-element.65), channel_id=1, source_target_pairs={{0,16},{4,20},{8,24},{12,28},{16,0},{20,4},{24,8},{28,12},{1,17},{... | collective-permute-start | bytes 98312 | tf_op jit(solution)/shard_map/ppermute | solution.py:409
  26.4 1.9 %collective-permute-done.7.refs_3_ = bf16[32,512]{1,0:T(8,128)(2,1)S(1)} collective-permute-done((bf16[32,512]{1,0:T(8,128)(2,1)S(1)}, bf16[32,512]{1,0:T(8,128)(2,1)S(1)}, u32[]{:S(2)}, u32[]{:S(2)}) %collective-permute-start.7) | collective-permute-done | bytes 32800 | tf_op jit(solution)/shard_map/ppermute | solution.py:409
  28.5 2.9 %self_attention.1 = (f32[256,1024]{1,0:T(8,128)S(1)}, f32[256,1024]{1,0:T(8,128)S(1)}, f32[256,512]{1,0:T(8,128)S(1)}, bf16[128,512]{1,0:T(8,128)(2,1)S(1)}) custom-call(s32[1]{0:T(128)} %bitcast.me_ref.rank_ref, bf16[256,1024]{1,0:T(8,128)(2,1)S(1)} %copy-done, bf16[256,256]{1,0:T(8,128)(2,1)S(1)} %copy-done.2, bf16[256,256]{1,0:T(8,128)(2,1)S(1)} %copy-done.3, ...), custom_call_target="tpu_custom_call" | custom-call | flops 1000000 | bytes 10000 | tf_op jit(solution)/shard_map/self_attention/pallas_call | solution.py:394
  31.5 0.8 %cross_attention.1 = (bf16[64,512]{1,0:T(8,128)(2,1)S(1)}, bf16[64,512]{1,0:T(8,128)(2,1)S(1)}, bf16[64,512]{1,0:T(8,128)(2,1)S(1)}, bf16[64,512]{1,0:T(8,128)(2...) custom-call(bf16[256,1024]{1,0:T(8,128)(2,1)S(1)} %copy-done, bf16[256,1024]{1,0:T(8,128)(2,1)S(1)} %copy-done.1, ...), custom_call_target="tpu_custom_call" | custom-call | flops 600000000 | bytes 3000000 | tf_op jit(solution)/shard_map/cross_attention/pallas_call | solution.py:394
  32.2 1.9 %collective-permute-start.17 = (bf16[64,512]{1,0:T(8,128)(2,1)S(1)}, bf16[64,512]{1,0:T(8,128)(2,1)S(1)}, u32[]{:S(2)}, u32[]{:S(2)}) collective-permute-start(bf16[64,512]{1,0:T(8,128)(2,1)S(1)} %get-tuple-element.78), channel_id=1, source_target_pairs={{0,1},{1,0},{2,3},{3,2},{4,5},{5,4},{6,7},{7,6},{8,9},{9,8},{10,11... | collective-permute-start | bytes 196616 | tf_op jit(solution)/shard_map/ppermute | solution.py:409
  34.1 1.7 %collective-permute-start.15 = (bf16[64,512]{1,0:T(8,128)(2,1)S(1)}, bf16[64,512]{1,0:T(8,128)(2,1)S(1)}, u32[]{:S(2)}, u32[]{:S(2)}) collective-permute-start(bf16[64,512]{1,0:T(8,128)(2,1)S(1)} %get-tuple-element.76), channel_id=1, source_target_pairs={{0,2},{1,3},{2,0},{3,1},{4,6},{5,7},{6,4},{7,5},{8,10},{9,11},{10,... | collective-permute-start | bytes 196616 | tf_op jit(solution)/shard_map/ppermute | solution.py:409
  35.8 0.9 %collective-permute-start.16 = (bf16[64,512]{1,0:T(8,128)(2,1)S(1)}, bf16[64,512]{1,0:T(8,128)(2,1)S(1)}, u32[]{:S(2)}, u32[]{:S(2)}) collective-permute-start(bf16[64,512]{1,0:T(8,128)(2,1)S(1)} %get-tuple-element.77), channel_id=1, source_target_pairs={{0,3},{1,2},{2,1},{3,0},{4,7},{5,6},{6,5},{7,4},{8,11},{9,10},{10,... | collective-permute-start | bytes 196616 | tf_op jit(solution)/shard_map/ppermute | solution.py:409
  37.2 1.0 %collective-permute-done.19.other_ref = s32[1,128]{1,0:T(1,128)S(1)} collective-permute-done((s32[1,128]{1,0:T(1,128)S(1)}, s32[1,128]{1,0:T(1,128)S(1)}, u32[]{:S(2)}, u32[]{:S(2)}) %collective-permute-start.19) | collective-permute-done | bytes 544 | tf_op jit(solution)/shard_map/ppermute | solution.py:409
  38.2 3.4 %collective-permute-start.24 = (bf16[32,1024]{1,0:T(8,128)(2,1)S(1)}, bf16[32,1024]{1,0:T(8,128)(2,1)S(1)}, u32[]{:S(2)}, u32[]{:S(2)}) collective-permute-start(bf16[32,1024]{1,0:T(8,128)(2,1)S(1)} %get-tuple-element.107), channel_id=1, source_target_pairs={{0,24},{4,28},{8,16},{12,20},{16,8},{20,12},{24,0},{28,4},{1,25},{... | collective-permute-start | bytes 196616 | tf_op jit(solution)/shard_map/ppermute | solution.py:409
  41.6 0.8 %collective-permute-done.15.refs_0_ = bf16[64,512]{1,0:T(8,128)(2,1)S(1)} collective-permute-done((bf16[64,512]{1,0:T(8,128)(2,1)S(1)}, bf16[64,512]{1,0:T(8,128)(2,1)S(1)}, u32[]{:S(2)}, u32[]{:S(2)}) %collective-permute-start.15) | collective-permute-done | bytes 65568 | tf_op jit(solution)/shard_map/ppermute | solution.py:409
  42.4 2.0 %collective-permute-start.25 = (bf16[32,1024]{1,0:T(8,128)(2,1)S(1)}, bf16[32,1024]{1,0:T(8,128)(2,1)S(1)}, u32[]{:S(2)}, u32[]{:S(2)}) collective-permute-start(bf16[32,1024]{1,0:T(8,128)(2,1)S(1)} %get-tuple-element.109), channel_id=1, source_target_pairs={{0,16},{4,20},{8,24},{12,28},{16,0},{20,4},{24,8},{28,12},{1,17},{... | collective-permute-start | bytes 196616 | tf_op jit(solution)/shard_map/ppermute | solution.py:409
  44.7 1.5 %collective-permute-start.22 = (bf16[32,1024]{1,0:T(8,128)(2,1)S(1)}, bf16[32,1024]{1,0:T(8,128)(2,1)S(1)}, u32[]{:S(2)}, u32[]{:S(2)}) collective-permute-start(bf16[32,1024]{1,0:T(8,128)(2,1)S(1)} %get-tuple-element.104), channel_id=1, source_target_pairs={{0,8},{4,12},{8,0},{12,4},{16,24},{20,28},{24,16},{28,20},{1,9},{5... | collective-permute-start | bytes 196616 | tf_op jit(solution)/shard_map/ppermute | solution.py:409
  46.1 2.0 %collective-permute-start.23 = (bf16[32,1024]{1,0:T(8,128)(2,1)S(1)}, bf16[32,1024]{1,0:T(8,128)(2,1)S(1)}, u32[]{:S(2)}, u32[]{:S(2)}) collective-permute-start(bf16[32,1024]{1,0:T(8,128)(2,1)S(1)} %get-tuple-element.105), channel_id=1, source_target_pairs={{0,16},{4,20},{8,24},{12,28},{16,0},{20,4},{24,8},{28,12},{1,17},{... | collective-permute-start | bytes 196616 | tf_op jit(solution)/shard_map/ppermute | solution.py:409
  48.2 1.6 %join_outputs.1 = (bf16[256,1024]{1,0:T(8,128)(2,1)}, bf16[256,1024]{1,0:T(8,128)(2,1)}, bf16[256,256]{1,0:T(8,128)(2,1)}, bf16[256,256]{1,0:T(8,128)(2,1)}) custom-call(bf16[8,64,256]{2,1,0:T(8,128)(2,1)S(1)} %get-tuple-element.90.w_ref, bf16[8,64,256]{2,1,0:T(8,128)(2,1)S(1)} %get-tuple-element.91.ds_ref, f32[256,1024]{1,0:T(8,128)S(1)} %get-tuple-element.92.out_ref, ...), custom_call_target="tpu_custom_call" | custom-call | flops 300000000 | bytes 5000000 | tf_op jit(solution)/shard_map/join_outputs/pallas_call | solution.py:394
  49.8 0.7 %collective-permute-done.23.refs_3_ = bf16[32,1024]{1,0:T(8,128)(2,1)S(1)} collective-permute-done((bf16[32,1024]{1,0:T(8,128)(2,1)S(1)}, bf16[32,1024]{1,0:T(8,128)(2,1)S(1)}, u32[]{:S(2)}, u32[]{:S(2)}) %collective-permute-start.23) | collective-permute-done | bytes 65568 | tf_op jit(solution)/shard_map/ppermute | solution.py:409
  50.7 1.5 %collective-permute-done.26.other_rows = bf16[64,2048]{1,0:T(8,128)(2,1)S(1)} collective-permute-done((bf16[64,2048]{1,0:T(8,128)(2,1)S(1)}, bf16[64,2048]{1,0:T(8,128)(2,1)S(1)}, u32[]{:S(2)}, u32[]{:S(2)}) %collective-permute-start.26) | collective-permute-done | bytes 262176 | tf_op jit(solution)/shard_map/ppermute | solution.py:409
  52.2 1.3 %sum_store_gradients.1 = (bf16[64,4,1024]{2,1,0:T(4,128)(2,1)}, bf16[64,4,1024]{2,1,0:T(4,128)(2,1)}) custom-call(s32[1]{0:T(128)} %bitcast.1.z_ref, s32[1,128]{1,0:T(1,128)S(1)} %get-tuple-element.81.target_ref, s32[1,128]{1,0:T(1,128)S(1)} %collective-permute-done.19.other_ref, bf16[64,2048]{1,0:T(8,128)(2,1)S(1)} %get-tuple-element.110.same_rows, ...), custom_call_target="tpu_custom_call" | custom-call | flops 200000000 | bytes 2000000 | tf_op jit(solution)/shard_map/sum_store_gradients/pallas_call | solution.py:394
  (42 shorter events, 1.9 us)
Async XLA Ops:
  0.6 6.1 %collective-permute-start = (bf16[64,4,1024]{2,1,0:T(4,128)(2,1)}, bf16[64,4,1024]{2,1,0:T(4,128)(2,1)S(1)}, u32[]{:S(2)}, u32[]{:S(2)}) collective-permute-start(bf16[64,4,1024]{2,1,0:T(4,128)(2,1)} %k_any.1), channel_id=1, source_target_pairs={{0,4},{4,0},{8,12},{12,8},{16,20},{20,16},{24,28},{28,24},{1,5},{5... | collective-permute-start | bytes 1572872 | tf_op jit(solution)/shard_map/ppermute | solution.py:409
  1.1 5.6 %collective-permute-start.1 = (bf16[64,4,1024]{2,1,0:T(4,128)(2,1)}, bf16[64,4,1024]{2,1,0:T(4,128)(2,1)S(1)}, u32[]{:S(2)}, u32[]{:S(2)}) collective-permute-start(bf16[64,4,1024]{2,1,0:T(4,128)(2,1)} %v_any.1), channel_id=1, source_target_pairs={{0,4},{4,0},{8,12},{12,8},{16,20},{20,16},{24,28},{28,24},{1,5},{5... | collective-permute-start | bytes 1572872 | tf_op jit(solution)/shard_map/ppermute | solution.py:409
  2.2 6.2 %collective-permute-start.4 = (s32[8,128]{1,0:T(8,128)S(1)}, s32[8,128]{1,0:T(8,128)S(1)}, u32[]{:S(2)}, u32[]{:S(2)}) collective-permute-start(s32[8,128]{1,0:T(8,128)S(1)} %plan_requests.1.refs_0_), channel_id=1, source_target_pairs={{0,16},{4,20},{8,24},{12,28},{16,0},{20,4},{24,8},{28,12},{1,17},{... | collective-permute-start | bytes 12296 | tf_op jit(solution)/shard_map/ppermute | solution.py:409
  5.2 3.6 %collective-permute-start.3 = (s32[8,128]{1,0:T(8,128)S(1)}, s32[8,128]{1,0:T(8,128)S(1)}, u32[]{:S(2)}, u32[]{:S(2)}) collective-permute-start(s32[8,128]{1,0:T(8,128)S(1)} %plan_requests.1.refs_0_), channel_id=1, source_target_pairs={{0,8},{4,12},{8,0},{12,4},{16,24},{20,28},{24,16},{28,20},{1,9},{5... | collective-permute-start | bytes 12296 | tf_op jit(solution)/shard_map/ppermute | solution.py:409
  6.7 4.5 %collective-permute-start.2 = (s32[8,128]{1,0:T(8,128)S(1)}, s32[8,128]{1,0:T(8,128)S(1)}, u32[]{:S(2)}, u32[]{:S(2)}) collective-permute-start(s32[8,128]{1,0:T(8,128)S(1)} %plan_requests.1.refs_0_), channel_id=1, source_target_pairs={{0,24},{4,28},{8,16},{12,20},{16,8},{20,12},{24,0},{28,4},{1,25},{... | collective-permute-start | bytes 12296 | tf_op jit(solution)/shard_map/ppermute | solution.py:409
  6.7 21.8 %copy-start = (bf16[256,1024]{1,0:T(8,128)(2,1)S(1)}, bf16[256,1024]{1,0:T(8,128)(2,1)}, u32[]{:S(2)}) copy-start(bf16[256,1024]{1,0:T(8,128)(2,1)} %q_ref.3) | copy-start | bytes 1572868
  6.7 21.8 %copy-start.1 = (bf16[256,1024]{1,0:T(8,128)(2,1)S(1)}, bf16[256,1024]{1,0:T(8,128)(2,1)}, u32[]{:S(2)}) copy-start(bf16[256,1024]{1,0:T(8,128)(2,1)} %do_ref.3) | copy-start | bytes 1572868
  6.7 21.8 %copy-start.2 = (bf16[256,256]{1,0:T(8,128)(2,1)S(1)}, bf16[256,256]{1,0:T(8,128)(2,1)}, u32[]{:S(2)}) copy-start(bf16[256,256]{1,0:T(8,128)(2,1)} %k_ref.1) | copy-start | bytes 393220
  6.7 21.8 %copy-start.3 = (bf16[256,256]{1,0:T(8,128)(2,1)S(1)}, bf16[256,256]{1,0:T(8,128)(2,1)}, u32[]{:S(2)}) copy-start(bf16[256,256]{1,0:T(8,128)(2,1)} %v_ref.1) | copy-start | bytes 393220
  11.7 5.6 %collective-permute-start.8 = (bf16[32,1536]{1,0:T(8,128)(2,1)S(1)}, bf16[32,1536]{1,0:T(8,128)(2,1)S(1)}, u32[]{:S(2)}, u32[]{:S(2)}) collective-permute-start(bf16[32,1536]{1,0:T(8,128)(2,1)S(1)} %get-tuple-element.67), channel_id=1, source_target_pairs={{0,24},{4,28},{8,16},{12,20},{16,8},{20,12},{24,0},{28,4},{1,25},{... | collective-permute-start | bytes 294920 | tf_op jit(solution)/shard_map/ppermute | solution.py:409
  11.8 6.0 %collective-permute-start.9 = (bf16[32,1536]{1,0:T(8,128)(2,1)S(1)}, bf16[32,1536]{1,0:T(8,128)(2,1)S(1)}, u32[]{:S(2)}, u32[]{:S(2)}) collective-permute-start(bf16[32,1536]{1,0:T(8,128)(2,1)S(1)} %get-tuple-element.68), channel_id=1, source_target_pairs={{0,8},{4,12},{8,0},{12,4},{16,24},{20,28},{24,16},{28,20},{1,9},{5... | collective-permute-start | bytes 294920 | tf_op jit(solution)/shard_map/ppermute | solution.py:409
  13.7 4.6 %collective-permute-start.10 = (bf16[32,1536]{1,0:T(8,128)(2,1)S(1)}, bf16[32,1536]{1,0:T(8,128)(2,1)S(1)}, u32[]{:S(2)}, u32[]{:S(2)}) collective-permute-start(bf16[32,1536]{1,0:T(8,128)(2,1)S(1)} %get-tuple-element.69), channel_id=1, source_target_pairs={{0,16},{4,20},{8,24},{12,28},{16,0},{20,4},{24,8},{28,12},{1,17},{... | collective-permute-start | bytes 294920 | tf_op jit(solution)/shard_map/ppermute | solution.py:409
  15.2 13.3 %collective-permute-start.12 = (bf16[128,512]{1,0:T(8,128)(2,1)S(1)}, bf16[128,512]{1,0:T(8,128)(2,1)S(1)}, u32[]{:S(2)}, u32[]{:S(2)}) collective-permute-start(bf16[128,512]{1,0:T(8,128)(2,1)S(1)} %get-tuple-element.71), channel_id=1, source_target_pairs={{0,4},{4,8},{8,12},{12,16},{16,20},{20,24},{24,28},{28,0},{1,5},{5... | collective-permute-start | bytes 393224 | tf_op jit(solution)/shard_map/ppermute | solution.py:541
  15.2 7.3 %collective-permute-start.5 = (bf16[32,512]{1,0:T(8,128)(2,1)S(1)}, bf16[32,512]{1,0:T(8,128)(2,1)S(1)}, u32[]{:S(2)}, u32[]{:S(2)}) collective-permute-start(bf16[32,512]{1,0:T(8,128)(2,1)S(1)} %get-tuple-element.63), channel_id=1, source_target_pairs={{0,24},{4,28},{8,16},{12,20},{16,8},{20,12},{24,0},{28,4},{1,25},{... | collective-permute-start | bytes 98312 | tf_op jit(solution)/shard_map/ppermute | solution.py:409
  17.2 5.6 %collective-permute-start.6 = (bf16[32,512]{1,0:T(8,128)(2,1)S(1)}, bf16[32,512]{1,0:T(8,128)(2,1)S(1)}, u32[]{:S(2)}, u32[]{:S(2)}) collective-permute-start(bf16[32,512]{1,0:T(8,128)(2,1)S(1)} %get-tuple-element.64), channel_id=1, source_target_pairs={{0,8},{4,12},{8,0},{12,4},{16,24},{20,28},{24,16},{28,20},{1,9},{5... | collective-permute-start | bytes 98312 | tf_op jit(solution)/shard_map/ppermute | solution.py:409
  18.5 12.9 %collective-permute-start.11 = (bf16[64,512]{1,0:T(8,128)(2,1)S(1)}, bf16[64,512]{1,0:T(8,128)(2,1)S(1)}, u32[]{:S(2)}, u32[]{:S(2)}) collective-permute-start(bf16[64,512]{1,0:T(8,128)(2,1)S(1)} %get-tuple-element.70), channel_id=1, source_target_pairs={{0,2},{1,3},{2,0},{3,1},{4,6},{5,7},{6,4},{7,5},{8,10},{9,11},{10,... | collective-permute-start | bytes 196616 | tf_op jit(solution)/shard_map/ppermute | solution.py:409
  21.2 10.3 %collective-permute-start.13 = (bf16[64,512]{1,0:T(8,128)(2,1)S(1)}, bf16[64,512]{1,0:T(8,128)(2,1)S(1)}, u32[]{:S(2)}, u32[]{:S(2)}) collective-permute-start(bf16[64,512]{1,0:T(8,128)(2,1)S(1)} %get-tuple-element.74), channel_id=1, source_target_pairs={{0,3},{1,2},{2,1},{3,0},{4,7},{5,6},{6,5},{7,4},{8,11},{9,10},{10,... | collective-permute-start | bytes 196616 | tf_op jit(solution)/shard_map/ppermute | solution.py:409
  22.6 8.9 %collective-permute-start.14 = (bf16[64,512]{1,0:T(8,128)(2,1)S(1)}, bf16[64,512]{1,0:T(8,128)(2,1)S(1)}, u32[]{:S(2)}, u32[]{:S(2)}) collective-permute-start(bf16[64,512]{1,0:T(8,128)(2,1)S(1)} %get-tuple-element.75), channel_id=1, source_target_pairs={{0,1},{1,0},{2,3},{3,2},{4,5},{5,4},{6,7},{7,6},{8,9},{9,8},{10,11... | collective-permute-start | bytes 196616 | tf_op jit(solution)/shard_map/ppermute | solution.py:409
  22.8 5.5 %collective-permute-start.7 = (bf16[32,512]{1,0:T(8,128)(2,1)S(1)}, bf16[32,512]{1,0:T(8,128)(2,1)S(1)}, u32[]{:S(2)}, u32[]{:S(2)}) collective-permute-start(bf16[32,512]{1,0:T(8,128)(2,1)S(1)} %get-tuple-element.65), channel_id=1, source_target_pairs={{0,16},{4,20},{8,24},{12,28},{16,0},{20,4},{24,8},{28,12},{1,17},{... | collective-permute-start | bytes 98312 | tf_op jit(solution)/shard_map/ppermute | solution.py:409
  32.2 4.5 %collective-permute-start.17 = (bf16[64,512]{1,0:T(8,128)(2,1)S(1)}, bf16[64,512]{1,0:T(8,128)(2,1)S(1)}, u32[]{:S(2)}, u32[]{:S(2)}) collective-permute-start(bf16[64,512]{1,0:T(8,128)(2,1)S(1)} %get-tuple-element.78), channel_id=1, source_target_pairs={{0,1},{1,0},{2,3},{3,2},{4,5},{5,4},{6,7},{7,6},{8,9},{9,8},{10,11... | collective-permute-start | bytes 196616 | tf_op jit(solution)/shard_map/ppermute | solution.py:409
  34.1 12.1 %collective-permute-start.20 = (bf16[128,512]{1,0:T(8,128)(2,1)S(1)}, bf16[128,512]{1,0:T(8,128)(2,1)S(1)}, u32[]{:S(2)}, u32[]{:S(2)}) collective-permute-start(bf16[128,512]{1,0:T(8,128)(2,1)S(1)} %get-tuple-element.95), channel_id=1, source_target_pairs={{4,0},{8,4},{12,8},{16,12},{20,16},{24,20},{28,24},{0,28},{5,1},{9... | collective-permute-start | bytes 393224 | tf_op jit(solution)/shard_map/ppermute | solution.py:557
  34.1 8.3 %collective-permute-start.15 = (bf16[64,512]{1,0:T(8,128)(2,1)S(1)}, bf16[64,512]{1,0:T(8,128)(2,1)S(1)}, u32[]{:S(2)}, u32[]{:S(2)}) collective-permute-start(bf16[64,512]{1,0:T(8,128)(2,1)S(1)} %get-tuple-element.76), channel_id=1, source_target_pairs={{0,2},{1,3},{2,0},{3,1},{4,6},{5,7},{6,4},{7,5},{8,10},{9,11},{10,... | collective-permute-start | bytes 196616 | tf_op jit(solution)/shard_map/ppermute | solution.py:409
  35.8 8.6 %collective-permute-start.16 = (bf16[64,512]{1,0:T(8,128)(2,1)S(1)}, bf16[64,512]{1,0:T(8,128)(2,1)S(1)}, u32[]{:S(2)}, u32[]{:S(2)}) collective-permute-start(bf16[64,512]{1,0:T(8,128)(2,1)S(1)} %get-tuple-element.77), channel_id=1, source_target_pairs={{0,3},{1,2},{2,1},{3,0},{4,7},{5,6},{6,5},{7,4},{8,11},{9,10},{10,... | collective-permute-start | bytes 196616 | tf_op jit(solution)/shard_map/ppermute | solution.py:409
  36.9 7.5 %collective-permute-start.18 = (bf16[32,1024]{1,0:T(8,128)(2,1)S(1)}, bf16[32,1024]{1,0:T(8,128)(2,1)S(1)}, u32[]{:S(2)}, u32[]{:S(2)}) collective-permute-start(bf16[32,1024]{1,0:T(8,128)(2,1)S(1)} %get-tuple-element.80), channel_id=1, source_target_pairs={{0,8},{4,12},{8,0},{12,4},{16,24},{20,28},{24,16},{28,20},{1,9},{5... | collective-permute-start | bytes 196616 | tf_op jit(solution)/shard_map/ppermute | solution.py:409
  37.0 1.2 %collective-permute-start.19 = (s32[1,128]{1,0:T(1,128)S(1)}, s32[1,128]{1,0:T(1,128)S(1)}, u32[]{:S(2)}, u32[]{:S(2)}) collective-permute-start(s32[1,128]{1,0:T(1,128)S(1)} %get-tuple-element.81.target_ref), channel_id=1, source_target_pairs={{0,4},{4,0},{8,12},{12,8},{16,20},{20,16},{24,28},{28,24},{1,5},{5... | collective-permute-start | bytes 1544 | tf_op jit(solution)/shard_map/ppermute | solution.py:409
  38.2 11.5 %collective-permute-start.24 = (bf16[32,1024]{1,0:T(8,128)(2,1)S(1)}, bf16[32,1024]{1,0:T(8,128)(2,1)S(1)}, u32[]{:S(2)}, u32[]{:S(2)}) collective-permute-start(bf16[32,1024]{1,0:T(8,128)(2,1)S(1)} %get-tuple-element.107), channel_id=1, source_target_pairs={{0,24},{4,28},{8,16},{12,20},{16,8},{20,12},{24,0},{28,4},{1,25},{... | collective-permute-start | bytes 196616 | tf_op jit(solution)/shard_map/ppermute | solution.py:409
  42.4 7.4 %collective-permute-start.25 = (bf16[32,1024]{1,0:T(8,128)(2,1)S(1)}, bf16[32,1024]{1,0:T(8,128)(2,1)S(1)}, u32[]{:S(2)}, u32[]{:S(2)}) collective-permute-start(bf16[32,1024]{1,0:T(8,128)(2,1)S(1)} %get-tuple-element.109), channel_id=1, source_target_pairs={{0,16},{4,20},{8,24},{12,28},{16,0},{20,4},{24,8},{28,12},{1,17},{... | collective-permute-start | bytes 196616 | tf_op jit(solution)/shard_map/ppermute | solution.py:409
  44.6 5.2 %collective-permute-start.21 = (bf16[32,1024]{1,0:T(8,128)(2,1)S(1)}, bf16[32,1024]{1,0:T(8,128)(2,1)S(1)}, u32[]{:S(2)}, u32[]{:S(2)}) collective-permute-start(bf16[32,1024]{1,0:T(8,128)(2,1)S(1)} %get-tuple-element.103), channel_id=1, source_target_pairs={{0,24},{4,28},{8,16},{12,20},{16,8},{20,12},{24,0},{28,4},{1,25},{... | collective-permute-start | bytes 196616 | tf_op jit(solution)/shard_map/ppermute | solution.py:409
  44.7 5.2 %collective-permute-start.22 = (bf16[32,1024]{1,0:T(8,128)(2,1)S(1)}, bf16[32,1024]{1,0:T(8,128)(2,1)S(1)}, u32[]{:S(2)}, u32[]{:S(2)}) collective-permute-start(bf16[32,1024]{1,0:T(8,128)(2,1)S(1)} %get-tuple-element.104), channel_id=1, source_target_pairs={{0,8},{4,12},{8,0},{12,4},{16,24},{20,28},{24,16},{28,20},{1,9},{5... | collective-permute-start | bytes 196616 | tf_op jit(solution)/shard_map/ppermute | solution.py:409
  46.1 4.4 %collective-permute-start.23 = (bf16[32,1024]{1,0:T(8,128)(2,1)S(1)}, bf16[32,1024]{1,0:T(8,128)(2,1)S(1)}, u32[]{:S(2)}, u32[]{:S(2)}) collective-permute-start(bf16[32,1024]{1,0:T(8,128)(2,1)S(1)} %get-tuple-element.105), channel_id=1, source_target_pairs={{0,16},{4,20},{8,24},{12,28},{16,0},{20,4},{24,8},{28,12},{1,17},{... | collective-permute-start | bytes 196616 | tf_op jit(solution)/shard_map/ppermute | solution.py:409
  50.6 1.6 %collective-permute-start.26 = (bf16[64,2048]{1,0:T(8,128)(2,1)S(1)}, bf16[64,2048]{1,0:T(8,128)(2,1)S(1)}, u32[]{:S(2)}, u32[]{:S(2)}) collective-permute-start(bf16[64,2048]{1,0:T(8,128)(2,1)S(1)} %get-tuple-element.111), channel_id=1, source_target_pairs={{0,4},{4,0},{8,12},{12,8},{16,20},{20,16},{24,28},{28,24},{1,5},{5... | collective-permute-start | bytes 786440 | tf_op jit(solution)/shard_map/ppermute | solution.py:409

commit v7 on v5

--- a/solution.py
+++ b/solution.py
@@ -563,6 +563,8 @@
     grads = grads[1:] + grads[:1]
     returned = []
     for name, half in (("scatter_near", grads[parts:]), ("scatter_far", grads[:parts])):
+        if not returned:
+            half[0], back = lax.optimization_barrier((half[0], back))
         if returned:
             half, returned[2] = lax.optimization_barrier((half, returned[2]))
         sent = call(
@@ -590,7 +592,9 @@
         300_000_000,
         5_000_000,
     )
-    returned[0], attended = lax.optimization_barrier((returned[0], attended))
+    returned[0], attended, other_target = lax.optimization_barrier(
+        (returned[0], attended, other_target)
+    )
     same, other = call(
         part_cores_kernel,
         "part_cores",

time: 50.8 us -> 50.4 us (level)
  waiting for transfers between devices: 10.3 us -> 7.07 us
  starting transfers between devices: 29.2 us -> 32 us
    ppermute x25, waiting for transfers between devices: 10.3 us -> 7.07 us  [swapped(): lax.ppermute(block, axis, [(i, i ^ apart) for i in range(lax.axis_size(ax...]
    ppermute x1, starting transfers between devices: 0.84 us -> 2.75 us  [body(): lax.ppermute(back, 'seq', [((i + 1) % devices, i) for i in range(devices)])]
    ppermute x25, starting transfers between devices: 28.4 us -> 29.2 us  [swapped(): lax.ppermute(block, axis, [(i, i ^ apart) for i in range(lax.axis_size(ax...]
  transfers between devices with their start and end apart: 27 -> 27, of which waited for: 10 -> 10; matrix products, arithmetic and copies ran while one was open for 0% -> 0% of each run, Pallas kernels for 15% -> 17%
where the time goes in v7:
time: 50.4 us; the launch traced here: 50.2 us
  starting transfers between devices  32 us (63%)
  Pallas kernels  10.3 us (20%)
  waiting for transfers between devices  7.07 us (14%)
  between operations  0.82 us (2%)
    ppermute x25, starting transfers between devices, swapped(): lax.ppermute(block, axis, [(i, i ^ apart) for i in range(lax.axis_size(ax...  29.2 us
    pallas_call x12, Pallas kernels, call(): pl.pallas_call(kernel, out_shape=tuple(outs), in_specs=[SMEM] * scalars +...  10.3 us
    ppermute x25, waiting for transfers between devices, swapped(): lax.ppermute(block, axis, [(i, i ^ apart) for i in range(lax.axis_size(ax...  7.07 us
    ppermute x1, starting transfers between devices, body(): lax.ppermute(back, 'seq', [((i + 1) % devices, i) for i in range(devices)])  2.75 us
  transfers between devices with their start and end apart: 27, of which 10 were waited for; matrix products, arithmetic and copies ran while one was open for 0% of the time, Pallas kernels for 17%

profile of v7, /device:TPU:0, one launch (start us, length us, event | category | flops | bytes accessed | tf_op | source)
XLA Modules:
  0.0 50.2 jit_solution(12515861749940151913)
XLA Ops:
  1.2 0.9 %plan_requests.1.refs_0_ = s32[8,128]{1,0:T(8,128)S(1)} custom-call(s32[4,4]{1,0:T(4,128)} %owner_any.3, s32[4,4]{1,0:T(4,128)} %slot_any.1), custom_call_target="tpu_custom_call" | custom-call | bytes 100000 | tf_op jit(solution)/shard_map/plan_requests/pallas_call | solution.py:394
  2.2 3.9 %collective-permute-start.2 = (s32[8,128]{1,0:T(8,128)S(1)}, s32[8,128]{1,0:T(8,128)S(1)}, u32[]{:S(2)}, u32[]{:S(2)}) collective-permute-start(s32[8,128]{1,0:T(8,128)S(1)} %plan_requests.1.refs_0_), channel_id=1, source_target_pairs={{0,24},{4,28},{8,16},{12,20},{16,8},{20,12},{24,0},{28,4},{1,25},{... | collective-permute-start | bytes 12296 | tf_op jit(solution)/shard_map/ppermute | solution.py:409
  6.1 0.5 %collective-permute-start.3 = (s32[8,128]{1,0:T(8,128)S(1)}, s32[8,128]{1,0:T(8,128)S(1)}, u32[]{:S(2)}, u32[]{:S(2)}) collective-permute-start(s32[8,128]{1,0:T(8,128)S(1)} %plan_requests.1.refs_0_), channel_id=1, source_target_pairs={{0,8},{4,12},{8,0},{12,4},{16,24},{20,28},{24,16},{28,20},{1,9},{5... | collective-permute-start | bytes 12296 | tf_op jit(solution)/shard_map/ppermute | solution.py:409
  6.8 1.5 %stage_store.1 = (bf16[512,2048]{1,0:T(8,128)(2,1)S(1)}, bf16[128,512]{1,0:T(8,128)(2,1)S(1)}, bf16[128,64]{1,0:T(8,128)(2,1)S(1)}) custom-call(s32[1]{0:T(128)} %bitcast.me_ref.rank_ref, s32[1]{0:T(128)} %bitcast.1.z_ref, bf16[64,4,1024]{2,1,0:T(4,128)(2,1)S(1)} %collective-permute-done.sibling_k_ref, ...), custom_call_target="tpu_custom_call" | custom-call | bytes 5000000 | tf_op jit(solution)/shard_map/stage_store/pallas_call | solution.py:394
  8.3 1.4 %collective-permute-done.3.refs_2_ = s32[8,128]{1,0:T(8,128)S(1)} collective-permute-done((s32[8,128]{1,0:T(8,128)S(1)}, s32[8,128]{1,0:T(8,128)S(1)}, u32[]{:S(2)}, u32[]{:S(2)}) %collective-permute-start.3) | collective-permute-done | bytes 4128 | tf_op jit(solution)/shard_map/ppermute | solution.py:409
  9.7 0.5 %collective-permute-done.4.refs_3_ = s32[8,128]{1,0:T(8,128)S(1)} collective-permute-done((s32[8,128]{1,0:T(8,128)S(1)}, s32[8,128]{1,0:T(8,128)S(1)}, u32[]{:S(2)}, u32[]{:S(2)}) %collective-permute-start.4) | collective-permute-done | bytes 4128 | tf_op jit(solution)/shard_map/ppermute | solution.py:409
  10.9 2.8 %collective-permute-start.8 = (bf16[32,1024]{1,0:T(8,128)(2,1)S(1)}, bf16[32,1024]{1,0:T(8,128)(2,1)S(1)}, u32[]{:S(2)}, u32[]{:S(2)}) collective-permute-start(bf16[32,1024]{1,0:T(8,128)(2,1)S(1)} %get-tuple-element.71), channel_id=1, source_target_pairs={{0,24},{4,28},{8,16},{12,20},{16,8},{20,12},{24,0},{28,4},{1,25},{... | collective-permute-start | bytes 196616 | tf_op jit(solution)/shard_map/ppermute | solution.py:409
  13.8 0.6 %collective-permute-start.9 = (bf16[32,1024]{1,0:T(8,128)(2,1)S(1)}, bf16[32,1024]{1,0:T(8,128)(2,1)S(1)}, u32[]{:S(2)}, u32[]{:S(2)}) collective-permute-start(bf16[32,1024]{1,0:T(8,128)(2,1)S(1)} %get-tuple-element.72), channel_id=1, source_target_pairs={{0,8},{4,12},{8,0},{12,4},{16,24},{20,28},{24,16},{28,20},{1,9},{5... | collective-permute-start | bytes 196616 | tf_op jit(solution)/shard_map/ppermute | solution.py:409
  14.3 1.4 %collective-permute-start.5 = (bf16[32,1024]{1,0:T(8,128)(2,1)S(1)}, bf16[32,1024]{1,0:T(8,128)(2,1)S(1)}, u32[]{:S(2)}, u32[]{:S(2)}) collective-permute-start(bf16[32,1024]{1,0:T(8,128)(2,1)S(1)} %get-tuple-element.66), channel_id=1, source_target_pairs={{0,24},{4,28},{8,16},{12,20},{16,8},{20,12},{24,0},{28,4},{1,25},{... | collective-permute-start | bytes 196616 | tf_op jit(solution)/shard_map/ppermute | solution.py:409
  15.7 0.8 %collective-permute-start.6 = (bf16[32,1024]{1,0:T(8,128)(2,1)S(1)}, bf16[32,1024]{1,0:T(8,128)(2,1)S(1)}, u32[]{:S(2)}, u32[]{:S(2)}) collective-permute-start(bf16[32,1024]{1,0:T(8,128)(2,1)S(1)} %get-tuple-element.67), channel_id=1, source_target_pairs={{0,8},{4,12},{8,0},{12,4},{16,24},{20,28},{24,16},{28,20},{1,9},{5... | collective-permute-start | bytes 196616 | tf_op jit(solution)/shard_map/ppermute | solution.py:409
  16.6 1.4 %collective-permute-start.7 = (bf16[32,1024]{1,0:T(8,128)(2,1)S(1)}, bf16[32,1024]{1,0:T(8,128)(2,1)S(1)}, u32[]{:S(2)}, u32[]{:S(2)}) collective-permute-start(bf16[32,1024]{1,0:T(8,128)(2,1)S(1)} %get-tuple-element.68), channel_id=1, source_target_pairs={{0,16},{4,20},{8,24},{12,28},{16,0},{20,4},{24,8},{28,12},{1,17},{... | collective-permute-start | bytes 196616 | tf_op jit(solution)/shard_map/ppermute | solution.py:409
  18.0 0.7 %collective-permute-done.9.refs_2_ = bf16[32,1024]{1,0:T(8,128)(2,1)S(1)} collective-permute-done((bf16[32,1024]{1,0:T(8,128)(2,1)S(1)}, bf16[32,1024]{1,0:T(8,128)(2,1)S(1)}, u32[]{:S(2)}, u32[]{:S(2)}) %collective-permute-start.9) | collective-permute-done | bytes 65568 | tf_op jit(solution)/shard_map/ppermute | solution.py:409
  18.9 2.7 %collective-permute-start.11 = (bf16[64,512]{1,0:T(8,128)(2,1)S(1)}, bf16[64,512]{1,0:T(8,128)(2,1)S(1)}, u32[]{:S(2)}, u32[]{:S(2)}) collective-permute-start(bf16[64,512]{1,0:T(8,128)(2,1)S(1)} %get-tuple-element.74), channel_id=1, source_target_pairs={{0,2},{1,3},{2,0},{3,1},{4,6},{5,7},{6,4},{7,5},{8,10},{9,11},{10,... | collective-permute-start | bytes 196616 | tf_op jit(solution)/shard_map/ppermute | solution.py:409
  21.5 2.3 %collective-permute-start.13 = (bf16[64,512]{1,0:T(8,128)(2,1)S(1)}, bf16[64,512]{1,0:T(8,128)(2,1)S(1)}, u32[]{:S(2)}, u32[]{:S(2)}) collective-permute-start(bf16[64,512]{1,0:T(8,128)(2,1)S(1)} %get-tuple-element.78), channel_id=1, source_target_pairs={{0,3},{1,2},{2,1},{3,0},{4,7},{5,6},{6,5},{7,4},{8,11},{9,10},{10,... | collective-permute-start | bytes 196616 | tf_op jit(solution)/shard_map/ppermute | solution.py:409
  24.2 2.9 %self_attention.1 = (f32[256,1024]{1,0:T(8,128)S(1)}, f32[256,1024]{1,0:T(8,128)S(1)}, f32[256,512]{1,0:T(8,128)S(1)}, bf16[128,512]{1,0:T(8,128)(2,1)S(1)}) custom-call(s32[1]{0:T(128)} %bitcast.me_ref.rank_ref, bf16[256,1024]{1,0:T(8,128)(2,1)S(1)} %copy-done, bf16[256,256]{1,0:T(8,128)(2,1)S(1)} %copy-done.2, bf16[256,256]{1,0:T(8,128)(2,1)S(1)} %copy-done.3, ...), custom_call_target="tpu_custom_call" | custom-call | flops 1000000 | bytes 10000 | tf_op jit(solution)/shard_map/self_attention/pallas_call | solution.py:394
  27.1 2.8 %collective-permute-start.18 = (bf16[128,512]{1,0:T(8,128)(2,1)S(1)}, bf16[128,512]{1,0:T(8,128)(2,1)S(1)}, u32[]{:S(2)}, u32[]{:S(2)}) collective-permute-start(bf16[128,512]{1,0:T(8,128)(2,1)S(1)} %get-tuple-element.83), channel_id=1, source_target_pairs={{4,0},{8,4},{12,8},{16,12},{20,16},{24,20},{28,24},{0,28},{5,1},{9... | collective-permute-start | bytes 393224 | tf_op jit(solution)/shard_map/ppermute | solution.py:548
  29.8 0.8 %cross_attention.1 = (bf16[64,512]{1,0:T(8,128)(2,1)S(1)}, bf16[64,512]{1,0:T(8,128)(2,1)S(1)}, bf16[64,512]{1,0:T(8,128)(2,1)S(1)}, bf16[64,512]{1,0:T(8,128)(2...) custom-call(bf16[256,1024]{1,0:T(8,128)(2,1)S(1)} %copy-done, bf16[256,1024]{1,0:T(8,128)(2,1)S(1)} %copy-done.1, ...), custom_call_target="tpu_custom_call" | custom-call | flops 600000000 | bytes 3000000 | tf_op jit(solution)/shard_map/cross_attention/pallas_call | solution.py:394
  30.6 1.8 %collective-permute-start.17 = (bf16[64,512]{1,0:T(8,128)(2,1)S(1)}, bf16[64,512]{1,0:T(8,128)(2,1)S(1)}, u32[]{:S(2)}, u32[]{:S(2)}) collective-permute-start(bf16[64,512]{1,0:T(8,128)(2,1)S(1)} %get-tuple-element.82), channel_id=1, source_target_pairs={{0,1},{1,0},{2,3},{3,2},{4,5},{5,4},{6,7},{7,6},{8,9},{9,8},{10,11... | collective-permute-start | bytes 196616 | tf_op jit(solution)/shard_map/ppermute | solution.py:409
  32.4 1.5 %collective-permute-start.15 = (bf16[64,512]{1,0:T(8,128)(2,1)S(1)}, bf16[64,512]{1,0:T(8,128)(2,1)S(1)}, u32[]{:S(2)}, u32[]{:S(2)}) collective-permute-start(bf16[64,512]{1,0:T(8,128)(2,1)S(1)} %get-tuple-element.80), channel_id=1, source_target_pairs={{0,2},{1,3},{2,0},{3,1},{4,6},{5,7},{6,4},{7,5},{8,10},{9,11},{10,... | collective-permute-start | bytes 196616 | tf_op jit(solution)/shard_map/ppermute | solution.py:409
  33.9 1.2 %collective-permute-start.16 = (bf16[64,512]{1,0:T(8,128)(2,1)S(1)}, bf16[64,512]{1,0:T(8,128)(2,1)S(1)}, u32[]{:S(2)}, u32[]{:S(2)}) collective-permute-start(bf16[64,512]{1,0:T(8,128)(2,1)S(1)} %get-tuple-element.81), channel_id=1, source_target_pairs={{0,3},{1,2},{2,1},{3,0},{4,7},{5,6},{6,5},{7,4},{8,11},{9,10},{10,... | collective-permute-start | bytes 196616 | tf_op jit(solution)/shard_map/ppermute | solution.py:409
  35.0 0.6 %collective-permute-done.17.refs_0_ = bf16[64,512]{1,0:T(8,128)(2,1)S(1)} collective-permute-done((bf16[64,512]{1,0:T(8,128)(2,1)S(1)}, bf16[64,512]{1,0:T(8,128)(2,1)S(1)}, u32[]{:S(2)}, u32[]{:S(2)}) %collective-permute-start.17) | collective-permute-done | bytes 65568 | tf_op jit(solution)/shard_map/ppermute | solution.py:409
  35.8 1.6 %collective-permute-start.19 = (bf16[32,1024]{1,0:T(8,128)(2,1)S(1)}, bf16[32,1024]{1,0:T(8,128)(2,1)S(1)}, u32[]{:S(2)}, u32[]{:S(2)}) collective-permute-start(bf16[32,1024]{1,0:T(8,128)(2,1)S(1)} %get-tuple-element.86), channel_id=1, source_target_pairs={{0,8},{4,12},{8,0},{12,4},{16,24},{20,28},{24,16},{28,20},{1,9},{5... | collective-permute-start | bytes 196616 | tf_op jit(solution)/shard_map/ppermute | solution.py:409
  37.4 1.1 %collective-permute-start.24 = (bf16[32,1024]{1,0:T(8,128)(2,1)S(1)}, bf16[32,1024]{1,0:T(8,128)(2,1)S(1)}, u32[]{:S(2)}, u32[]{:S(2)}) collective-permute-start(bf16[32,1024]{1,0:T(8,128)(2,1)S(1)} %get-tuple-element.113), channel_id=1, source_target_pairs={{0,24},{4,28},{8,16},{12,20},{16,8},{20,12},{24,0},{28,4},{1,25},{... | collective-permute-start | bytes 196616 | tf_op jit(solution)/shard_map/ppermute | solution.py:409
  38.5 0.6 %collective-permute-done.15.refs_0_ = bf16[64,512]{1,0:T(8,128)(2,1)S(1)} collective-permute-done((bf16[64,512]{1,0:T(8,128)(2,1)S(1)}, bf16[64,512]{1,0:T(8,128)(2,1)S(1)}, u32[]{:S(2)}, u32[]{:S(2)}) %collective-permute-start.15) | collective-permute-done | bytes 65568 | tf_op jit(solution)/shard_map/ppermute | solution.py:409
  39.1 1.1 %collective-permute-start.25 = (bf16[32,1024]{1,0:T(8,128)(2,1)S(1)}, bf16[32,1024]{1,0:T(8,128)(2,1)S(1)}, u32[]{:S(2)}, u32[]{:S(2)}) collective-permute-start(bf16[32,1024]{1,0:T(8,128)(2,1)S(1)} %get-tuple-element.115), channel_id=1, source_target_pairs={{0,16},{4,20},{8,24},{12,28},{16,0},{20,4},{24,8},{28,12},{1,17},{... | collective-permute-start | bytes 196616 | tf_op jit(solution)/shard_map/ppermute | solution.py:409
  40.7 1.5 %collective-permute-start.21 = (bf16[32,1024]{1,0:T(8,128)(2,1)S(1)}, bf16[32,1024]{1,0:T(8,128)(2,1)S(1)}, u32[]{:S(2)}, u32[]{:S(2)}) collective-permute-start(bf16[32,1024]{1,0:T(8,128)(2,1)S(1)} %get-tuple-element.109), channel_id=1, source_target_pairs={{0,24},{4,28},{8,16},{12,20},{16,8},{20,12},{24,0},{28,4},{1,25},{... | collective-permute-start | bytes 196616 | tf_op jit(solution)/shard_map/ppermute | solution.py:409
  42.2 0.8 %collective-permute-start.22 = (bf16[32,1024]{1,0:T(8,128)(2,1)S(1)}, bf16[32,1024]{1,0:T(8,128)(2,1)S(1)}, u32[]{:S(2)}, u32[]{:S(2)}) collective-permute-start(bf16[32,1024]{1,0:T(8,128)(2,1)S(1)} %get-tuple-element.110), channel_id=1, source_target_pairs={{0,8},{4,12},{8,0},{12,4},{16,24},{20,28},{24,16},{28,20},{1,9},{5... | collective-permute-start | bytes 196616 | tf_op jit(solution)/shard_map/ppermute | solution.py:409
  43.0 1.2 %collective-permute-start.23 = (bf16[32,1024]{1,0:T(8,128)(2,1)S(1)}, bf16[32,1024]{1,0:T(8,128)(2,1)S(1)}, u32[]{:S(2)}, u32[]{:S(2)}) collective-permute-start(bf16[32,1024]{1,0:T(8,128)(2,1)S(1)} %get-tuple-element.111), channel_id=1, source_target_pairs={{0,16},{4,20},{8,24},{12,28},{16,0},{20,4},{24,8},{28,12},{1,17},{... | collective-permute-start | bytes 196616 | tf_op jit(solution)/shard_map/ppermute | solution.py:409
  44.3 1.6 %join_outputs.1 = (bf16[256,1024]{1,0:T(8,128)(2,1)}, bf16[256,1024]{1,0:T(8,128)(2,1)}, bf16[256,256]{1,0:T(8,128)(2,1)}, bf16[256,256]{1,0:T(8,128)(2,1)}) custom-call(bf16[8,64,256]{2,1,0:T(8,128)(2,1)S(1)} %get-tuple-element.95.w_ref, bf16[8,64,256]{2,1,0:T(8,128)(2,1)S(1)} %get-tuple-element.96.ds_ref, f32[256,1024]{1,0:T(8,128)S(1)} %get-tuple-element.97.out_ref, ...), custom_call_target="tpu_custom_call" | custom-call | flops 300000000 | bytes 5000000 | tf_op jit(solution)/shard_map/join_outputs/pallas_call | solution.py:394
  46.5 0.8 %collective-permute-done.23.refs_3_ = bf16[32,1024]{1,0:T(8,128)(2,1)S(1)} collective-permute-done((bf16[32,1024]{1,0:T(8,128)(2,1)S(1)}, bf16[32,1024]{1,0:T(8,128)(2,1)S(1)}, u32[]{:S(2)}, u32[]{:S(2)}) %collective-permute-start.23) | collective-permute-done | bytes 65568 | tf_op jit(solution)/shard_map/ppermute | solution.py:409
  47.4 1.5 %collective-permute-done.26.other_rows = bf16[64,2048]{1,0:T(8,128)(2,1)S(1)} collective-permute-done((bf16[64,2048]{1,0:T(8,128)(2,1)S(1)}, bf16[64,2048]{1,0:T(8,128)(2,1)S(1)}, u32[]{:S(2)}, u32[]{:S(2)}) %collective-permute-start.26) | collective-permute-done | bytes 262176 | tf_op jit(solution)/shard_map/ppermute | solution.py:409
  48.9 1.3 %sum_store_gradients.1 = (bf16[64,4,1024]{2,1,0:T(4,128)(2,1)}, bf16[64,4,1024]{2,1,0:T(4,128)(2,1)}) custom-call(s32[1]{0:T(128)} %bitcast.1.z_ref, s32[1,128]{1,0:T(1,128)S(1)} %get-tuple-element.102.target_ref, s32[1,128]{1,0:T(1,128)S(1)} %collective-permute-done.20.other_ref, bf16[64,2048]{1,0:T(8,128)(2,1)S(1)} %get-tuple-element.116.same_rows, ...), custom_call_target="tpu_custom_call" | custom-call | flops 200000000 | bytes 2000000 | tf_op jit(solution)/shard_map/sum_store_gradients/pallas_call | solution.py:394
  (42 shorter events, 3.4 us)
Async XLA Ops:
  0.6 6.1 %collective-permute-start = (bf16[64,4,1024]{2,1,0:T(4,128)(2,1)}, bf16[64,4,1024]{2,1,0:T(4,128)(2,1)S(1)}, u32[]{:S(2)}, u32[]{:S(2)}) collective-permute-start(bf16[64,4,1024]{2,1,0:T(4,128)(2,1)} %k_any.1), channel_id=1, source_target_pairs={{0,4},{4,0},{8,12},{12,8},{16,20},{20,16},{24,28},{28,24},{1,5},{5... | collective-permute-start | bytes 1572872 | tf_op jit(solution)/shard_map/ppermute | solution.py:409
  1.1 5.6 %collective-permute-start.1 = (bf16[64,4,1024]{2,1,0:T(4,128)(2,1)}, bf16[64,4,1024]{2,1,0:T(4,128)(2,1)S(1)}, u32[]{:S(2)}, u32[]{:S(2)}) collective-permute-start(bf16[64,4,1024]{2,1,0:T(4,128)(2,1)} %v_any.1), channel_id=1, source_target_pairs={{0,4},{4,0},{8,12},{12,8},{16,20},{20,16},{24,28},{28,24},{1,5},{5... | collective-permute-start | bytes 1572872 | tf_op jit(solution)/shard_map/ppermute | solution.py:409
  2.2 6.2 %collective-permute-start.2 = (s32[8,128]{1,0:T(8,128)S(1)}, s32[8,128]{1,0:T(8,128)S(1)}, u32[]{:S(2)}, u32[]{:S(2)}) collective-permute-start(s32[8,128]{1,0:T(8,128)S(1)} %plan_requests.1.refs_0_), channel_id=1, source_target_pairs={{0,24},{4,28},{8,16},{12,20},{16,8},{20,12},{24,0},{28,4},{1,25},{... | collective-permute-start | bytes 12296 | tf_op jit(solution)/shard_map/ppermute | solution.py:409
  6.1 3.6 %collective-permute-start.3 = (s32[8,128]{1,0:T(8,128)S(1)}, s32[8,128]{1,0:T(8,128)S(1)}, u32[]{:S(2)}, u32[]{:S(2)}) collective-permute-start(s32[8,128]{1,0:T(8,128)S(1)} %plan_requests.1.refs_0_), channel_id=1, source_target_pairs={{0,8},{4,12},{8,0},{12,4},{16,24},{20,28},{24,16},{28,20},{1,9},{5... | collective-permute-start | bytes 12296 | tf_op jit(solution)/shard_map/ppermute | solution.py:409
  6.6 3.6 %collective-permute-start.4 = (s32[8,128]{1,0:T(8,128)S(1)}, s32[8,128]{1,0:T(8,128)S(1)}, u32[]{:S(2)}, u32[]{:S(2)}) collective-permute-start(s32[8,128]{1,0:T(8,128)S(1)} %plan_requests.1.refs_0_), channel_id=1, source_target_pairs={{0,16},{4,20},{8,24},{12,28},{16,0},{20,4},{24,8},{28,12},{1,17},{... | collective-permute-start | bytes 12296 | tf_op jit(solution)/shard_map/ppermute | solution.py:409
  6.7 17.4 %copy-start = (bf16[256,1024]{1,0:T(8,128)(2,1)S(1)}, bf16[256,1024]{1,0:T(8,128)(2,1)}, u32[]{:S(2)}) copy-start(bf16[256,1024]{1,0:T(8,128)(2,1)} %q_ref.3) | copy-start | bytes 1572868
  6.7 17.4 %copy-start.1 = (bf16[256,1024]{1,0:T(8,128)(2,1)S(1)}, bf16[256,1024]{1,0:T(8,128)(2,1)}, u32[]{:S(2)}) copy-start(bf16[256,1024]{1,0:T(8,128)(2,1)} %do_ref.3) | copy-start | bytes 1572868
  6.8 17.4 %copy-start.2 = (bf16[256,256]{1,0:T(8,128)(2,1)S(1)}, bf16[256,256]{1,0:T(8,128)(2,1)}, u32[]{:S(2)}) copy-start(bf16[256,256]{1,0:T(8,128)(2,1)} %k_ref.1) | copy-start | bytes 393220
  6.8 17.4 %copy-start.3 = (bf16[256,256]{1,0:T(8,128)(2,1)S(1)}, bf16[256,256]{1,0:T(8,128)(2,1)}, u32[]{:S(2)}) copy-start(bf16[256,256]{1,0:T(8,128)(2,1)} %v_ref.1) | copy-start | bytes 393220
  10.7 5.0 %collective-permute-start.10 = (bf16[32,1024]{1,0:T(8,128)(2,1)S(1)}, bf16[32,1024]{1,0:T(8,128)(2,1)S(1)}, u32[]{:S(2)}, u32[]{:S(2)}) collective-permute-start(bf16[32,1024]{1,0:T(8,128)(2,1)S(1)} %get-tuple-element.73), channel_id=1, source_target_pairs={{0,16},{4,20},{8,24},{12,28},{16,0},{20,4},{24,8},{28,12},{1,17},{... | collective-permute-start | bytes 196616 | tf_op jit(solution)/shard_map/ppermute | solution.py:409
  10.9 5.7 %collective-permute-start.8 = (bf16[32,1024]{1,0:T(8,128)(2,1)S(1)}, bf16[32,1024]{1,0:T(8,128)(2,1)S(1)}, u32[]{:S(2)}, u32[]{:S(2)}) collective-permute-start(bf16[32,1024]{1,0:T(8,128)(2,1)S(1)} %get-tuple-element.71), channel_id=1, source_target_pairs={{0,24},{4,28},{8,16},{12,20},{16,8},{20,12},{24,0},{28,4},{1,25},{... | collective-permute-start | bytes 196616 | tf_op jit(solution)/shard_map/ppermute | solution.py:409
  13.7 10.4 %collective-permute-start.12 = (bf16[128,512]{1,0:T(8,128)(2,1)S(1)}, bf16[128,512]{1,0:T(8,128)(2,1)S(1)}, u32[]{:S(2)}, u32[]{:S(2)}) collective-permute-start(bf16[128,512]{1,0:T(8,128)(2,1)S(1)} %get-tuple-element.75), channel_id=1, source_target_pairs={{0,4},{4,8},{8,12},{12,16},{16,20},{20,24},{24,28},{28,0},{1,5},{5... | collective-permute-start | bytes 393224 | tf_op jit(solution)/shard_map/ppermute | solution.py:532
  13.8 4.9 %collective-permute-start.9 = (bf16[32,1024]{1,0:T(8,128)(2,1)S(1)}, bf16[32,1024]{1,0:T(8,128)(2,1)S(1)}, u32[]{:S(2)}, u32[]{:S(2)}) collective-permute-start(bf16[32,1024]{1,0:T(8,128)(2,1)S(1)} %get-tuple-element.72), channel_id=1, source_target_pairs={{0,8},{4,12},{8,0},{12,4},{16,24},{20,28},{24,16},{28,20},{1,9},{5... | collective-permute-start | bytes 196616 | tf_op jit(solution)/shard_map/ppermute | solution.py:409
  14.3 7.2 %collective-permute-start.5 = (bf16[32,1024]{1,0:T(8,128)(2,1)S(1)}, bf16[32,1024]{1,0:T(8,128)(2,1)S(1)}, u32[]{:S(2)}, u32[]{:S(2)}) collective-permute-start(bf16[32,1024]{1,0:T(8,128)(2,1)S(1)} %get-tuple-element.66), channel_id=1, source_target_pairs={{0,24},{4,28},{8,16},{12,20},{16,8},{20,12},{24,0},{28,4},{1,25},{... | collective-permute-start | bytes 196616 | tf_op jit(solution)/shard_map/ppermute | solution.py:409
  15.7 8.1 %collective-permute-start.6 = (bf16[32,1024]{1,0:T(8,128)(2,1)S(1)}, bf16[32,1024]{1,0:T(8,128)(2,1)S(1)}, u32[]{:S(2)}, u32[]{:S(2)}) collective-permute-start(bf16[32,1024]{1,0:T(8,128)(2,1)S(1)} %get-tuple-element.67), channel_id=1, source_target_pairs={{0,8},{4,12},{8,0},{12,4},{16,24},{20,28},{24,16},{28,20},{1,9},{5... | collective-permute-start | bytes 196616 | tf_op jit(solution)/shard_map/ppermute | solution.py:409
  16.6 7.3 %collective-permute-start.7 = (bf16[32,1024]{1,0:T(8,128)(2,1)S(1)}, bf16[32,1024]{1,0:T(8,128)(2,1)S(1)}, u32[]{:S(2)}, u32[]{:S(2)}) collective-permute-start(bf16[32,1024]{1,0:T(8,128)(2,1)S(1)} %get-tuple-element.68), channel_id=1, source_target_pairs={{0,16},{4,20},{8,24},{12,28},{16,0},{20,4},{24,8},{28,12},{1,17},{... | collective-permute-start | bytes 196616 | tf_op jit(solution)/shard_map/ppermute | solution.py:409
  18.9 10.9 %collective-permute-start.11 = (bf16[64,512]{1,0:T(8,128)(2,1)S(1)}, bf16[64,512]{1,0:T(8,128)(2,1)S(1)}, u32[]{:S(2)}, u32[]{:S(2)}) collective-permute-start(bf16[64,512]{1,0:T(8,128)(2,1)S(1)} %get-tuple-element.74), channel_id=1, source_target_pairs={{0,2},{1,3},{2,0},{3,1},{4,6},{5,7},{6,4},{7,5},{8,10},{9,11},{10,... | collective-permute-start | bytes 196616 | tf_op jit(solution)/shard_map/ppermute | solution.py:409
  21.5 8.3 %collective-permute-start.13 = (bf16[64,512]{1,0:T(8,128)(2,1)S(1)}, bf16[64,512]{1,0:T(8,128)(2,1)S(1)}, u32[]{:S(2)}, u32[]{:S(2)}) collective-permute-start(bf16[64,512]{1,0:T(8,128)(2,1)S(1)} %get-tuple-element.78), channel_id=1, source_target_pairs={{0,3},{1,2},{2,1},{3,0},{4,7},{5,6},{6,5},{7,4},{8,11},{9,10},{10,... | collective-permute-start | bytes 196616 | tf_op jit(solution)/shard_map/ppermute | solution.py:409
  24.0 5.8 %collective-permute-start.14 = (bf16[64,512]{1,0:T(8,128)(2,1)S(1)}, bf16[64,512]{1,0:T(8,128)(2,1)S(1)}, u32[]{:S(2)}, u32[]{:S(2)}) collective-permute-start(bf16[64,512]{1,0:T(8,128)(2,1)S(1)} %get-tuple-element.79), channel_id=1, source_target_pairs={{0,1},{1,0},{2,3},{3,2},{4,5},{5,4},{6,7},{7,6},{8,9},{9,8},{10,11... | collective-permute-start | bytes 196616 | tf_op jit(solution)/shard_map/ppermute | solution.py:409
  27.1 8.6 %collective-permute-start.18 = (bf16[128,512]{1,0:T(8,128)(2,1)S(1)}, bf16[128,512]{1,0:T(8,128)(2,1)S(1)}, u32[]{:S(2)}, u32[]{:S(2)}) collective-permute-start(bf16[128,512]{1,0:T(8,128)(2,1)S(1)} %get-tuple-element.83), channel_id=1, source_target_pairs={{4,0},{8,4},{12,8},{16,12},{20,16},{24,20},{28,24},{0,28},{5,1},{9... | collective-permute-start | bytes 393224 | tf_op jit(solution)/shard_map/ppermute | solution.py:548
  30.6 5.0 %collective-permute-start.17 = (bf16[64,512]{1,0:T(8,128)(2,1)S(1)}, bf16[64,512]{1,0:T(8,128)(2,1)S(1)}, u32[]{:S(2)}, u32[]{:S(2)}) collective-permute-start(bf16[64,512]{1,0:T(8,128)(2,1)S(1)} %get-tuple-element.82), channel_id=1, source_target_pairs={{0,1},{1,0},{2,3},{3,2},{4,5},{5,4},{6,7},{7,6},{8,9},{9,8},{10,11... | collective-permute-start | bytes 196616 | tf_op jit(solution)/shard_map/ppermute | solution.py:409
  32.4 6.7 %collective-permute-start.15 = (bf16[64,512]{1,0:T(8,128)(2,1)S(1)}, bf16[64,512]{1,0:T(8,128)(2,1)S(1)}, u32[]{:S(2)}, u32[]{:S(2)}) collective-permute-start(bf16[64,512]{1,0:T(8,128)(2,1)S(1)} %get-tuple-element.80), channel_id=1, source_target_pairs={{0,2},{1,3},{2,0},{3,1},{4,6},{5,7},{6,4},{7,5},{8,10},{9,11},{10,... | collective-permute-start | bytes 196616 | tf_op jit(solution)/shard_map/ppermute | solution.py:409
  33.9 6.3 %collective-permute-start.16 = (bf16[64,512]{1,0:T(8,128)(2,1)S(1)}, bf16[64,512]{1,0:T(8,128)(2,1)S(1)}, u32[]{:S(2)}, u32[]{:S(2)}) collective-permute-start(bf16[64,512]{1,0:T(8,128)(2,1)S(1)} %get-tuple-element.81), channel_id=1, source_target_pairs={{0,3},{1,2},{2,1},{3,0},{4,7},{5,6},{6,5},{7,4},{8,11},{9,10},{10,... | collective-permute-start | bytes 196616 | tf_op jit(solution)/shard_map/ppermute | solution.py:409
  35.8 4.7 %collective-permute-start.19 = (bf16[32,1024]{1,0:T(8,128)(2,1)S(1)}, bf16[32,1024]{1,0:T(8,128)(2,1)S(1)}, u32[]{:S(2)}, u32[]{:S(2)}) collective-permute-start(bf16[32,1024]{1,0:T(8,128)(2,1)S(1)} %get-tuple-element.86), channel_id=1, source_target_pairs={{0,8},{4,12},{8,0},{12,4},{16,24},{20,28},{24,16},{28,20},{1,9},{5... | collective-permute-start | bytes 196616 | tf_op jit(solution)/shard_map/ppermute | solution.py:409
  37.4 5.6 %collective-permute-start.20 = (s32[1,128]{1,0:T(1,128)S(1)}, s32[1,128]{1,0:T(1,128)S(1)}, u32[]{:S(2)}, u32[]{:S(2)}) collective-permute-start(s32[1,128]{1,0:T(1,128)S(1)} %get-tuple-element.102.target_ref), channel_id=1, source_target_pairs={{0,4},{4,0},{8,12},{12,8},{16,20},{20,16},{24,28},{28,24},{1,5},{5... | collective-permute-start | bytes 1544 | tf_op jit(solution)/shard_map/ppermute | solution.py:409
  37.4 8.5 %collective-permute-start.24 = (bf16[32,1024]{1,0:T(8,128)(2,1)S(1)}, bf16[32,1024]{1,0:T(8,128)(2,1)S(1)}, u32[]{:S(2)}, u32[]{:S(2)}) collective-permute-start(bf16[32,1024]{1,0:T(8,128)(2,1)S(1)} %get-tuple-element.113), channel_id=1, source_target_pairs={{0,24},{4,28},{8,16},{12,20},{16,8},{20,12},{24,0},{28,4},{1,25},{... | collective-permute-start | bytes 196616 | tf_op jit(solution)/shard_map/ppermute | solution.py:409
  39.1 6.8 %collective-permute-start.25 = (bf16[32,1024]{1,0:T(8,128)(2,1)S(1)}, bf16[32,1024]{1,0:T(8,128)(2,1)S(1)}, u32[]{:S(2)}, u32[]{:S(2)}) collective-permute-start(bf16[32,1024]{1,0:T(8,128)(2,1)S(1)} %get-tuple-element.115), channel_id=1, source_target_pairs={{0,16},{4,20},{8,24},{12,28},{16,0},{20,4},{24,8},{28,12},{1,17},{... | collective-permute-start | bytes 196616 | tf_op jit(solution)/shard_map/ppermute | solution.py:409
  40.7 5.3 %collective-permute-start.21 = (bf16[32,1024]{1,0:T(8,128)(2,1)S(1)}, bf16[32,1024]{1,0:T(8,128)(2,1)S(1)}, u32[]{:S(2)}, u32[]{:S(2)}) collective-permute-start(bf16[32,1024]{1,0:T(8,128)(2,1)S(1)} %get-tuple-element.109), channel_id=1, source_target_pairs={{0,24},{4,28},{8,16},{12,20},{16,8},{20,12},{24,0},{28,4},{1,25},{... | collective-permute-start | bytes 196616 | tf_op jit(solution)/shard_map/ppermute | solution.py:409
  42.2 4.3 %collective-permute-start.22 = (bf16[32,1024]{1,0:T(8,128)(2,1)S(1)}, bf16[32,1024]{1,0:T(8,128)(2,1)S(1)}, u32[]{:S(2)}, u32[]{:S(2)}) collective-permute-start(bf16[32,1024]{1,0:T(8,128)(2,1)S(1)} %get-tuple-element.110), channel_id=1, source_target_pairs={{0,8},{4,12},{8,0},{12,4},{16,24},{20,28},{24,16},{28,20},{1,9},{5... | collective-permute-start | bytes 196616 | tf_op jit(solution)/shard_map/ppermute | solution.py:409
  43.0 4.3 %collective-permute-start.23 = (bf16[32,1024]{1,0:T(8,128)(2,1)S(1)}, bf16[32,1024]{1,0:T(8,128)(2,1)S(1)}, u32[]{:S(2)}, u32[]{:S(2)}) collective-permute-start(bf16[32,1024]{1,0:T(8,128)(2,1)S(1)} %get-tuple-element.111), channel_id=1, source_target_pairs={{0,16},{4,20},{8,24},{12,28},{16,0},{20,4},{24,8},{28,12},{1,17},{... | collective-permute-start | bytes 196616 | tf_op jit(solution)/shard_map/ppermute | solution.py:409
  47.3 1.6 %collective-permute-start.26 = (bf16[64,2048]{1,0:T(8,128)(2,1)S(1)}, bf16[64,2048]{1,0:T(8,128)(2,1)S(1)}, u32[]{:S(2)}, u32[]{:S(2)}) collective-permute-start(bf16[64,2048]{1,0:T(8,128)(2,1)S(1)} %get-tuple-element.117), channel_id=1, source_target_pairs={{0,4},{4,0},{8,12},{12,8},{16,20},{20,16},{24,28},{28,24},{1,5},{5... | collective-permute-start | bytes 786440 | tf_op jit(solution)/shard_map/ppermute | solution.py:409
